TPU v7x, 32 devices: a whole 2x2x4 slice. The times are simulated.
32 devices in a mesh: rep: 2 (over core), req: 8 (over z, y), tp: 2 (over x).
Axes of the slice: x: 2, y: 2, z: 4, core: 2. Of those that a mesh axis runs over, the one named last changes fastest.
Arguments:
- hidden: bfloat16 [256, 1536], P(('rep', 'req'), 'tp'), may hold values from -6 to 6
- lengths: int32 [2, 128], P(None, 'req'), may hold values from 16 to 1024, as said below
- migrate: int32 [8], P('req'), may hold values from 0 to 15
- kv_cache: bfloat16 [256, 1024, 8, 128], P(('rep', 'req'), None, 'tp'), may hold values from -250 to 250
- attn_gain: float32 [1536], replicated, may hold values from 0.1 to 1.9
- moe_gain: float32 [1536], replicated, may hold values from 0.1 to 1.9
- w_query: bfloat16 [1536, 1536], P(None, 'tp'), may hold values from -0.15625 to 0.15625
- key_value_weight: bfloat16 [1536, 1024], P(None, 'tp'), may hold values from -0.15625 to 0.15625
- output_weight: bfloat16 [1536, 1536], P('tp'), may hold values from -0.25 to 0.25
- w_gateup: bfloat16 [16, 1536, 2, 512], P(('rep', 'req'), None, None, 'tp'), may hold values from -0.15625 to 0.15625
- w_down: bfloat16 [16, 512, 1536], P(('rep', 'req'), 'tp'), may hold values from -0.25 to 0.25
- expert_ids: int32 [256, 8], P(('rep', 'req')), may hold values from 0 to 15, all different within a row; in each aligned block of 16 rows (0 to 15, 16 to 31, ...) at most 16 rows name the same one
- expert_gates: float32 [256, 8], P(('rep', 'req')), may hold values from 0.1 to 0.4
Outputs:
- layer_out: bfloat16 [256, 1536], P(('rep', 'req'), 'tp')
Inputs may be any that keep to these rules, and one draw needn't show every extreme that they name: A request attends to its first lengths positions and to its own new key. `expert_ids`: each row names 8 distinct experts; among the rows of one device (an aligned block of 16 rows) no expert is named more than 16 times, and in some blocks one expert is named exactly 16 times.
All inputs are finite; a program needn't handle non-finite values.
Results may differ from a plain program's by a relative error of at most 0.015.
Values may be sent and summed in bfloat16 or wider, within the bound.
No kernel may reach another device: no remote copies, remote signals or barrier semaphores. Data moves between devices by JAX's collectives and lax.ppermute only.
A program may use at most 128 MiB of HBM per device.

v0:
```python
import jax
import jax.numpy as jnp
from jax import lax
from jax.sharding import PartitionSpec as P

HEAD_SIZE = 64


epsilon = 1e-06
rope_base = 10000.0
masked_score = -1e30


def swapped(value, axis, apart):
    return lax.ppermute(value, axis, [(i, i ^ 1 << apart) for i in range(lax.axis_size(axis))])


def rms_norm(values, gain):
    mean_square = jnp.mean(values * values, axis=-1, keepdims=True)
    return values * lax.rsqrt(mean_square + epsilon) * gain


def apply_rotation(values, position):
    half_width = values.shape[-1] // 2
    inv_freq = rope_base ** (-jnp.arange(half_width, dtype=jnp.float32) * 2.0 / values.shape[-1])
    angles = position.astype(jnp.float32)[:, None, None] * inv_freq
    cosine = jnp.cos(angles)
    sine_part = jnp.sin(angles)
    first_half = values[..., :half_width]
    second_half = values[..., half_width:]
    return jnp.concatenate(
        [
            first_half * cosine - second_half * sine_part,
            second_half * cosine + first_half * sine_part,
        ],
        axis=-1,
    )


def attention(
    token_part, kv_rows, request_extent, attn_gain, w_query, key_value_weight, output_weight
):
    tokens = lax.all_gather(token_part, "tp", axis=1, tiled=True)
    row_count = tokens.shape[0]
    head_dim = HEAD_SIZE
    local_kv = kv_rows.shape[2]
    local_query = w_query.shape[1] // head_dim
    group_size = local_query // local_kv
    normalized_input = rms_norm(tokens.astype(jnp.float32), attn_gain).astype(jnp.bfloat16)
    query_vectors = jnp.dot(normalized_input, w_query, preferred_element_type=jnp.float32).reshape(
        row_count, local_query, head_dim
    )
    key_value_rows = jnp.dot(
        normalized_input, key_value_weight, preferred_element_type=jnp.float32
    ).reshape(row_count, local_kv, 2 * head_dim)
    query_vectors = (
        apply_rotation(query_vectors, request_extent)
        .astype(jnp.bfloat16)
        .reshape(row_count, local_kv, group_size, head_dim)
    )
    key_new = apply_rotation(key_value_rows[..., :head_dim], request_extent).astype(jnp.bfloat16)
    value_new = key_value_rows[..., head_dim:].astype(jnp.bfloat16)
    score_scale = head_dim ** (-0.5)
    cache_keys = kv_rows[..., :head_dim]
    cache_values = kv_rows[..., head_dim:]
    scores = (
        jnp.einsum("rhgd,rthd->rhgt", query_vectors, cache_keys, preferred_element_type=jnp.float32)
        * score_scale
    )
    own_score = (
        jnp.einsum("rhgd,rhd->rhg", query_vectors, key_new, preferred_element_type=jnp.float32)
        * score_scale
    )
    positions = jnp.arange(kv_rows.shape[1], dtype=jnp.int32)
    visible = positions[None, None, None, :] < request_extent[:, None, None, None]
    scores = jnp.where(visible, scores, masked_score)
    row_peak = jnp.maximum(jnp.max(scores, axis=-1), own_score)
    cache_prob = jnp.exp(scores - row_peak[..., None])
    own_prob = jnp.exp(own_score - row_peak)
    denominator = jnp.sum(cache_prob, axis=-1) + own_prob
    cache_weight = (cache_prob / denominator[..., None]).astype(jnp.bfloat16)
    own_weight = (own_prob / denominator).astype(jnp.bfloat16)
    mixture = jnp.einsum(
        "rhgt,rthd->rhgd", cache_weight, cache_values, preferred_element_type=jnp.float32
    )
    mixture = (
        mixture
        + own_weight.astype(jnp.float32)[..., None] * value_new.astype(jnp.float32)[:, :, None, :]
    )
    context = mixture.reshape(row_count, local_query * head_dim).astype(jnp.bfloat16)
    partial_out = jnp.dot(context, output_weight, preferred_element_type=jnp.float32)
    return tokens.astype(jnp.float32) + lax.psum(partial_out.astype(jnp.bfloat16), "tp").astype(
        jnp.float32
    )


def shards(
    hidden,
    lengths,
    migrate,
    kv_cache,
    attn_gain,
    moe_gain,
    w_query,
    key_value_weight,
    output_weight,
    w_gateup,
    w_down,
    expert_ids,
    expert_gates,
):
    row_count = hidden.shape[0]
    replica = lax.axis_index("rep")
    slot_index = jnp.arange(row_count, dtype=jnp.int32)
    chosen_slot = migrate[0]
    is_moved = slot_index == chosen_slot
    own_span = lax.dynamic_index_in_dim(lengths, replica, 0, keepdims=False)
    other_span = lax.dynamic_index_in_dim(lengths, 1 - replica, 0, keepdims=False)
    picked_cache = lax.dynamic_slice_in_dim(kv_cache, chosen_slot, 1, 0)
    picked_row = lax.dynamic_slice_in_dim(hidden, chosen_slot, 1, 0)
    cache_width = picked_cache.size
    packed = jnp.concatenate([picked_cache.reshape(1, cache_width), picked_row], axis=1)
    arrived = swapped(packed, "rep", 0)
    moved_cache = arrived[:, :cache_width].reshape(picked_cache.shape)
    moved_row = arrived[:, cache_width:]
    served_cache = lax.dynamic_update_slice_in_dim(kv_cache, moved_cache, chosen_slot, 0)
    served_rows = lax.dynamic_update_slice_in_dim(hidden, moved_row, chosen_slot, 0)
    request_extent = jnp.where(is_moved, other_span, own_span)
    residual = attention(
        served_rows,
        served_cache,
        request_extent,
        attn_gain,
        w_query,
        key_value_weight,
        output_weight,
    )
    full_width = moe_gain.shape[0]
    quarter = full_width // lax.axis_size("tp")
    expert_in = rms_norm(residual, moe_gain).astype(jnp.bfloat16)
    own_residual = lax.dynamic_slice_in_dim(residual, lax.axis_index("tp") * quarter, quarter, 1)
    expert_count = lax.axis_size("rep") * lax.axis_size("req")
    top_count = expert_ids.shape[1]
    capacity = min(row_count, max(3, 3 * row_count * top_count // expert_count))
    flat_ids = expert_ids.reshape(-1)
    matches = (flat_ids[:, None] == jnp.arange(expert_count, dtype=jnp.int32)[None, :]).astype(
        jnp.int32
    )
    slot_rank = jnp.sum((jnp.cumsum(matches, axis=0) - matches) * matches, axis=1)
    slot_target = flat_ids * capacity + slot_rank
    slot_table = (
        slot_target[:, None] == jnp.arange(expert_count * capacity, dtype=jnp.int32)[None, :]
    ).astype(jnp.float32)
    route_table = slot_table.reshape(row_count, top_count, -1).sum(axis=1)
    gate_table = (
        (slot_table * expert_gates.reshape(-1, 1)).reshape(row_count, top_count, -1).sum(axis=1)
    )
    outbound = jnp.einsum(
        "rs,rd->sd", route_table.astype(jnp.bfloat16), expert_in, preferred_element_type=jnp.float32
    ).astype(jnp.bfloat16)
    outbound = outbound.reshape(expert_count, capacity, -1)
    gate_up = w_gateup[0].reshape(w_gateup.shape[1], -1)
    down_rows = w_down[0]
    arrived_rows = lax.all_to_all(outbound, ("rep", "req"), split_axis=0, concat_axis=0, tiled=True)
    model_width = arrived_rows.shape[2]
    flattened = arrived_rows.reshape(-1, model_width)
    projected = jnp.dot(flattened, gate_up, preferred_element_type=jnp.float32)
    split_at = projected.shape[1] // 2
    activation = (jax.nn.silu(projected[:, :split_at]) * projected[:, split_at:]).astype(
        jnp.bfloat16
    )
    expert_part = jnp.dot(activation, down_rows, preferred_element_type=jnp.float32)
    expert_part = expert_part.reshape(arrived_rows.shape[0], arrived_rows.shape[1], model_width)
    returned = lax.all_to_all(
        expert_part.astype(jnp.bfloat16), ("rep", "req"), split_axis=0, concat_axis=0, tiled=True
    ).astype(expert_part.dtype)
    returned_rows = returned.reshape(expert_count * capacity, -1)
    combined = jnp.dot(
        gate_table,
        returned_rows,
        precision=lax.Precision.HIGHEST,
        preferred_element_type=jnp.float32,
    )
    expert_mix = lax.psum_scatter(
        combined.astype(jnp.bfloat16), "tp", scatter_dimension=1, tiled=True
    ).astype(jnp.float32)
    return (own_residual + expert_mix).astype(jnp.bfloat16)


def solution(mesh):
    placed = (
        P(("rep", "req"), "tp"),
        P(None, "req"),
        P("req"),
        P(("rep", "req"), None, "tp", None),
        P(),
        P(),
        P(None, "tp"),
        P(None, "tp"),
        P("tp", None),
        P(("rep", "req"), None, None, "tp"),
        P(("rep", "req"), "tp", None),
        P(("rep", "req"), None),
        P(("rep", "req"), None),
    )
    return jax.shard_map(
        shards, mesh=mesh, in_specs=placed, out_specs=P(("rep", "req"), "tp"), check_vma=False
    )
```

profile of v0, /device:TPU:0, one launch (start us, length us, event | category | flops | bytes accessed | tf_op | source)
XLA Modules:
  0.0 177.1 jit_solution(3132837096941192567)
XLA Ops:
  6.5 0.9 copy.45
  8.1 1.6 constant_dynamic-slice_fusion.3
  9.7 1.7 reshape.200
  11.4 10.5 %pad_maximum_fusion = bf16[1,525056]{1,0:T(2,128)(2,1)} fusion(bf16[1,768]{1,0:T(2,128)(2,1)S(1)} %constant_dynamic-slice_fusion.2, bf16[1,524288]{1,0:T(2,128)(2,1)} %reshape.200), kind=kLoop, calls=%fused_computation.8 | loop fusion | flops 2100224 | bytes 2100224 | tf_op jit(solution)/shard_map/concatenate | solution.py:122
  22.0 0.5 collective-permute-start
  23.0 26.2 %copy.31 = bf16[16,1024,4,128]{1,3,2,0:T(8,128)(2,1)} copy(bf16[16,1024,4,128]{3,2,1,0:T(4,128)(2,1)} %param.16) | data formatting | bytes 33554432 | tf_op args[3]
  49.4 0.7 convert_reduce_fusion
  50.2 0.7 iota_compare_fusion.2
  51.0 0.7 slice.48
  51.7 5.2 %all_gather.3 = bf16[16,1536]{1,0:T(8,128)(2,1)S(1)} all-gather(bf16[16,768]{1,0:T(8,128)(2,1)S(1)} %dynamic_update_slice.6), channel_id=1, replica_groups=mesh['rep'=2,'req'=8,'tp'=2] {'tp'}, dimensions={1}, use_global_device_ids=true | all-gather | bytes 73728 | tf_op jit(solution)/shard_map/all_gather | solution.py:43
  56.9 18.5 %slice_reduce_fusion = bf16[524288]{0:T(1024)(128)(2,1)S(1)} fusion(bf16[1,525056]{1,0:T(2,128)(2,1)} %collective-permute-done), kind=kLoop, calls=%fused_computation.9 | loop fusion | bytes 2097152 | tf_op jit(solution)/shard_map/slice | solution.py:124
  75.5 1.5 copy.32
  77.1 2.2 %fusion.33 = f32[16,768]{1,0:T(8,128)S(1)} fusion(bf16[1536,768]{1,0:T(8,128)(2,1)} %param.19, bf16[16,1536]{1,0:T(8,128)(2,1)S(1)} %all_gather.3, f32[1536]{0:T(1024)S(1)} %copy-done.3, f32[16]{0:T(128)S(1)} %add_rsqrt_fusion.1), kind=kOutput, calls=%fused_computation.57 | convolution fusion | flops 37847040 | bytes 2463808 | tf_op jit(solution)/shard_map/dot_general | solution.py:50
  79.3 0.7 reshape.201
  80.1 1.8 %fusion.31 = f32[16,512]{1,0:T(8,128)S(1)} fusion(bf16[1536,512]{1,0:T(8,128)(2,1)} %param.20, bf16[16,1536]{1,0:T(8,128)(2,1)S(1)} %all_gather.3, f32[1536]{0:T(1024)} %param.17, f32[16]{0:T(128)} %copy-done.9), kind=kOutput, calls=%fused_computation.56 | convolution fusion | flops 25264128 | bytes 1660992 | tf_op jit(solution)/shard_map/dot_general | solution.py:53
  82.1 1.1 subtract_convert_fusion
  83.3 1.1 constant_dynamic-update-slice_fusion
  84.7 4.8 %fusion.40 = (f32[16,4,3]{2,1,0:T(4,128)S(1)}, f32[16,4,3,1024]{3,2,1,0:T(4,128)S(1)}) fusion(bf16[16,1024,4,128]{1,3,2,0:T(8,128)(2,1)} %constant_dynamic-update-slice_fusion, bf16[16,4,3,32]{3,2,1,0:T(4,128)(2,1)S(1)} %copy.30, bf16[16,4,3,32]{3,2,1,0:T(4,128)(2,1)S(1)} %copy.29, pred[16,1024]{1,0:T(8,128)(4,1)S(1)} %copy-done.5), kind=kOutput, calls=%fused_computation.73 | convolution fusion | flops 25804608 | bytes 9216768 | tf_op jit(solution)/shard_map/rhgd,rthd->rhgt/dot_general | solution.py:67
  89.5 0.5 fusion.16
  90.1 5.7 %fusion.10 = bf16[16,4,3,64]{3,2,1,0:T(4,128)(2,1)S(1)} fusion(bf16[16,1024,4,128]{1,3,2,0:T(8,128)(2,1)} %constant_dynamic-update-slice_fusion, f32[16,4,3,1024]{3,2,1,0:T(4,128)S(1)} %get-tuple-element.20, f32[16,4,3]{2,1,0:T(4,128)S(1)} %get-tuple-element.14, f32[16,4,3]{2,1,0:T(4,128)S(1)} %multiply_maximum_fusion, f32[16,4,64]{2,1,0:T(4,128)S(1)} %fusion.29, ...), kind=kOutput, calls=%fused_computation.12 | convolution fusion | flops 25792512 | bytes 9218304 | tf_op jit(solution)/shard_map/rhgt,rthd->rhgd/dot_general | solution.py:83
  95.9 0.4 convolution_convert_fusion.3
  96.4 9.3 %psum.7 = bf16[16,1536]{1,0:T(8,128)(2,1)S(1)} all-reduce(bf16[16,1536]{1,0:T(8,128)(2,1)S(1)} %convolution_convert_fusion.3), channel_id=1, replica_groups=mesh['rep'=2,'req'=8,'tp'=2] {'tp'}, use_global_device_ids=true, to_apply=%region_3.4 | all-reduce | flops 24576 | bytes 98304 | tf_op jit(solution)/shard_map/psum | solution.py:92
  105.8 1.3 convolution_convert_fusion.1
  107.1 5.8 %all-to-all-start = ((bf16[16,16,1536]{2,1,0:T(8,128)(2,1)}), bf16[16,16,1536]{2,1,0:T(8,128)(2,1)S(1)}, u32[]{:S(2)}, u32[]{:S(2)}) async-start(bf16[16,16,1536]{2,1,0:T(8,128)(2,1)} %bitcast.8), calls=%async_computation | async-start | bytes 1572864 | tf_op jit(solution)/shard_map/all_to_all | solution.py:164
  113.0 2.9 %copy.38 = bf16[192,8,2,256]{3,1,2,0:T(8,128)(2,1)} copy(bf16[192,8,2,256]{3,2,1,0:T(2,128)(2,1)} %bitcast.47) | data formatting | bytes 3145728
  115.9 18.3 %all-to-all-done = bf16[16,16,1536]{2,1,0:T(8,128)(2,1)S(1)} async-done(((bf16[16,16,1536]{2,1,0:T(8,128)(2,1)}), bf16[16,16,1536]{2,1,0:T(8,128)(2,1)S(1)}, u32[]{:S(2)}, u32[]{:S(2)}) %all-to-all-start) | async-done | bytes 786464 | tf_op jit(solution)/shard_map/all_to_all | solution.py:164
  134.2 2.0 %fusion.41 = f32[256,512]{1,0:T(8,128)S(1)} fusion(bf16[256,1536]{1,0:T(8,128)(2,1)S(1)} %bitcast.46, bf16[1536,512]{1,0:T(8,128)(2,1)} %bitcast.43), kind=kOutput, calls=%fused_computation.74 | convolution fusion | flops 402653184 | bytes 2883584 | tf_op jit(solution)/shard_map/dot_general | solution.py:167
  136.3 0.4 convolution_convert_fusion
  136.7 24.2 %all_to_all.10 = bf16[16,16,1536]{2,1,0:T(8,128)(2,1)S(1)} all-to-all(bf16[16,16,1536]{2,1,0:T(8,128)(2,1)S(1)} %convolution_convert_fusion), channel_id=1, replica_groups=mesh['rep'=2,'req'=8,'tp'=2] {'rep','req'}, dimensions={0} | all-to-all | bytes 1572864 | tf_op jit(solution)/shard_map/all_to_all | solution.py:174
  160.9 1.0 convolution_convert_fusion.2
  161.9 7.0 %reduce-scatter.2.cloned.1.call-done = bf16[16,768]{1,0:T(8,128)(2,1)} async-done(((bf16[16,1536]{1,0:T(8,128)(2,1)}), bf16[16,768]{1,0:T(8,128)(2,1)}) %reduce-scatter.2.cloned.1.call-update) | async-done | bytes 24592 | tf_op jit(solution)/shard_map/reduce_scatter | solution.py:184
  168.9 1.4 add_convert_fusion.1
  (55 shorter events, 2.2 us)
Async XLA Ops:
  6.5 89.4 %copy-start = (bf16[768,1536]{1,0:T(8,128)(2,1)S(1)}, bf16[768,1536]{1,0:T(8,128)(2,1)}, u32[]{:S(2)}) copy-start(bf16[768,1536]{1,0:T(8,128)(2,1)} %param.21) | copy-start | bytes 7077892
  11.4 11.0 %copy-start.7 = (s32[16,8]{0,1:T(8,128)S(1)}, s32[16,8]{0,1:T(8,128)}, u32[]{:S(2)}) copy-start(s32[16,8]{0,1:T(8,128)} %param.24) | copy-start | bytes 1540
  22.0 29.0 %collective-permute-start = (bf16[1,525056]{1,0:T(2,128)(2,1)}, bf16[1,525056]{1,0:T(2,128)(2,1)}, u32[]{:S(2)}, u32[]{:S(2)}) collective-permute-start(bf16[1,525056]{1,0:T(2,128)(2,1)} %pad_maximum_fusion), channel_id=1, source_target_pairs={{0,16},{16,0},{1,17},{17,1},{2,18},{18,2},{3,19},{19,3},{4,20},{20... | collective-permute-start | bytes 3150344 | tf_op jit(solution)/shard_map/ppermute | solution.py:15
  23.0 26.3 %copy-start.8 = (f32[16,8]{0,1:T(8,128)S(1)}, f32[16,8]{0,1:T(8,128)}, u32[]{:S(2)}) copy-start(f32[16,8]{0,1:T(8,128)} %param.25) | copy-start | bytes 1540
  23.0 26.4 %copy-start.10 = (s32[2,16]{1,0:T(2,128)S(1)}, s32[2,16]{1,0:T(2,128)}, u32[]{:S(2)}) copy-start(s32[2,16]{1,0:T(2,128)} %param.14) | copy-start | bytes 388
  56.9 20.2 %copy-start.3 = (f32[1536]{0:T(1024)S(1)}, f32[1536]{0:T(1024)}, u32[]{:S(2)}) copy-start(f32[1536]{0:T(1024)} %param.17) | copy-start | bytes 18436
  77.1 2.2 %copy-start.9 = (f32[16]{0:T(128)}, f32[16]{0:T(128)S(1)}, u32[]{:S(2)}) copy-start(f32[16]{0:T(128)S(1)} %add_rsqrt_fusion.1) | copy-start | bytes 196
  77.1 6.2 %copy-start.1 = (bf16[1,1024,4,128]{1,3,2,0:T(8,128)(2,1)S(1)}, bf16[1,1024,4,128]{1,3,2,0:T(8,128)(2,1)}, u32[]{:S(2)}) copy-start(bf16[1,1024,4,128]{1,3,2,0:T(8,128)(2,1)} %copy.32) | copy-start | bytes 3145732
  81.9 2.8 %copy-start.5 = (pred[16,1024]{1,0:T(8,128)(4,1)S(1)}, pred[16,1024]{1,0:T(8,128)(4,1)}, u32[]{:S(2)}) copy-start(pred[16,1024]{1,0:T(8,128)(4,1)} %iota_compare_fusion.2) | copy-start | bytes 49156
  95.8 10.0 %copy-start.4 = (bf16[16,256]{1,0:T(8,128)(2,1)S(1)}, bf16[16,256]{1,0:T(8,128)(2,1)}, u32[]{:S(2)}) copy-start(bf16[16,256]{1,0:T(8,128)(2,1)} %get-tuple-element.5) | copy-start | bytes 24580
  95.8 10.0 %copy-start.6 = (f32[1536]{0:T(1024)S(1)}, f32[1536]{0:T(1024)}, u32[]{:S(2)}) copy-start(f32[1536]{0:T(1024)} %param.18) | copy-start | bytes 18436
  107.1 27.0 %all-to-all-start = ((bf16[16,16,1536]{2,1,0:T(8,128)(2,1)}), bf16[16,16,1536]{2,1,0:T(8,128)(2,1)S(1)}, u32[]{:S(2)}, u32[]{:S(2)}) async-start(bf16[16,16,1536]{2,1,0:T(8,128)(2,1)} %bitcast.8), calls=%async_computation | async-start | bytes 1572864 | tf_op jit(solution)/shard_map/all_to_all | solution.py:164
  113.0 55.9 %reduce-scatter.2.cloned.1.call-start = ((), (), s32[]{:S(2)}) async-start(), calls=%async_computation.3 | async-start | bytes 73728 | tf_op jit(solution)/shard_map/reduce_scatter | solution.py:184
  134.2 2.1 %copy-start.2 = (bf16[1,256,1536]{2,1,0:T(8,128)(2,1)S(1)}, bf16[1,256,1536]{2,1,0:T(8,128)(2,1)}, u32[]{:S(2)}) copy-start(bf16[1,256,1536]{2,1,0:T(8,128)(2,1)} %param.23) | copy-start | bytes 2359300
Sparse Core Ops, SparseCore 0:
  162.0 6.8 reduce-scatter.1
where the time goes:
time: 178 us; the launch traced here: 177 us
  local copies, waits for them, and re-layouts  56.4 us (32%)
  blocking collectives  38.7 us (22%)
  waiting for transfers between devices  25.3 us (14%)
  matrix products  19.9 us (11%)
  other arithmetic  16.1 us (9%)
  between operations  14.4 us (8%)
  starting transfers between devices  6.32 us (4%)
    unnamed x27, local copies, waits for them, and re-layouts  30.1 us
    all_to_all x1, blocking collectives, shards(): lax.all_to_all(expert_part.astype(jnp.bfloat16), ('rep', 'req'), split_ax...  24.2 us
    slice x1, local copies, waits for them, and re-layouts, shards(): moved_cache = arrived[:, :cache_width].reshape(picked_cache.shape)  18.5 us
    all_to_all x1, waiting for transfers between devices, shards(): lax.all_to_all(outbound, ('rep', 'req'), split_axis=0, concat_axis=0, til...  18.3 us
    concatenate x1, other arithmetic, shards(): jnp.concatenate([picked_cache.reshape(1, cache_width), picked_row], axis=1)  10.5 us
    psum x1, blocking collectives, attention(): lax.psum(partial_out.astype(jnp.bfloat16), 'tp').astype(jnp.float32)  9.31 us
    reduce_scatter x1, waiting for transfers between devices, shards(): lax.psum_scatter(combined.astype(jnp.bfloat16), 'tp', scatter_dimension=1...  6.98 us
    all_to_all x1, starting transfers between devices, shards(): lax.all_to_all(outbound, ('rep', 'req'), split_axis=0, concat_axis=0, til...  5.82 us
  transfers between devices with their start and end apart: 3, of which 2 were waited for; matrix products, arithmetic and copies ran while one was open for 18% of the time, Pallas kernels for 0%

commit v1 on v0

v1 whole, which is shorter than its diff:
```python
import jax
import jax.numpy as jnp
from jax import lax
from jax.experimental import pallas as pl
from jax.experimental.pallas import tpu as pltpu
from jax.sharding import PartitionSpec as P

HEAD = 64
EPS = 1e-06
ROPE_BASE = 10000.0
MASKED = -1e30
LANES = 128
QROWS = 16
SPAN = 128
UNROLL = 4
MIB = 1 << 20

bf16 = jnp.bfloat16
f32 = jnp.float32


def vmem():
    return pl.BlockSpec(memory_space=pltpu.VMEM)


def smem():
    return pl.BlockSpec(memory_space=pltpu.SMEM)


def hbm():
    return pl.BlockSpec(memory_space=pl.ANY)


def swapped(value, axis):
    return lax.ppermute(value, axis, [(i, i ^ 1) for i in range(lax.axis_size(axis))])


def normed_rows(rows, gain):
    mean_square = jnp.mean(rows * rows, axis=-1, keepdims=True)
    return (rows * lax.rsqrt(mean_square + EPS) * gain).astype(bf16)


def attention_kernel(n_parts, *refs):
    place, lens = refs[0], refs[1]
    parts = refs[2 : 2 + n_parts]
    (cos_ref, sin_ref, gain_ref, wq_hbm, wkv_hbm, wo_hbm, kv_hbm) = refs[2 + n_parts : 9 + n_parts]
    (tok_out, keep_out, send_out) = refs[9 + n_parts : 12 + n_parts]
    (wq, wkv, wo, kvbuf, qf, qb, kvn, scores, macc, lacc, oacc, ctx, items, wsem, ksem) = refs[12 + n_parts :]
    rows = tok_out.shape[0]
    n_query = wq.shape[1] // HEAD
    n_kv = wkv.shape[1] // (2 * HEAD)
    group = n_query // n_kv
    per = kv_hbm.shape[1] // (SPAN * n_kv)
    wide = SPAN * n_kv
    rep, tp = place[0], place[1]

    copies = [
        pltpu.make_async_copy(src, dst, wsem.at[i])
        for i, (src, dst) in enumerate(((wq_hbm, wq), (wkv_hbm, wkv), (wo_hbm, wo)))
    ]
    copies[0].start()
    copies[1].start()

    def kv_copy(item):
        r, c = item // per, item % per
        start = pl.multiple_of(c * wide, wide)
        return pltpu.make_async_copy(
            kv_hbm.at[r, pl.ds(start, wide)], kvbuf.at[r, pl.ds(start, wide)], ksem.at[item]
        )

    def plan_row(r, n):
        def plan_chunk(c, n):
            items[n] = r * per + c
            kv_copy(r * per + c).start()
            return n + 1

        return lax.fori_loop(0, (lens[rep, r] + SPAN - 1) // SPAN, plan_chunk, n)

    total = lax.fori_loop(0, rows, plan_row, 0)
    for u in range(UNROLL):
        items[total + u] = rows * per
    blocks = (total + UNROLL - 1) // UNROLL
    copies[2].start()

    if n_parts == 2:
        tokens = jnp.concatenate(
            [
                jnp.where(tp == 0, parts[0][...], parts[1][...]),
                jnp.where(tp == 0, parts[1][...], parts[0][...]),
            ],
            axis=1,
        )
    else:
        tokens = parts[0][...]
    tok_out[...] = tokens
    normed = normed_rows(tokens.astype(f32), gain_ref[...])

    lane = lax.broadcasted_iota(jnp.int32, (rows, LANES), 1)
    low_half = lane < HEAD
    first = lane % HEAD < HEAD // 2
    cosine, sine = cos_ref[...], sin_ref[...]

    def rotate(v):
        partner = jnp.where(first, pltpu.roll(v, LANES - HEAD // 2, 1), pltpu.roll(v, HEAD // 2, 1))
        return v * cosine + partner * sine

    qf[...] = jnp.zeros_like(qf)
    kvn[...] = jnp.zeros_like(kvn)
    macc[...] = jnp.full_like(macc, MASKED)
    lacc[...] = jnp.zeros_like(lacc)
    oacc[...] = jnp.zeros_like(oacc)
    copies[0].wait()
    queries = jnp.dot(normed, wq[...], preferred_element_type=f32)
    for k in range(n_query // 2):
        turned = rotate(queries[:, k * LANES : (k + 1) * LANES]).astype(bf16).astype(f32)
        turned = turned * HEAD**-0.5
        qf[pl.ds(2 * k, rows, stride=QROWS), :] = jnp.where(low_half, turned, 0.0)
        qf[pl.ds(2 * k + 1, rows, stride=QROWS), :] = jnp.where(low_half, pltpu.roll(turned, HEAD, 1), 0.0)
    copies[1].wait()
    keyval = jnp.dot(normed, wkv[...], preferred_element_type=f32)
    for h in range(n_kv):
        v = keyval[:, h * LANES : (h + 1) * LANES]
        new = jnp.where(low_half, rotate(v), v).astype(bf16).astype(f32)
        for g in range(group):
            kvn[pl.ds(h * group + g, rows, stride=QROWS), :] = new
    qb[...] = qf[...].astype(bf16).reshape(qb.shape)

    row_head = lax.broadcasted_iota(jnp.int32, (QROWS, wide), 0) // group
    column = lax.broadcasted_iota(jnp.int32, (QROWS, wide), 1)
    reach = jnp.where(column % n_kv == row_head, column // n_kv, 1 << 30)

    def folded(op, value):
        out = value[:, :LANES]
        for j in range(1, wide // LANES):
            out = op(out, value[:, j * LANES : (j + 1) * LANES])
        return out

    def chunk(i):
        item = items[i]
        r = item // per
        c = item % per
        kr = jnp.minimum(r, rows - 1)
        return r, c, kvbuf[kr, pl.ds(pl.multiple_of(c * wide, wide), wide), :]

    def score_block(b, carry):
        for u in range(UNROLL):

            @pl.when(b * UNROLL + u < total)
            def _():
                kv_copy(items[b * UNROLL + u]).wait()

        for u in range(UNROLL):
            i = b * UNROLL + u
            r, c, kv = chunk(i)
            s = lax.dot_general(qb[r], kv, (((1,), (1,)), ((), ())), preferred_element_type=f32)
            span = lens[rep, jnp.minimum(r, rows - 1)]
            limit = jnp.where(r < rows, span - c * SPAN, 0)
            s = jnp.where(reach < limit, s, MASKED)
            scores[i] = s
            macc[r] = jnp.maximum(macc[r], folded(jnp.maximum, s))
        return carry

    lax.fori_loop(0, blocks, score_block, 0)

    own = jnp.sum(qf[...] * kvn[...], axis=-1, keepdims=True)
    peak = jnp.maximum(jnp.max(macc[...].reshape(qf.shape), axis=-1, keepdims=True), own)
    own_p = jnp.exp(own - peak)
    macc[...] = jnp.broadcast_to(peak, qf.shape).reshape(macc.shape)

    def value_block(b, carry):
        for u in range(UNROLL):
            i = b * UNROLL + u
            r, c, kv = chunk(i)
            m = macc[r]
            p = jnp.exp(scores[i] - jnp.concatenate([m] * (wide // LANES), axis=1))
            lacc[r] += folded(jnp.add, p)
            oacc[r] += jnp.dot(p.astype(bf16), kv, preferred_element_type=f32)
        return carry

    lax.fori_loop(0, blocks, value_block, 0)

    total_p = jnp.sum(lacc[...].reshape(qf.shape), axis=-1, keepdims=True) + own_p
    qf[...] = (oacc[...].reshape(qf.shape) + own_p * kvn[...]) / total_p
    for k in range(n_query // 2):
        a = qf[pl.ds(2 * k, rows, stride=QROWS), :]
        b = qf[pl.ds(2 * k + 1, rows, stride=QROWS), :]
        ctx[:, k * LANES : (k + 1) * LANES] = jnp.where(low_half, pltpu.roll(a, HEAD, 1), b).astype(bf16)
    copies[2].wait()
    partial = jnp.dot(ctx[...], wo[...], preferred_element_type=f32)
    keep_out[...] = partial
    send_out[...] = partial.astype(bf16)


def attention(place, lens, parts, cosine, sine, gain, wq, wkv, wo, kv):
    rows = parts[0].shape[0]
    width = wq.shape[0]
    n_kv = wkv.shape[1] // (2 * HEAD)
    per = kv.shape[1] // (SPAN * n_kv)
    slots = rows * per + UNROLL
    many = rows + 1
    return pl.pallas_call(
        lambda *refs: attention_kernel(len(parts), *refs),
        out_shape=(
            jax.ShapeDtypeStruct((rows, width), bf16),
            jax.ShapeDtypeStruct((rows, width), f32),
            jax.ShapeDtypeStruct((rows, width), bf16),
        ),
        in_specs=[smem(), smem()] + [vmem()] * (len(parts) + 3) + [hbm()] * 4,
        out_specs=(vmem(), vmem(), vmem()),
        scratch_shapes=[
            pltpu.VMEM(wq.shape, bf16),
            pltpu.VMEM(wkv.shape, bf16),
            pltpu.VMEM(wo.shape, bf16),
            pltpu.VMEM(kv.shape, bf16),
            pltpu.VMEM((many * QROWS, LANES), f32),
            pltpu.VMEM((many, QROWS, LANES), bf16),
            pltpu.VMEM((many * QROWS, LANES), f32),
            pltpu.VMEM((slots, QROWS, SPAN * n_kv), f32),
            pltpu.VMEM((many, QROWS, LANES), f32),
            pltpu.VMEM((many, QROWS, LANES), f32),
            pltpu.VMEM((many, QROWS, LANES), f32),
            pltpu.VMEM((rows, wq.shape[1]), bf16),
            pltpu.SMEM((slots,), jnp.int32),
            pltpu.SemaphoreType.DMA((3,)),
            pltpu.SemaphoreType.DMA((rows * per,)),
        ],
        compiler_params=pltpu.CompilerParams(vmem_limit_bytes=44 * MIB),
        name="attention",
    )(place, lens, *parts, cosine, sine, gain, wq, wkv, wo, kv)


def expert_input_kernel(n_tp, place, moved_slot, tokens, keep, other, gain, ids, gates, payload, residual_out):
    rows, width = tokens.shape
    tp = place[1]
    residual = tokens[...].astype(f32) + keep[...] + other[...].astype(f32)
    part = width // n_tp
    mine = residual[:, :part]
    for t in range(1, n_tp):
        mine = jnp.where(tp == t, residual[:, t * part : (t + 1) * part], mine)
    residual_out[...] = mine
    expert_in = normed_rows(residual, gain[...])
    extra = payload.shape[2] - width
    n_experts = (place[3])
    lane = lax.broadcasted_iota(jnp.int32, (rows, extra), 1)
    table = jnp.zeros((rows, extra), f32)
    low = jnp.zeros((rows, extra), f32)
    for k in range(ids.shape[1]):
        chosen = ids[:, k : k + 1]
        weight = gates[:, k : k + 1]
        top = weight.astype(bf16).astype(f32)
        table = jnp.where(lane == chosen, top, table)
        table = jnp.where(lane == chosen + n_experts, weight - top, table)
    slot = lax.broadcasted_iota(jnp.int32, (rows, extra), 0)
    table = jnp.where((lane == 2 * n_experts) & (slot == moved_slot[0]), 1.0, table)
    table = table.astype(bf16)
    for q in range(payload.shape[0]):
        payload[q, :, :width] = expert_in
        payload[q, :, width:] = table


def expert_input(n_tp, n_req, extra, place, migrate, tokens, keep, other, gain, ids, gates):
    rows, width = tokens.shape
    return pl.pallas_call(
        lambda *refs: expert_input_kernel(n_tp, *refs),
        out_shape=(
            jax.ShapeDtypeStruct((n_req, rows, width + extra), bf16),
            jax.ShapeDtypeStruct((rows, width // n_tp), f32),
        ),
        in_specs=[smem(), smem()] + [vmem()] * 6,
        out_specs=(vmem(), vmem()),
        name="expert_input",
    )(place, migrate, tokens, keep, other, gain, ids, gates)


def expert_rows(rows, gate_up, down):
    projected = jnp.dot(rows, gate_up, preferred_element_type=f32)
    hidden = projected.shape[1] // 2
    gate, up = projected[:, :hidden], projected[:, hidden:]
    active = (gate / (1.0 + jnp.exp(-gate)) * up).astype(bf16)
    return jnp.dot(active, down, preferred_element_type=f32)


def own_expert_kernel(x, gate_up, down, y):
    width = down.shape[1]
    y[...] = expert_rows(x[:, :width], gate_up[...], down[...])


def own_expert(x, gate_up, down):
    return pl.pallas_call(
        own_expert_kernel,
        out_shape=jax.ShapeDtypeStruct((x.shape[0], down.shape[1]), f32),
        in_specs=[vmem()] * 3,
        out_specs=vmem(),
        compiler_params=pltpu.CompilerParams(vmem_limit_bytes=32 * MIB),
        name="own_expert",
    )(x, gate_up, down)


def other_expert_kernel(place, x_own, x_other, y_own, gate_up, down, keep, send):
    width = down.shape[1]
    expert, n_experts = place[2], place[3]
    y_other = expert_rows(x_other[:, :width], gate_up[...], down[...])
    own_table = x_own[:, width:].astype(f32)
    other_table = x_other[:, width:].astype(f32)
    lane = lax.broadcasted_iota(jnp.int32, own_table.shape, 1)

    def picked(table, mask):
        return jnp.sum(jnp.where(mask, table, 0.0), axis=-1, keepdims=True)

    mine = (lane == expert) | (lane == expert + n_experts)
    own_gate, other_gate = picked(own_table, mine), picked(other_table, mine)
    moved = picked(own_table, lane == 2 * n_experts) > 0.5
    from_own = y_own[...] * jnp.where(moved, other_gate, own_gate)
    from_other = y_other * jnp.where(moved, own_gate, other_gate)
    keep[...] = jnp.where(moved, from_other, from_own)
    send[...] = jnp.where(moved, from_own, from_other).astype(bf16)


def other_expert(place, x_own, x_other, y_own, gate_up, down):
    return pl.pallas_call(
        other_expert_kernel,
        out_shape=(
            jax.ShapeDtypeStruct(y_own.shape, f32),
            jax.ShapeDtypeStruct(y_own.shape, bf16),
        ),
        in_specs=[smem()] + [vmem()] * 5,
        out_specs=(vmem(), vmem()),
        compiler_params=pltpu.CompilerParams(vmem_limit_bytes=40 * MIB),
        name="other_expert",
    )(place, x_own, x_other, y_own, gate_up, down)


def pair_sum_kernel(n_tp, keep, recv, out):
    n_req, _, rows, part = out.shape
    total = (keep[...] + recv[...].astype(f32)).astype(bf16)
    for q in range(n_req):
        for t in range(n_tp):
            out[q, t] = total[q * rows : (q + 1) * rows, t * part : (t + 1) * part]


def pair_sum(n_tp, n_req, keep, recv):
    rows, part = keep.shape[0] // n_req, keep.shape[1] // n_tp
    return pl.pallas_call(
        lambda *refs: pair_sum_kernel(n_tp, *refs),
        out_shape=jax.ShapeDtypeStruct((n_req, n_tp, rows, part), bf16),
        in_specs=[vmem()] * 2,
        out_specs=vmem(),
        compiler_params=pltpu.CompilerParams(vmem_limit_bytes=32 * MIB),
        name="pair_sum",
    )(keep, recv)


def final_kernel(moved_slot, pieces, own_residual, other_residual, out):
    total = pieces[0].astype(f32)
    for i in range(1, pieces.shape[0]):
        total = total + pieces[i].astype(f32)
    slot = lax.broadcasted_iota(jnp.int32, total.shape, 0)
    residual = jnp.where(slot == moved_slot[0], other_residual[...], own_residual[...])
    out[...] = (residual + total).astype(bf16)


def final(migrate, pieces, own_residual, other_residual):
    return pl.pallas_call(
        final_kernel,
        out_shape=jax.ShapeDtypeStruct(own_residual.shape, bf16),
        in_specs=[smem()] + [vmem()] * 3,
        out_specs=vmem(),
        name="final",
    )(migrate, pieces, own_residual, other_residual)


def shards(
    hidden,
    lengths,
    migrate,
    kv_cache,
    attn_gain,
    moe_gain,
    w_query,
    key_value_weight,
    output_weight,
    w_gateup,
    w_down,
    expert_ids,
    expert_gates,
):
    rows = hidden.shape[0]
    rep, req, tp = lax.axis_index("rep"), lax.axis_index("req"), lax.axis_index("tp")
    n_rep, n_req, n_tp = lax.axis_size("rep"), lax.axis_size("req"), lax.axis_size("tp")
    n_experts = n_rep * n_req
    place = jnp.stack([rep, tp, rep * n_req + req, jnp.int32(n_experts)]).astype(jnp.int32)

    if n_tp == 2:
        parts = [hidden, swapped(hidden, "tp")]
    else:
        parts = [lax.all_gather(hidden, "tp", axis=1, tiled=True)]

    span = lax.dynamic_index_in_dim(lengths, rep, 0, keepdims=False)
    half = HEAD // 2
    inv_freq = ROPE_BASE ** (-jnp.arange(half, dtype=f32) * 2.0 / HEAD)
    angles = span.astype(f32)[:, None] * inv_freq
    cosine, sine = jnp.cos(angles), jnp.sin(angles)
    cosine = jnp.concatenate([cosine] * 4, axis=1)
    sine = jnp.concatenate([-sine, sine, -sine, sine], axis=1)

    kv_rows = kv_cache.reshape(rows, -1, LANES)
    tokens, keep, send = attention(
        place,
        lengths,
        parts,
        cosine,
        sine,
        attn_gain[None, :],
        w_query,
        key_value_weight,
        output_weight,
        kv_rows,
    )
    if n_tp == 2:
        other = swapped(send, "tp")
    else:
        other = lax.psum(keep.astype(bf16), "tp").astype(f32) - keep
    extra = -(-(2 * n_experts + 1) // LANES) * LANES
    payload, residual = expert_input(
        n_tp, n_req, extra, place, migrate, tokens, keep, other, moe_gain[None, :], expert_ids, expert_gates
    )
    other_residual = swapped(residual, "rep")
    x_own = lax.all_to_all(payload, "req", split_axis=0, concat_axis=0, tiled=True)
    x_own = x_own.reshape(n_req * rows, -1)
    x_other = swapped(x_own, "rep")
    gate_up = w_gateup[0].reshape(w_gateup.shape[1], -1)
    down = w_down[0]
    y_own = own_expert(x_own, gate_up, down)
    mix_keep, mix_send = other_expert(place, x_own, x_other, y_own, gate_up, down)
    mix_recv = swapped(mix_send, "rep")
    pieces = pair_sum(n_tp, n_req, mix_keep, mix_recv)
    pieces = pieces.reshape(n_req * n_tp, rows, -1)
    pieces = lax.all_to_all(pieces, ("req", "tp"), split_axis=0, concat_axis=0, tiled=True)
    return final(migrate, pieces, residual, other_residual)


def solution(mesh):
    placed = (
        P(("rep", "req"), "tp"),
        P(None, "req"),
        P("req"),
        P(("rep", "req"), None, "tp", None),
        P(),
        P(),
        P(None, "tp"),
        P(None, "tp"),
        P("tp", None),
        P(("rep", "req"), None, None, "tp"),
        P(("rep", "req"), "tp", None),
        P(("rep", "req"), None),
        P(("rep", "req"), None),
    )
    return jax.shard_map(
        shards, mesh=mesh, in_specs=placed, out_specs=P(("rep", "req"), "tp"), check_vma=False
    )
```

time: 178 us -> 73.9 us (0.42)
  local copies, waits for them, and re-layouts: 56.4 us -> 11.8 us
  matrix products: 19.9 us -> 0 us
  blocking collectives: 38.7 us -> 21.8 us
  other arithmetic: 16.1 us -> 0.98 us
  Pallas kernels: 0 us -> 14.7 us
  between operations: 14.4 us -> 0.78 us
  waiting for transfers between devices: 25.3 us -> 15.6 us
  starting transfers between devices: 6.32 us -> 8.93 us
    dot_general x10 -> x0, matrix products: 19.9 us -> none  [the longest x1 5.72 us: attention(): jnp.einsum('rhgt,rthd->rhgd', cache_weight, cache_values, preferred_eleme...]
    unnamed x27 -> x39, local copies, waits for them, and re-layouts: 30.1 us -> 10.5 us
    slice x2 -> x0, local copies, waits for them, and re-layouts: 19.2 us -> none  [the longest x1 18.5 us: shards(): moved_cache = arrived[:, :cache_width].reshape(picked_cache.shape)]
    pallas_call x0 -> x6, Pallas kernels: none -> 14.7 us  [the longest x1 8.51 us: attention(): pl.pallas_call(lambda *refs: attention_kernel(len(parts), *refs), out_sha...]
    concatenate x2 -> x1, other arithmetic: 10.6 us -> 0.08 us  [shards(): cosine = jnp.concatenate([cosine] * 4, axis=1)]
    psum x1 -> x0, blocking collectives: 9.31 us -> none  [attention(): lax.psum(partial_out.astype(jnp.bfloat16), 'tp').astype(jnp.float32)]
    reduce_scatter x1 -> x0, waiting for transfers between devices: 6.98 us -> none  [shards(): lax.psum_scatter(combined.astype(jnp.bfloat16), 'tp', scatter_dimension=1...]
    all_to_all x1, waiting for transfers between devices: 18.3 us -> 11.8 us  [shards(): lax.all_to_all(pieces, ('req', 'tp'), split_axis=0, concat_axis=0, tiled=...]
  transfers between devices with their start and end apart: 3 -> 6, of which waited for: 2 -> 5; matrix products, arithmetic and copies ran while one was open for 18% -> 5% of each run, Pallas kernels for 0% -> 1%
where the time goes in v1:
time: 73.9 us; the launch traced here: 74.5 us
  blocking collectives  21.8 us (29%)
  waiting for transfers between devices  15.6 us (21%)
  Pallas kernels  14.7 us (20%)
  local copies, waits for them, and re-layouts  11.8 us (16%)
  starting transfers between devices  8.93 us (12%)
  other arithmetic  0.98 us (1%)
  between operations  0.78 us (1%)
    all_to_all x1, blocking collectives, shards(): lax.all_to_all(payload, 'req', split_axis=0, concat_axis=0, tiled=True)  21.8 us
    all_to_all x1, waiting for transfers between devices, shards(): lax.all_to_all(pieces, ('req', 'tp'), split_axis=0, concat_axis=0, tiled=...  11.8 us
    unnamed x39, local copies, waits for them, and re-layouts  10.5 us
    pallas_call x1, Pallas kernels, attention(): pl.pallas_call(lambda *refs: attention_kernel(len(parts), *refs), out_sha...  8.51 us
    ppermute x5, starting transfers between devices, swapped(): lax.ppermute(value, axis, [(i, i ^ 1) for i in range(lax.axis_size(axis))])  5.34 us
    ppermute x5, waiting for transfers between devices, swapped(): lax.ppermute(value, axis, [(i, i ^ 1) for i in range(lax.axis_size(axis))])  3.78 us
    all_to_all x1, starting transfers between devices, shards(): lax.all_to_all(pieces, ('req', 'tp'), split_axis=0, concat_axis=0, tiled=...  3.59 us
    pallas_call x1, Pallas kernels, expert_input(): pl.pallas_call(lambda *refs: expert_input_kernel(n_tp, *refs), out_shape=...  1.83 us
  transfers between devices with their start and end apart: 6, of which 5 were waited for; matrix products, arithmetic and copies ran while one was open for 5% of the time, Pallas kernels for 1%

profile of v1, /device:TPU:0, one launch (start us, length us, event | category | flops | bytes accessed | tf_op | source)
XLA Modules:
  0.0 74.5 jit_solution(13105424564749430479)
XLA Ops:
  0.0 2.9 %collective-permute-start = (bf16[16,768]{1,0:T(8,128)(2,1)}, bf16[16,768]{1,0:T(8,128)(2,1)S(1)}, u32[]{:S(2)}, u32[]{:S(2)}) collective-permute-start(bf16[16,768]{1,0:T(8,128)(2,1)} %refs_2_.1), channel_id=1, source_target_pairs={{0,1},{1,0},{2,3},{3,2},{4,5},{5,4},{6,7},{7,6},{8,9},{9,8},{10,11... | collective-permute-start | bytes 73736 | tf_op jit(solution)/shard_map/ppermute | solution.py:35
  3.0 0.7 convert_bitcast_fusion
  3.9 0.7 broadcast_in_dim.8.refs_6_
  4.6 0.3 collective-permute-done.refs_3_
  5.0 1.7 %copy-done.1 = bf16[1536,768]{1,0:T(8,128)(2,1)S(1)} copy-done((bf16[1536,768]{1,0:T(8,128)(2,1)S(1)}, bf16[1536,768]{1,0:T(8,128)(2,1)}, u32[]{:S(2)}) %copy-start.1) | copy-done | bytes 2359320
  6.6 1.7 %copy-done.2 = bf16[768,1536]{1,0:T(8,128)(2,1)S(1)} copy-done((bf16[768,1536]{1,0:T(8,128)(2,1)S(1)}, bf16[768,1536]{1,0:T(8,128)(2,1)}, u32[]{:S(2)}) %copy-start.2) | copy-done | bytes 2359320
  8.3 1.4 %copy-done.3 = bf16[1536,512]{1,0:T(8,128)(2,1)S(1)} copy-done((bf16[1536,512]{1,0:T(8,128)(2,1)S(1)}, bf16[1536,512]{1,0:T(8,128)(2,1)}, u32[]{:S(2)}) %copy-start.3) | copy-done | bytes 1572888
  9.7 0.7 copy-done.6
  10.4 0.7 copy-done.9
  11.1 8.5 %attention.1 = (bf16[16,1536]{1,0:T(8,128)(2,1)S(1)}, f32[16,1536]{1,0:T(8,128)S(1)}, bf16[16,1536]{1,0:T(8,128)(2,1)S(1)}) custom-call(s32[4]{0:T(128)S(1)} %pad_add_fusion.refs_0_.place, s32[2,16]{1,0:T(2,128)S(1)} %copy-done.9, bf16[16,768]{1,0:T(8,128)(2,1)S(1)} %copy-done.6, bf16[16,768]{1,0:T(8,128)(2,1)S(1)} %collective-permute-done.refs_3_, ...), custom_call_target="tpu_custom_call" | custom-call | tf_op jit(solution)/shard_map/attention/pallas_call | solution.py:201
  19.7 0.6 copy-done.4
  20.3 0.6 copy-done.5
  20.9 2.0 %collective-permute-start.1 = (bf16[16,1536]{1,0:T(8,128)(2,1)S(1)}, bf16[16,1536]{1,0:T(8,128)(2,1)S(1)}, u32[]{:S(2)}, u32[]{:S(2)}) collective-permute-start(bf16[16,1536]{1,0:T(8,128)(2,1)S(1)} %get-tuple-element.14), channel_id=1, source_target_pairs={{0,1},{1,0},{2,3},{3,2},{4,5},{5,4},{6,7},{7,6},{8,9},{9,8},{10,11... | collective-permute-start | bytes 147464 | tf_op jit(solution)/shard_map/ppermute | solution.py:35
  23.6 0.7 copy.14.refs_6_
  24.3 0.7 copy.15.refs_7_
  24.9 0.6 broadcast_in_dim.9.refs_5_
  25.5 0.6 copy-done.13
  26.2 1.8 %expert_input.1 = (bf16[8,16,1664]{2,1,0:T(8,128)(2,1)}, f32[16,768]{1,0:T(8,128)}) custom-call(s32[4]{0:T(128)} %copy-done.7, s32[1]{0:T(128)S(6)} %copy.17.refs_1_.moved_slot, bf16[16,1536]{1,0:T(8,128)(2,1)} %copy-done.5, f32[16,1536]{1,0:T(8,128)} %copy-done.4, bf16[16,1536]{1,0:T(8,128)(2,1)} %copy-done.13, f32[1,1536]{1,0:T(1,128)} %broadcast_in_dim.9.refs_5_, ...), custom_call_target="tpu_custom_call" | custom-call | tf_op jit(solution)/shard_map/expert_input/pallas_call | solution.py:263
  28.0 21.8 %all_to_all.10 = bf16[8,16,1664]{2,1,0:T(8,128)(2,1)S(1)} all-to-all(bf16[8,16,1664]{2,1,0:T(8,128)(2,1)} %get-tuple-element.15), channel_id=1, replica_groups=mesh['rep'=2,'req'=8,'tp'=2] {'req'}, dimensions={0} | all-to-all | bytes 851968 | tf_op jit(solution)/shard_map/all_to_all | solution.py:428
  49.8 0.4 copy.16
  50.2 0.6 own_expert.1.y_own
  50.8 0.8 %collective-permute-done.2.x_other = bf16[128,1664]{1,0:T(8,128)(2,1)S(1)} collective-permute-done((bf16[128,1664]{1,0:T(8,128)(2,1)S(1)}, bf16[128,1664]{1,0:T(8,128)(2,1)S(1)}, u32[]{:S(2)}, u32[]{:S(2)}) %collective-permute-start.2) | collective-permute-done | bytes 426016 | tf_op jit(solution)/shard_map/ppermute | solution.py:35
  51.5 1.2 %other_expert.1 = (f32[128,1536]{1,0:T(8,128)S(1)}, bf16[128,1536]{1,0:T(8,128)(2,1)S(1)}) custom-call(s32[4]{0:T(128)S(1)} %copy-done.8, bf16[128,1664]{1,0:T(8,128)(2,1)S(1)} %bitcast.16, bf16[128,1664]{1,0:T(8,128)(2,1)S(1)} %collective-permute-done.2.x_other, f32[128,1536]{1,0:T(8,128)S(1)} %own_expert.1.y_own, bf16[1536,512]{1,0:T(8,128)(2,1)S(1)} %bitcast.13, ...), custom_call_target="tpu_custom_call" | custom-call | tf_op jit(solution)/shard_map/other_expert/pallas_call | solution.py:320
  52.7 0.2 collective-permute-start.3
  52.9 1.6 %collective-permute-done.3.refs_1_ = bf16[128,1536]{1,0:T(8,128)(2,1)S(1)} collective-permute-done((bf16[128,1536]{1,0:T(8,128)(2,1)S(1)}, bf16[128,1536]{1,0:T(8,128)(2,1)S(1)}, u32[]{:S(2)}, u32[]{:S(2)}) %collective-permute-start.3) | collective-permute-done | bytes 393248 | tf_op jit(solution)/shard_map/ppermute | solution.py:35
  54.5 0.8 %pair_sum.1 = bf16[8,2,16,768]{3,2,1,0:T(8,128)(2,1)} custom-call(f32[128,1536]{1,0:T(8,128)S(1)} %get-tuple-element.16.refs_0_, bf16[128,1536]{1,0:T(8,128)(2,1)S(1)} %collective-permute-done.3.refs_1_), custom_call_target="tpu_custom_call" | custom-call | tf_op jit(solution)/shard_map/pair_sum/pallas_call | solution.py:343
  55.3 3.6 %all-to-all-start.1 = ((bf16[16,16,768]{2,1,0:T(8,128)(2,1)}), bf16[16,16,768]{2,1,0:T(8,128)(2,1)S(1)}, u32[]{:S(2)}, u32[]{:S(2)}) async-start(bf16[16,16,768]{2,1,0:T(8,128)(2,1)} %bitcast.7), calls=%async_computation.1 | async-start | bytes 786432 | tf_op jit(solution)/shard_map/all_to_all | solution.py:438
  59.0 0.2 collective-permute-start.4
  59.1 1.1 %collective-permute-done.4.other_residual = f32[16,768]{1,0:T(8,128)S(1)} collective-permute-done((f32[16,768]{1,0:T(8,128)S(1)}, f32[16,768]{1,0:T(8,128)S(1)}, u32[]{:S(2)}, u32[]{:S(2)}) %collective-permute-start.4) | collective-permute-done | bytes 49184 | tf_op jit(solution)/shard_map/ppermute | solution.py:35
  60.3 11.8 %all-to-all-done.1.pieces = bf16[16,16,768]{2,1,0:T(8,128)(2,1)S(1)} async-done(((bf16[16,16,768]{2,1,0:T(8,128)(2,1)}), bf16[16,16,768]{2,1,0:T(8,128)(2,1)S(1)}, u32[]{:S(2)}, u32[]{:S(2)}) %all-to-all-start.1) | async-done | bytes 393248 | tf_op jit(solution)/shard_map/all_to_all | solution.py:438
  72.0 0.8 %copy-done.11 = bf16[16,16,768]{2,1,0:T(8,128)(2,1)} copy-done((bf16[16,16,768]{2,1,0:T(8,128)(2,1)}, bf16[16,16,768]{2,1,0:T(8,128)(2,1)S(1)}, u32[]{:S(2)}) %copy-start.11) | copy-done | bytes 393240
  72.8 1.7 %final.1 = bf16[16,768]{1,0:T(8,128)(2,1)} custom-call(s32[1]{0:T(128)S(6)} %copy.17.refs_1_.moved_slot, bf16[16,16,768]{2,1,0:T(8,128)(2,1)} %copy-done.11, f32[16,768]{1,0:T(8,128)} %get-tuple-element.18.own_residual, f32[16,768]{1,0:T(8,128)} %copy-done.14), custom_call_target="tpu_custom_call" | custom-call | tf_op jit(solution)/shard_map/final/pallas_call | solution.py:363
  (33 shorter events, 0.3 us)
Async XLA Ops:
  0.0 5.0 %collective-permute-start = (bf16[16,768]{1,0:T(8,128)(2,1)}, bf16[16,768]{1,0:T(8,128)(2,1)S(1)}, u32[]{:S(2)}, u32[]{:S(2)}) collective-permute-start(bf16[16,768]{1,0:T(8,128)(2,1)} %refs_2_.1), channel_id=1, source_target_pairs={{0,1},{1,0},{2,3},{3,2},{4,5},{5,4},{6,7},{7,6},{8,9},{9,8},{10,11... | collective-permute-start | bytes 73736 | tf_op jit(solution)/shard_map/ppermute | solution.py:35
  3.9 15.7 %copy-start.7 = (s32[4]{0:T(128)}, s32[4]{0:T(128)S(1)}, u32[]{:S(2)}) copy-start(s32[4]{0:T(128)S(1)} %pad_add_fusion.refs_0_.place) | copy-start | bytes 52
  5.0 1.7 %copy-start.1 = (bf16[1536,768]{1,0:T(8,128)(2,1)S(1)}, bf16[1536,768]{1,0:T(8,128)(2,1)}, u32[]{:S(2)}) copy-start(bf16[1536,768]{1,0:T(8,128)(2,1)} %refs_7_.2) | copy-start | bytes 7077892
  6.6 1.7 %copy-start.2 = (bf16[768,1536]{1,0:T(8,128)(2,1)S(1)}, bf16[768,1536]{1,0:T(8,128)(2,1)}, u32[]{:S(2)}) copy-start(bf16[768,1536]{1,0:T(8,128)(2,1)} %refs_9_.1) | copy-start | bytes 7077892
  8.3 1.4 %copy-start.3 = (bf16[1536,512]{1,0:T(8,128)(2,1)S(1)}, bf16[1536,512]{1,0:T(8,128)(2,1)}, u32[]{:S(2)}) copy-start(bf16[1536,512]{1,0:T(8,128)(2,1)} %refs_8_.1) | copy-start | bytes 4718596
  9.7 0.7 copy-start.6
  10.4 0.7 copy-start.9
  11.1 12.5 %copy-start.16 = (s32[16,8]{0,1:T(8,128)S(1)}, s32[16,8]{0,1:T(8,128)}, u32[]{:S(2)}) copy-start(s32[16,8]{0,1:T(8,128)} %param.24) | copy-start | bytes 1540
  11.1 13.2 %copy-start.17 = (f32[16,8]{0,1:T(8,128)S(1)}, f32[16,8]{0,1:T(8,128)}, u32[]{:S(2)}) copy-start(f32[16,8]{0,1:T(8,128)} %param.25) | copy-start | bytes 1540
  11.1 13.8 %copy-start.15 = (f32[1536]{0:T(1024)S(1)}, f32[1536]{0:T(1024)}, u32[]{:S(2)}) copy-start(f32[1536]{0:T(1024)} %param.18) | copy-start | bytes 18436
  11.1 38.7 %copy-start.10 = (bf16[1,1536,2,256]{3,2,1,0:T(2,128)(2,1)S(1)}, bf16[1,1536,2,256]{3,2,1,0:T(2,128)(2,1)}, u32[]{:S(2)}) copy-start(bf16[1,1536,2,256]{3,2,1,0:T(2,128)(2,1)} %param.22) | copy-start | bytes 4718596
  19.7 0.6 copy-start.4
  20.3 0.6 copy-start.5
  20.9 29.2 %copy-start = (bf16[1,256,1536]{2,1,0:T(8,128)(2,1)S(1)}, bf16[1,256,1536]{2,1,0:T(8,128)(2,1)}, u32[]{:S(2)}) copy-start(bf16[1,256,1536]{2,1,0:T(8,128)(2,1)} %param.23) | copy-start | bytes 2359300
  20.9 4.6 %collective-permute-start.1 = (bf16[16,1536]{1,0:T(8,128)(2,1)S(1)}, bf16[16,1536]{1,0:T(8,128)(2,1)S(1)}, u32[]{:S(2)}, u32[]{:S(2)}) collective-permute-start(bf16[16,1536]{1,0:T(8,128)(2,1)S(1)} %get-tuple-element.14), channel_id=1, source_target_pairs={{0,1},{1,0},{2,3},{3,2},{4,5},{5,4},{6,7},{7,6},{8,9},{9,8},{10,11... | collective-permute-start | bytes 147464 | tf_op jit(solution)/shard_map/ppermute | solution.py:35
  25.5 0.6 copy-start.13
  49.8 1.8 %collective-permute-start.2 = (bf16[128,1664]{1,0:T(8,128)(2,1)S(1)}, bf16[128,1664]{1,0:T(8,128)(2,1)S(1)}, u32[]{:S(2)}, u32[]{:S(2)}) collective-permute-start(bf16[128,1664]{1,0:T(8,128)(2,1)S(1)} %bitcast.14), channel_id=1, source_target_pairs={{0,16},{16,0},{1,17},{17,1},{2,18},{18,2},{3,19},{19,3},{4,20},{20... | collective-permute-start | bytes 1277960 | tf_op jit(solution)/shard_map/ppermute | solution.py:35
  50.1 1.4 %copy-start.8 = (s32[4]{0:T(128)S(1)}, s32[4]{0:T(128)}, u32[]{:S(2)}) copy-start(s32[4]{0:T(128)} %copy-done.7) | copy-start | bytes 52
  50.8 8.2 %copy-start.12 = (f32[16,768]{1,0:T(8,128)S(1)}, f32[16,768]{1,0:T(8,128)}, u32[]{:S(2)}) copy-start(f32[16,768]{1,0:T(8,128)} %get-tuple-element.18.own_residual) | copy-start | bytes 147460
  52.7 1.8 %collective-permute-start.3 = (bf16[128,1536]{1,0:T(8,128)(2,1)S(1)}, bf16[128,1536]{1,0:T(8,128)(2,1)S(1)}, u32[]{:S(2)}, u32[]{:S(2)}) collective-permute-start(bf16[128,1536]{1,0:T(8,128)(2,1)S(1)} %get-tuple-element.17), channel_id=1, source_target_pairs={{0,16},{16,0},{1,17},{17,1},{2,18},{18,2},{3,19},{19,3},{4,20},{20... | collective-permute-start | bytes 1179656 | tf_op jit(solution)/shard_map/ppermute | solution.py:35
  55.3 16.7 %all-to-all-start.1 = ((bf16[16,16,768]{2,1,0:T(8,128)(2,1)}), bf16[16,16,768]{2,1,0:T(8,128)(2,1)S(1)}, u32[]{:S(2)}, u32[]{:S(2)}) async-start(bf16[16,16,768]{2,1,0:T(8,128)(2,1)} %bitcast.7), calls=%async_computation.1 | async-start | bytes 786432 | tf_op jit(solution)/shard_map/all_to_all | solution.py:438
  59.0 1.3 %collective-permute-start.4 = (f32[16,768]{1,0:T(8,128)S(1)}, f32[16,768]{1,0:T(8,128)S(1)}, u32[]{:S(2)}, u32[]{:S(2)}) collective-permute-start(f32[16,768]{1,0:T(8,128)S(1)} %copy-done.12), channel_id=1, source_target_pairs={{0,16},{16,0},{1,17},{17,1},{2,18},{18,2},{3,19},{19,3},{4,20},{20... | collective-permute-start | bytes 147464 | tf_op jit(solution)/shard_map/ppermute | solution.py:35
  60.3 11.8 %copy-start.14 = (f32[16,768]{1,0:T(8,128)}, f32[16,768]{1,0:T(8,128)S(1)}, u32[]{:S(2)}) copy-start(f32[16,768]{1,0:T(8,128)S(1)} %collective-permute-done.4.other_residual) | copy-start | bytes 147460
  72.0 0.8 %copy-start.11 = (bf16[16,16,768]{2,1,0:T(8,128)(2,1)}, bf16[16,16,768]{2,1,0:T(8,128)(2,1)S(1)}, u32[]{:S(2)}) copy-start(bf16[16,16,768]{2,1,0:T(8,128)(2,1)S(1)} %all-to-all-done.1.pieces) | copy-start | bytes 1179652

commit v2 on v1

v2 whole, which is shorter than its diff:
```python
import jax
import jax.numpy as jnp
from jax import lax
from jax.experimental import pallas as pl
from jax.experimental.pallas import tpu as pltpu
from jax.sharding import PartitionSpec as P

HEAD = 64
EPS = 1e-06
ROPE_BASE = 10000.0
MASKED = -1e30
LANES = 128
QROWS = 16
SPAN = 128
UNROLL = 16
PIECES = 4
MIB = 1 << 20

bf16 = jnp.bfloat16
f32 = jnp.float32


def vmem():
    return pl.BlockSpec(memory_space=pltpu.VMEM)


def smem():
    return pl.BlockSpec(memory_space=pltpu.SMEM)


def hbm():
    return pl.BlockSpec(memory_space=pl.ANY)


def swapped(value, axis):
    return lax.ppermute(value, axis, [(i, i ^ 1) for i in range(lax.axis_size(axis))])


def normed_rows(rows, gain):
    mean_square = jnp.mean(rows * rows, axis=-1, keepdims=True)
    return (rows * lax.rsqrt(mean_square + EPS) * gain).astype(bf16)


def fetch_kernel(wide, per, *refs):
    (lens_hbm, moved_slot, ids_hbm, gates_hbm, gain_hbm, own_hbm, wq_hbm, wkv_hbm) = refs[:8]
    (own, wq, wkv, gain, cos_out, sin_out, table_out, spans, items, count, moved_out) = refs[8:19]
    lens, ids_t, gates_t, sems = refs[19:]
    rows = own.shape[0]
    rep = lax.axis_index("rep")

    pairs = (
        (lens_hbm, lens),
        (ids_hbm, ids_t),
        (gates_hbm, gates_t),
        (own_hbm, own),
        (gain_hbm, gain),
    )
    for src, dst in ((wq_hbm, wq), (wkv_hbm, wkv)):
        part = src.shape[0] // PIECES
        pairs += tuple((src.at[pl.ds(i * part, part)], dst.at[pl.ds(i * part, part)]) for i in range(PIECES))
    copies = [pltpu.make_async_copy(src, dst, sems.at[i]) for i, (src, dst) in enumerate(pairs)]
    for copy in copies:
        copy.start()

    lane = lax.broadcasted_iota(jnp.int32, (rows, LANES), 1)
    slot = lax.broadcasted_iota(jnp.int32, (rows, LANES), 0)
    half = HEAD // 2
    freq = jnp.zeros((1, LANES), f32)
    for i in range(half):
        freq = jnp.where(lane[:1] % half == i, ROPE_BASE ** (-2.0 * i / HEAD), freq)

    for copy in copies[:3]:
        copy.wait()
    span = jnp.zeros((rows, LANES), jnp.int32)
    for r in range(rows):
        span = jnp.where(slot == r, lens[rep, r], span)
        spans[r] = lens[rep, r]
    angle = span.astype(f32) * freq
    sine = jnp.sin(angle)
    cos_out[...] = jnp.cos(angle)
    sin_out[...] = jnp.where(lane % HEAD < half, -sine, sine)

    n_experts = lax.axis_size("rep") * lax.axis_size("req")
    extra = table_out.shape[1]
    lane = lax.broadcasted_iota(jnp.int32, (rows, extra), 1)
    slot = lax.broadcasted_iota(jnp.int32, (rows, extra), 0)
    ids, gates = jnp.transpose(ids_t[...]), jnp.transpose(gates_t[...])
    table = jnp.where((lane == 2 * n_experts) & (slot == moved_slot[0]), 1.0, jnp.zeros((rows, extra), f32))
    for k in range(ids.shape[1]):
        chosen, weight = ids[:, k : k + 1], gates[:, k : k + 1]
        top = weight.astype(bf16).astype(f32)
        table = jnp.where(lane == chosen, top, table)
        table = jnp.where(lane == chosen + n_experts, weight - top, table)
    table_out[...] = table.astype(bf16)

    def plan_row(r, n):
        def plan_chunk(c, n):
            items[n] = r * per + c
            return n + 1

        return lax.fori_loop(0, (spans[r] + SPAN - 1) // SPAN, plan_chunk, n)

    total = lax.fori_loop(0, rows, plan_row, 0)
    for u in range(UNROLL):
        items[total + u] = rows * per
    count[0] = total
    moved_out[0] = moved_slot[0]

    for copy in copies[3:]:
        copy.wait()


def far(*arrays):
    return [pltpu.with_memory_space_constraint(x, pltpu.HBM) for x in arrays]


def close(*arrays):
    return [pltpu.with_memory_space_constraint(x, pltpu.SMEM) for x in arrays]


def near(*arrays):
    return [pltpu.with_memory_space_constraint(x, pltpu.VMEM) for x in arrays]


def fetch(extra, lens, migrate, ids, gates, gain, own, wq, wkv, kv):
    rows = own.shape[0]
    wide = SPAN * (wkv.shape[1] // (2 * HEAD))
    per = kv.shape[1] // wide
    outs = [(own.shape, bf16), (wq.shape, bf16), (wkv.shape, bf16), (gain.shape, f32)]
    outs += [((rows, LANES), f32), ((rows, LANES), f32), ((rows, extra), bf16)]
    scalars = [(rows,), (rows * per + UNROLL,), (1,), (1,)]
    return pl.pallas_call(
        lambda *refs: fetch_kernel(wide, per, *refs),
        out_shape=tuple(pltpu.VMEM(shape, dtype) for shape, dtype in outs)
        + tuple(pltpu.SMEM(shape, jnp.int32) for shape in scalars),
        in_specs=[hbm(), smem()] + [hbm()] * 6,
        out_specs=(vmem(),) * len(outs) + (smem(),) * len(scalars),
        scratch_shapes=[
            pltpu.SMEM(lens.shape, jnp.int32),
            pltpu.VMEM(ids.shape[::-1], jnp.int32),
            pltpu.VMEM(gates.shape[::-1], f32),
            pltpu.SemaphoreType.DMA((5 + 2 * PIECES,)),
        ],
        compiler_params=pltpu.CompilerParams(vmem_limit_bytes=8 * MIB),
        name="fetch",
    )(*far(lens), migrate, *far(ids.T, gates.T, gain, own, wq, wkv))


def attention_kernel(n_parts, *refs):
    spans, items, count = refs[:3]
    refs = refs[3:]
    parts = refs[:n_parts]
    (cos_ref, sin_ref, gain_ref, wq, wkv, wo_hbm, kv_hbm) = refs[n_parts : 7 + n_parts]
    (tok_out, keep_out, send_out) = refs[7 + n_parts : 10 + n_parts]
    (wo, kvbuf, qf, qb, kvn, mixes, sums, peaks, macc, lacc, oacc, ctx, wsem, ksem) = refs[10 + n_parts :]
    rows = tok_out.shape[0]
    n_query = wq.shape[1] // HEAD
    n_kv = wkv.shape[1] // (2 * HEAD)
    group = n_query // n_kv
    wide = SPAN * n_kv
    per = kv_hbm.shape[1] // wide
    tp = lax.axis_index("tp")

    def kv_copy(r):
        size = pl.multiple_of((spans[r] + SPAN - 1) // SPAN * wide, wide)
        return pltpu.make_async_copy(
            kv_hbm.at[r, pl.ds(0, size)], kvbuf.at[r, pl.ds(0, size)], ksem.at[r]
        )

    total = count[0]
    blocks = (total + UNROLL - 1) // UNROLL
    for r in range(rows // 2):
        kv_copy(r).start()
    part = wo.shape[0] // PIECES
    wo_copies = [
        pltpu.make_async_copy(wo_hbm.at[pl.ds(i * part, part)], wo.at[pl.ds(i * part, part)], wsem.at[i])
        for i in range(PIECES)
    ]
    for copy in wo_copies:
        copy.start()

    if n_parts == 2:
        tokens = jnp.concatenate(
            [
                jnp.where(tp == 0, parts[0][...], parts[1][...]),
                jnp.where(tp == 0, parts[1][...], parts[0][...]),
            ],
            axis=1,
        )
    else:
        tokens = parts[0][...]
    tok_out[...] = tokens
    normed = normed_rows(tokens.astype(f32), gain_ref[...].reshape(1, -1))

    lane = lax.broadcasted_iota(jnp.int32, (rows, LANES), 1)
    low_half = lane < HEAD
    first = lane % HEAD < HEAD // 2
    cosine, sine = cos_ref[...], sin_ref[...]

    def rotate(v):
        partner = jnp.where(first, pltpu.roll(v, LANES - HEAD // 2, 1), pltpu.roll(v, HEAD // 2, 1))
        return v * cosine + partner * sine

    qf[...] = jnp.zeros_like(qf)
    kvn[...] = jnp.zeros_like(kvn)
    macc[...] = jnp.full_like(macc, MASKED)
    lacc[...] = jnp.zeros_like(lacc)
    oacc[...] = jnp.zeros_like(oacc)
    queries = jnp.dot(normed, wq[...], preferred_element_type=f32)
    for k in range(n_query // 2):
        turned = rotate(queries[:, k * LANES : (k + 1) * LANES]).astype(bf16).astype(f32)
        turned = turned * HEAD**-0.5
        qf[pl.ds(2 * k, rows, stride=QROWS), :] = jnp.where(low_half, turned, 0.0)
        qf[pl.ds(2 * k + 1, rows, stride=QROWS), :] = jnp.where(low_half, pltpu.roll(turned, HEAD, 1), 0.0)
    for r in range(rows // 2, rows):
        kv_copy(r).start()
    keyval = jnp.dot(normed, wkv[...], preferred_element_type=f32)
    for h in range(n_kv):
        v = keyval[:, h * LANES : (h + 1) * LANES]
        new = jnp.where(low_half, rotate(v), v).astype(bf16).astype(f32)
        for g in range(group):
            kvn[pl.ds(h * group + g, rows, stride=QROWS), :] = new
    qb[...] = qf[...].astype(bf16).reshape(qb.shape)

    query_row = lax.broadcasted_iota(jnp.int32, (QROWS, wide), 0)
    row_head = sum((query_row >= h * group).astype(jnp.int32) for h in range(1, n_kv + 1))
    column = lax.broadcasted_iota(jnp.int32, (QROWS, wide), 1)
    reach = jnp.where(column % n_kv == row_head, column // n_kv, 1 << 30)

    def folded(op, value):
        out = value[:, :LANES]
        for j in range(1, wide // LANES):
            out = op(out, value[:, j * LANES : (j + 1) * LANES])
        return out

    def chunk(i):
        item = items[i]
        r = item // per
        c = item % per
        kr = jnp.minimum(r, rows - 1)
        return r, c, kvbuf[kr, pl.ds(pl.multiple_of(c * wide, wide), wide), :]

    def arrive(r, carry):
        kv_copy(r).wait()
        return carry

    def block(b, ready):
        last = jnp.minimum(items[b * UNROLL + UNROLL - 1] // per, rows - 1) + 1
        lax.fori_loop(ready, last, arrive, 0)
        got = [chunk(b * UNROLL + u) for u in range(UNROLL)]
        dots = [
            lax.dot_general(qb[r], kv, (((1,), (1,)), ((), ())), preferred_element_type=f32) for r, c, kv in got
        ]
        tops, probs = [], []
        for (r, c, kv), s in zip(got, dots):
            span = spans[jnp.minimum(r, rows - 1)]
            limit = jnp.where(r < rows, span - c * SPAN, 0)
            s = jnp.where(reach < limit, s, MASKED)
            top = jnp.max(folded(jnp.maximum, s), axis=-1, keepdims=True)
            tops.append(jnp.broadcast_to(top, (QROWS, LANES)))
            probs.append(jnp.exp(s - top))
        for u, ((r, c, kv), p) in enumerate(zip(got, probs)):
            i = b * UNROLL + u
            mixes[i] = jnp.dot(p.astype(bf16), kv, preferred_element_type=f32)
            sums[i] = folded(jnp.add, p)
            peaks[i] = tops[u]
        for (r, c, kv), top in zip(got, tops):
            macc[r] = jnp.maximum(macc[r], top)
        return last

    lax.fori_loop(0, blocks, block, 0)

    own = jnp.sum(qf[...] * kvn[...], axis=-1, keepdims=True)
    peak = jnp.maximum(macc[...].reshape(qf.shape), own)
    own_p = jnp.exp(own - peak)
    macc[...] = peak.reshape(macc.shape)

    def merge(b, carry):
        for u in range(UNROLL):
            i = b * UNROLL + u
            r = items[i] // per
            weight = jnp.exp(peaks[i] - macc[r])
            lacc[r] += weight * sums[i]
            oacc[r] += weight * mixes[i]
        return carry

    lax.fori_loop(0, blocks, merge, 0)

    total_p = jnp.sum(lacc[...].reshape(qf.shape), axis=-1, keepdims=True) + own_p
    qf[...] = (oacc[...].reshape(qf.shape) + own_p * kvn[...]) / total_p
    for k in range(n_query // 2):
        a = qf[pl.ds(2 * k, rows, stride=QROWS), :]
        b = qf[pl.ds(2 * k + 1, rows, stride=QROWS), :]
        ctx[:, k * LANES : (k + 1) * LANES] = jnp.where(low_half, pltpu.roll(a, HEAD, 1), b).astype(bf16)
    for copy in wo_copies:
        copy.wait()
    partial = jnp.dot(ctx[...], wo[...], preferred_element_type=f32)
    keep_out[...] = partial
    send_out[...] = partial.astype(bf16)


def attention(plan, parts, cosine, sine, gain, wq, wkv, wo, kv):
    rows = parts[0].shape[0]
    width = wq.shape[0]
    n_kv = wkv.shape[1] // (2 * HEAD)
    per = kv.shape[1] // (SPAN * n_kv)
    slots = rows * per + UNROLL
    many = rows + 1
    return pl.pallas_call(
        lambda *refs: attention_kernel(len(parts), *refs),
        out_shape=(
            pltpu.VMEM((rows, width), bf16),
            pltpu.VMEM((rows, width), f32),
            pltpu.VMEM((rows, width), bf16),
        ),
        in_specs=[smem()] * 3 + [vmem()] * (len(parts) + 5) + [hbm()] * 2,
        out_specs=(vmem(), vmem(), vmem()),
        scratch_shapes=[
            pltpu.VMEM(wo.shape, bf16),
            pltpu.VMEM(kv.shape, bf16),
            pltpu.VMEM((many * QROWS, LANES), f32),
            pltpu.VMEM((many, QROWS, LANES), bf16),
            pltpu.VMEM((many * QROWS, LANES), f32),
            pltpu.VMEM((slots, QROWS, LANES), f32),
            pltpu.VMEM((slots, QROWS, LANES), f32),
            pltpu.VMEM((slots, QROWS, LANES), f32),
            pltpu.VMEM((many, QROWS, LANES), f32),
            pltpu.VMEM((many, QROWS, LANES), f32),
            pltpu.VMEM((many, QROWS, LANES), f32),
            pltpu.VMEM((rows, wq.shape[1]), bf16),
            pltpu.SemaphoreType.DMA((PIECES,)),
            pltpu.SemaphoreType.DMA((rows,)),
        ],
        compiler_params=pltpu.CompilerParams(vmem_limit_bytes=36 * MIB),
        name="attention",
    )(*close(*plan), *near(*parts, cosine, sine, gain, wq, wkv), *far(wo, kv))


def expert_input_kernel(n_tp, tokens, keep, other, gain, table, payload, residual_out):
    width = tokens.shape[1]
    tp = lax.axis_index("tp")
    residual = tokens[...].astype(f32) + keep[...] + other[...].astype(f32)
    part = width // n_tp
    mine = residual[:, :part]
    for t in range(1, n_tp):
        mine = jnp.where(tp == t, residual[:, t * part : (t + 1) * part], mine)
    residual_out[...] = mine
    expert_in = normed_rows(residual, gain[...].reshape(1, -1))
    for q in range(payload.shape[0]):
        payload[q, :, :width] = expert_in
        payload[q, :, width:] = table[...]


def expert_input(n_tp, n_req, tokens, keep, other, gain, table):
    rows, width = tokens.shape
    return pl.pallas_call(
        lambda *refs: expert_input_kernel(n_tp, *refs),
        out_shape=(
            pltpu.VMEM((n_req, rows, width + table.shape[1]), bf16),
            pltpu.VMEM((rows, width // n_tp), f32),
        ),
        in_specs=[vmem()] * 5,
        out_specs=(vmem(), vmem()),
        compiler_params=pltpu.CompilerParams(vmem_limit_bytes=8 * MIB),
        name="expert_input",
    )(*near(tokens, keep, other), gain, *near(table))


def expert_rows(rows, gate_up, down):
    projected = jnp.dot(rows, gate_up, preferred_element_type=f32)
    hidden = projected.shape[1] // 2
    gate, up = projected[:, :hidden], projected[:, hidden:]
    active = (gate / (1.0 + jnp.exp(-gate)) * up).astype(bf16)
    return jnp.dot(active, down, preferred_element_type=f32)


def own_expert_kernel(x, gate_up, down, y):
    width = down.shape[1]
    y[...] = expert_rows(x[:, :width], gate_up[...], down[...])


def own_expert(x, gate_up, down):
    return pl.pallas_call(
        own_expert_kernel,
        out_shape=jax.ShapeDtypeStruct((x.shape[0], down.shape[1]), f32),
        in_specs=[vmem()] * 3,
        out_specs=vmem(),
        compiler_params=pltpu.CompilerParams(vmem_limit_bytes=32 * MIB),
        name="own_expert",
    )(x, gate_up, down)


def other_expert_kernel(x_own, x_other, y_own, gate_up, down, keep, send):
    width = down.shape[1]
    n_req = lax.axis_size("req")
    n_experts = lax.axis_size("rep") * n_req
    expert = lax.axis_index("rep") * n_req + lax.axis_index("req")
    y_other = expert_rows(x_other[:, :width], gate_up[...], down[...])
    own_table = x_own[:, width:].astype(f32)
    other_table = x_other[:, width:].astype(f32)
    lane = lax.broadcasted_iota(jnp.int32, own_table.shape, 1)

    def picked(table, mask):
        return jnp.sum(jnp.where(mask, table, 0.0), axis=-1, keepdims=True)

    mine = (lane == expert) | (lane == expert + n_experts)
    own_gate, other_gate = picked(own_table, mine), picked(other_table, mine)
    moved = picked(own_table, lane == 2 * n_experts) > 0.5
    from_own = y_own[...] * jnp.where(moved, other_gate, own_gate)
    from_other = y_other * jnp.where(moved, own_gate, other_gate)
    keep[...] = jnp.where(moved, from_other, from_own)
    send[...] = jnp.where(moved, from_own, from_other).astype(bf16)


def other_expert(x_own, x_other, y_own, gate_up, down):
    return pl.pallas_call(
        other_expert_kernel,
        out_shape=(
            jax.ShapeDtypeStruct(y_own.shape, f32),
            jax.ShapeDtypeStruct(y_own.shape, bf16),
        ),
        in_specs=[vmem()] * 5,
        out_specs=(vmem(), vmem()),
        compiler_params=pltpu.CompilerParams(vmem_limit_bytes=40 * MIB),
        name="other_expert",
    )(x_own, x_other, y_own, gate_up, down)


def pair_sum_kernel(n_tp, keep, recv, out):
    n_req, _, rows, part = out.shape
    total = (keep[...] + recv[...].astype(f32)).astype(bf16)
    for q in range(n_req):
        for t in range(n_tp):
            out[q, t] = total[q * rows : (q + 1) * rows, t * part : (t + 1) * part]


def pair_sum(n_tp, n_req, keep, recv):
    rows, part = keep.shape[0] // n_req, keep.shape[1] // n_tp
    return pl.pallas_call(
        lambda *refs: pair_sum_kernel(n_tp, *refs),
        out_shape=jax.ShapeDtypeStruct((n_req, n_tp, rows, part), bf16),
        in_specs=[vmem()] * 2,
        out_specs=vmem(),
        compiler_params=pltpu.CompilerParams(vmem_limit_bytes=32 * MIB),
        name="pair_sum",
    )(keep, recv)


def final_kernel(moved_slot, pieces, own_residual, other_residual, out):
    total = pieces[0].astype(f32)
    for i in range(1, pieces.shape[0]):
        total = total + pieces[i].astype(f32)
    slot = lax.broadcasted_iota(jnp.int32, total.shape, 0)
    residual = jnp.where(slot == moved_slot[0], other_residual[...], own_residual[...])
    out[...] = (residual + total).astype(bf16)


def final(moved, pieces, own_residual, other_residual):
    return pl.pallas_call(
        final_kernel,
        out_shape=jax.ShapeDtypeStruct(own_residual.shape, bf16),
        in_specs=[smem()] + [vmem()] * 3,
        out_specs=vmem(),
        compiler_params=pltpu.CompilerParams(vmem_limit_bytes=8 * MIB),
        name="final",
    )(*close(moved), pieces, own_residual, other_residual)


def shards(
    hidden,
    lengths,
    migrate,
    kv_cache,
    attn_gain,
    moe_gain,
    w_query,
    key_value_weight,
    output_weight,
    w_gateup,
    w_down,
    expert_ids,
    expert_gates,
):
    rows = hidden.shape[0]
    n_rep, n_req, n_tp = lax.axis_size("rep"), lax.axis_size("req"), lax.axis_size("tp")
    extra = -(-(2 * n_rep * n_req + 1) // LANES) * LANES

    if n_tp == 2:
        other_part = swapped(hidden, "tp")
    else:
        all_parts = lax.all_gather(hidden, "tp", axis=1, tiled=True)
    kv = kv_cache.reshape(rows, -1, LANES)
    own, wq, wkv, gain, cosine, sine, table, *plan, moved = fetch(
        extra,
        lengths,
        migrate,
        expert_ids,
        expert_gates,
        attn_gain,
        hidden,
        w_query,
        key_value_weight,
        kv,
    )
    parts = [own, other_part] if n_tp == 2 else [all_parts]
    tokens, keep, send = attention(plan, parts, cosine, sine, gain, wq, wkv, output_weight, kv)
    if n_tp == 2:
        other = swapped(send, "tp")
    else:
        other = lax.psum(keep.astype(bf16), "tp").astype(f32) - keep
    payload, residual = expert_input(n_tp, n_req, tokens, keep, other, moe_gain, table)
    other_residual = swapped(residual, "rep")
    x_own = lax.all_to_all(payload, "req", split_axis=0, concat_axis=0, tiled=True)
    x_own = x_own.reshape(n_req * rows, -1)
    x_other = swapped(x_own, "rep")
    gate_up = w_gateup[0].reshape(w_gateup.shape[1], -1)
    down = w_down[0]
    y_own = own_expert(x_own, gate_up, down)
    mix_keep, mix_send = other_expert(x_own, x_other, y_own, gate_up, down)
    mix_recv = swapped(mix_send, "rep")
    pieces = pair_sum(n_tp, n_req, mix_keep, mix_recv)
    pieces = pieces.reshape(n_req * n_tp, rows, -1)
    pieces = lax.all_to_all(pieces, ("req", "tp"), split_axis=0, concat_axis=0, tiled=True)
    return final(moved, pieces, residual, other_residual)


def solution(mesh):
    placed = (
        P(("rep", "req"), "tp"),
        P(None, "req"),
        P("req"),
        P(("rep", "req"), None, "tp", None),
        P(),
        P(),
        P(None, "tp"),
        P(None, "tp"),
        P("tp", None),
        P(("rep", "req"), None, None, "tp"),
        P(("rep", "req"), "tp", None),
        P(("rep", "req"), None),
        P(("rep", "req"), None),
    )
    return jax.shard_map(
        shards, mesh=mesh, in_specs=placed, out_specs=P(("rep", "req"), "tp"), check_vma=False
    )
```

time: 73.9 us -> 58.4 us (0.79)
  local copies, waits for them, and re-layouts: 11.8 us -> 0.35 us
  blocking collectives: 21.8 us -> 18.1 us
  waiting for transfers between devices: 15.6 us -> 18.3 us
  Pallas kernels: 14.7 us -> 12.9 us
  other arithmetic: 0.98 us -> 0 us
  starting transfers between devices: 8.93 us -> 8.05 us
    unnamed x39 -> x7, local copies, waits for them, and re-layouts: 10.5 us -> 0.35 us
    all_to_all x1, blocking collectives: 21.8 us -> 18.1 us  [shards(): lax.all_to_all(payload, 'req', split_axis=0, concat_axis=0, tiled=True)]
    ppermute x5, waiting for transfers between devices: 3.78 us -> 6.5 us  [swapped(): lax.ppermute(value, axis, [(i, i ^ 1) for i in range(lax.axis_size(axis))])]
    pallas_call x0 -> x1, Pallas kernels: none -> 2.25 us  [fetch(): pl.pallas_call(lambda *refs: fetch_kernel(wide, per, *refs), out_shape=tu...]
    pallas_call x1, Pallas kernels: 1.83 us -> 0.13 us  [expert_input(): pl.pallas_call(lambda *refs: expert_input_kernel(n_tp, *refs), out_shape=...]
    broadcast_in_dim x2 -> x0, local copies, waits for them, and re-layouts: 1.31 us -> none  [the longest x1 0.71 us: shards(): attn_gain[None, :]]
    pallas_call x1, Pallas kernels: 1.69 us -> 0.67 us  [final(): pl.pallas_call(final_kernel, out_shape=jax.ShapeDtypeStruct(own_residual....]
    ppermute x5, starting transfers between devices: 5.34 us -> 4.5 us  [swapped(): lax.ppermute(value, axis, [(i, i ^ 1) for i in range(lax.axis_size(axis))])]
  transfers between devices with their start and end apart: 6 -> 6, of which waited for: 5 -> 5; matrix products, arithmetic and copies ran while one was open for 5% -> 1% of each run, Pallas kernels for 1% -> 5%
where the time goes in v2:
time: 58.4 us
  waiting for transfers between devices  18.3 us (31%)
  blocking collectives  18.1 us (31%)
  Pallas kernels  12.9 us (22%)
  starting transfers between devices  8.05 us (14%)
  between operations  0.75 us (1%)
    all_to_all x1, blocking collectives, shards(): lax.all_to_all(payload, 'req', split_axis=0, concat_axis=0, tiled=True)  18.1 us
    all_to_all x1, waiting for transfers between devices, shards(): lax.all_to_all(pieces, ('req', 'tp'), split_axis=0, concat_axis=0, tiled=...  11.8 us
    pallas_call x1, Pallas kernels, attention(): pl.pallas_call(lambda *refs: attention_kernel(len(parts), *refs), out_sha...  7.77 us
    ppermute x5, waiting for transfers between devices, swapped(): lax.ppermute(value, axis, [(i, i ^ 1) for i in range(lax.axis_size(axis))])  6.5 us
    ppermute x5, starting transfers between devices, swapped(): lax.ppermute(value, axis, [(i, i ^ 1) for i in range(lax.axis_size(axis))])  4.5 us
    all_to_all x1, starting transfers between devices, shards(): lax.all_to_all(pieces, ('req', 'tp'), split_axis=0, concat_axis=0, tiled=...  3.55 us
    pallas_call x1, Pallas kernels, fetch(): pl.pallas_call(lambda *refs: fetch_kernel(wide, per, *refs), out_shape=tu...  2.25 us
  transfers between devices with their start and end apart: 6, of which 5 were waited for; matrix products, arithmetic and copies ran while one was open for 1% of the time, Pallas kernels for 5%

profile of v2, /device:TPU:0, one launch (start us, length us, event | category | flops | bytes accessed | tf_op | source)
XLA Modules:
  0.0 58.4 jit_solution(379669687469307638)
XLA Ops:
  0.0 2.9 %collective-permute-start = (bf16[16,768]{1,0:T(8,128)(2,1)}, bf16[16,768]{1,0:T(8,128)(2,1)S(1)}, u32[]{:S(2)}, u32[]{:S(2)}) collective-permute-start(bf16[16,768]{1,0:T(8,128)(2,1)} %refs_5_.1), channel_id=1, source_target_pairs={{0,1},{1,0},{2,3},{3,2},{4,5},{5,4},{6,7},{7,6},{8,9},{9,8},{10,11... | collective-permute-start | bytes 73736 | tf_op jit(solution)/shard_map/ppermute | solution.py:36
  3.6 2.3 %fetch.1 = (bf16[16,768]{1,0:T(8,128)(2,1)S(1)}, bf16[1536,768]{1,0:T(8,128)(2,1)S(1)}, bf16[1536,512]{1,0:T(8,128)(2,1)S(1)}, f32[1536]{0:T(1024)S(1)}, f32[16,...) custom-call(s32[2,16]{1,0:T(2,128)} %refs_0_.1, ...), custom_call_target="tpu_custom_call" | custom-call | tf_op jit(solution)/shard_map/fetch/pallas_call | solution.py:132
  5.8 0.0 collective-permute-done.refs_4_
  5.9 0.0 copy-start.1
  5.9 0.0 copy-start.2
  5.9 7.8 %attention.1 = (bf16[16,1536]{1,0:T(8,128)(2,1)S(1)}, f32[16,1536]{1,0:T(8,128)S(1)}, bf16[16,1536]{1,0:T(8,128)(2,1)S(1)}) custom-call(s32[16]{0:T(128)S(4)} %get-tuple-element.24.refs_0_, s32[144]{0:T(256)S(4)} %get-tuple-element.25.refs_1_, s32[1]{0:T(128)S(4)} %get-tuple-element.26.refs_2_, bf16[16,768]{1,0:T(8,128)(2,1)S(1)} %get-tuple-element.27.refs_3_, ...), custom_call_target="tpu_custom_call" | custom-call | tf_op jit(solution)/shard_map/attention/pallas_call | solution.py:309
  13.7 0.0 copy-start
  13.7 1.2 %collective-permute-start.1 = (bf16[16,1536]{1,0:T(8,128)(2,1)S(1)}, bf16[16,1536]{1,0:T(8,128)(2,1)S(1)}, u32[]{:S(2)}, u32[]{:S(2)}) collective-permute-start(bf16[16,1536]{1,0:T(8,128)(2,1)S(1)} %get-tuple-element.35), channel_id=1, source_target_pairs={{0,1},{1,0},{2,3},{3,2},{4,5},{5,4},{6,7},{7,6},{8,9},{9,8},{10,11... | collective-permute-start | bytes 147464 | tf_op jit(solution)/shard_map/ppermute | solution.py:36
  14.8 3.0 %collective-permute-done.1.refs_2_ = bf16[16,1536]{1,0:T(8,128)(2,1)S(1)} collective-permute-done((bf16[16,1536]{1,0:T(8,128)(2,1)S(1)}, bf16[16,1536]{1,0:T(8,128)(2,1)S(1)}, u32[]{:S(2)}, u32[]{:S(2)}) %collective-permute-start.1) | collective-permute-done | bytes 49184 | tf_op jit(solution)/shard_map/ppermute | solution.py:36
  17.8 0.0 copy-done.1
  17.8 0.1 expert_input.1
  18.0 18.1 %all_to_all.10 = bf16[8,16,1664]{2,1,0:T(8,128)(2,1)S(1)} all-to-all(bf16[8,16,1664]{2,1,0:T(8,128)(2,1)S(1)} %get-tuple-element.37), channel_id=1, replica_groups=mesh['rep'=2,'req'=8,'tp'=2] {'req'}, dimensions={0} | all-to-all | bytes 851968 | tf_op jit(solution)/shard_map/all_to_all | solution.py:513
  36.1 0.0 collective-permute-start.2
  36.1 0.0 copy-done.2
  36.1 0.3 copy.14
  36.4 0.0 copy-done
  36.4 0.6 %own_expert.1.y_own = f32[128,1536]{1,0:T(8,128)S(1)} custom-call(bf16[128,1664]{1,0:T(8,128)(2,1)S(1)} %bitcast.12, bf16[1536,512]{1,0:T(8,128)(2,1)S(1)} %bitcast.9, bf16[256,1536]{1,0:T(8,128)(2,1)S(1)} %bitcast.14), custom_call_target="tpu_custom_call" | custom-call | tf_op jit(solution)/shard_map/own_expert/pallas_call | solution.py:383
  37.0 0.8 %collective-permute-done.2.x_other = bf16[128,1664]{1,0:T(8,128)(2,1)S(1)} collective-permute-done((bf16[128,1664]{1,0:T(8,128)(2,1)S(1)}, bf16[128,1664]{1,0:T(8,128)(2,1)S(1)}, u32[]{:S(2)}, u32[]{:S(2)}) %collective-permute-start.2) | collective-permute-done | bytes 426016 | tf_op jit(solution)/shard_map/ppermute | solution.py:36
  37.8 0.6 %other_expert.1 = (f32[128,1536]{1,0:T(8,128)S(1)}, bf16[128,1536]{1,0:T(8,128)(2,1)S(1)}) custom-call(bf16[128,1664]{1,0:T(8,128)(2,1)S(1)} %bitcast.13, bf16[128,1664]{1,0:T(8,128)(2,1)S(1)} %collective-permute-done.2.x_other, f32[128,1536]{1,0:T(8,128)S(1)} %own_expert.1.y_own, bf16[1536,512]{1,0:T(8,128)(2,1)S(1)} %bitcast.10, bf16[256,1536]{1,0:T(8,128)(2,1)S(1)} %bitcast.15), custom_call_target="tpu_custom_call" | custom-call | tf_op jit(solution)/shard_map/other_expert/pallas_call | solution.py:416
  38.5 0.2 collective-permute-start.3
  38.7 1.6 %collective-permute-done.3.refs_1_ = bf16[128,1536]{1,0:T(8,128)(2,1)S(1)} collective-permute-done((bf16[128,1536]{1,0:T(8,128)(2,1)S(1)}, bf16[128,1536]{1,0:T(8,128)(2,1)S(1)}, u32[]{:S(2)}, u32[]{:S(2)}) %collective-permute-start.3) | collective-permute-done | bytes 393248 | tf_op jit(solution)/shard_map/ppermute | solution.py:36
  40.3 0.8 %pair_sum.1 = bf16[8,2,16,768]{3,2,1,0:T(8,128)(2,1)} custom-call(f32[128,1536]{1,0:T(8,128)S(1)} %get-tuple-element.38.refs_0_, bf16[128,1536]{1,0:T(8,128)(2,1)S(1)} %collective-permute-done.3.refs_1_), custom_call_target="tpu_custom_call" | custom-call | tf_op jit(solution)/shard_map/pair_sum/pallas_call | solution.py:439
  41.1 3.6 %all-to-all-start.1 = ((bf16[16,16,768]{2,1,0:T(8,128)(2,1)}), bf16[16,16,768]{2,1,0:T(8,128)(2,1)S(1)}, u32[]{:S(2)}, u32[]{:S(2)}) async-start(bf16[16,16,768]{2,1,0:T(8,128)(2,1)} %bitcast.5), calls=%async_computation.1 | async-start | bytes 786432 | tf_op jit(solution)/shard_map/all_to_all | solution.py:523
  44.6 0.2 collective-permute-start.4
  44.8 1.1 %collective-permute-done.4.other_residual = f32[16,768]{1,0:T(8,128)S(1)} collective-permute-done((f32[16,768]{1,0:T(8,128)S(1)}, f32[16,768]{1,0:T(8,128)S(1)}, u32[]{:S(2)}, u32[]{:S(2)}) %collective-permute-start.4) | collective-permute-done | bytes 49184 | tf_op jit(solution)/shard_map/ppermute | solution.py:36
  45.9 11.8 %all-to-all-done.1.pieces = bf16[16,16,768]{2,1,0:T(8,128)(2,1)S(1)} async-done(((bf16[16,16,768]{2,1,0:T(8,128)(2,1)}), bf16[16,16,768]{2,1,0:T(8,128)(2,1)S(1)}, u32[]{:S(2)}, u32[]{:S(2)}) %all-to-all-start.1) | async-done | bytes 393248 | tf_op jit(solution)/shard_map/all_to_all | solution.py:523
  57.7 0.7 %final.1 = bf16[16,768]{1,0:T(8,128)(2,1)} custom-call(s32[1]{0:T(128)S(4)} %get-tuple-element.23.moved_slot, bf16[16,16,768]{2,1,0:T(8,128)(2,1)S(1)} %all-to-all-done.1.pieces, f32[16,768]{1,0:T(8,128)S(1)} %get-tuple-element.40.own_residual, f32[16,768]{1,0:T(8,128)S(1)} %collective-permute-done.4.other_residual), custom_call_target="tpu_custom_call" | custom-call | tf_op jit(solution)/shard_map/final/pallas_call | solution.py:459
Async XLA Ops:
  0.0 5.9 %collective-permute-start = (bf16[16,768]{1,0:T(8,128)(2,1)}, bf16[16,768]{1,0:T(8,128)(2,1)S(1)}, u32[]{:S(2)}, u32[]{:S(2)}) collective-permute-start(bf16[16,768]{1,0:T(8,128)(2,1)} %refs_5_.1), channel_id=1, source_target_pairs={{0,1},{1,0},{2,3},{3,2},{4,5},{5,4},{6,7},{7,6},{8,9},{9,8},{10,11... | collective-permute-start | bytes 73736 | tf_op jit(solution)/shard_map/ppermute | solution.py:36
  5.9 12.0 %copy-start.1 = (f32[1536]{0:T(1024)S(1)}, f32[1536]{0:T(1024)}, u32[]{:S(2)}) copy-start(f32[1536]{0:T(1024)} %refs_3_.1) | copy-start | bytes 18436
  5.9 30.2 %copy-start.2 = (bf16[1,1536,2,256]{3,2,1,0:T(2,128)(2,1)S(1)}, bf16[1,1536,2,256]{3,2,1,0:T(2,128)(2,1)}, u32[]{:S(2)}) copy-start(bf16[1,1536,2,256]{3,2,1,0:T(2,128)(2,1)} %param.22) | copy-start | bytes 4718596
  13.7 22.7 %copy-start = (bf16[1,256,1536]{2,1,0:T(8,128)(2,1)S(1)}, bf16[1,256,1536]{2,1,0:T(8,128)(2,1)}, u32[]{:S(2)}) copy-start(bf16[1,256,1536]{2,1,0:T(8,128)(2,1)} %param.23) | copy-start | bytes 2359300
  13.7 4.2 %collective-permute-start.1 = (bf16[16,1536]{1,0:T(8,128)(2,1)S(1)}, bf16[16,1536]{1,0:T(8,128)(2,1)S(1)}, u32[]{:S(2)}, u32[]{:S(2)}) collective-permute-start(bf16[16,1536]{1,0:T(8,128)(2,1)S(1)} %get-tuple-element.35), channel_id=1, source_target_pairs={{0,1},{1,0},{2,3},{3,2},{4,5},{5,4},{6,7},{7,6},{8,9},{9,8},{10,11... | collective-permute-start | bytes 147464 | tf_op jit(solution)/shard_map/ppermute | solution.py:36
  36.1 1.8 %collective-permute-start.2 = (bf16[128,1664]{1,0:T(8,128)(2,1)S(1)}, bf16[128,1664]{1,0:T(8,128)(2,1)S(1)}, u32[]{:S(2)}, u32[]{:S(2)}) collective-permute-start(bf16[128,1664]{1,0:T(8,128)(2,1)S(1)} %bitcast.11), channel_id=1, source_target_pairs={{0,16},{16,0},{1,17},{17,1},{2,18},{18,2},{3,19},{19,3},{4,20},{20... | collective-permute-start | bytes 1277960 | tf_op jit(solution)/shard_map/ppermute | solution.py:36
  38.5 1.8 %collective-permute-start.3 = (bf16[128,1536]{1,0:T(8,128)(2,1)S(1)}, bf16[128,1536]{1,0:T(8,128)(2,1)S(1)}, u32[]{:S(2)}, u32[]{:S(2)}) collective-permute-start(bf16[128,1536]{1,0:T(8,128)(2,1)S(1)} %get-tuple-element.39), channel_id=1, source_target_pairs={{0,16},{16,0},{1,17},{17,1},{2,18},{18,2},{3,19},{19,3},{4,20},{20... | collective-permute-start | bytes 1179656 | tf_op jit(solution)/shard_map/ppermute | solution.py:36
  41.1 16.7 %all-to-all-start.1 = ((bf16[16,16,768]{2,1,0:T(8,128)(2,1)}), bf16[16,16,768]{2,1,0:T(8,128)(2,1)S(1)}, u32[]{:S(2)}, u32[]{:S(2)}) async-start(bf16[16,16,768]{2,1,0:T(8,128)(2,1)} %bitcast.5), calls=%async_computation.1 | async-start | bytes 786432 | tf_op jit(solution)/shard_map/all_to_all | solution.py:523
  44.6 1.3 %collective-permute-start.4 = (f32[16,768]{1,0:T(8,128)S(1)}, f32[16,768]{1,0:T(8,128)S(1)}, u32[]{:S(2)}, u32[]{:S(2)}) collective-permute-start(f32[16,768]{1,0:T(8,128)S(1)} %get-tuple-element.40.own_residual), channel_id=1, source_target_pairs={{0,16},{16,0},{1,17},{17,1},{2,18},{18,2},{3,19},{19,3},{4,20},{20... | collective-permute-start | bytes 147464 | tf_op jit(solution)/shard_map/ppermute | solution.py:36

commit v3 on v2

--- a/solution.py
+++ b/solution.py
@@ -41,10 +41,16 @@
     return (rows * lax.rsqrt(mean_square + EPS) * gain).astype(bf16)
 
 
+def rest_copy(kv_hbm, kvbuf, sem, spans, wide, r):
+    count = (spans[r] + SPAN - 1) // SPAN - 1
+    rest = pl.ds(wide, pl.multiple_of(count * wide, wide))
+    return count > 0, pltpu.make_async_copy(kv_hbm.at[r, rest], kvbuf.at[r, rest], sem.at[r])
+
+
 def fetch_kernel(wide, per, *refs):
-    (lens_hbm, moved_slot, ids_hbm, gates_hbm, gain_hbm, own_hbm, wq_hbm, wkv_hbm) = refs[:8]
-    (own, wq, wkv, gain, cos_out, sin_out, table_out, spans, items, count, moved_out) = refs[8:19]
-    lens, ids_t, gates_t, sems = refs[19:]
+    (lens_hbm, ids_hbm, gates_hbm, gain_hbm, own_hbm, kv_hbm) = refs[:6]
+    (own, gain, cos_out, sin_out, table_out, kvbuf, spans, items, count) = refs[6:15]
+    lens, ids_t, gates_t, sems, ksem = refs[15:]
     rows = own.shape[0]
     rep = lax.axis_index("rep")
 
@@ -55,11 +61,12 @@
         (own_hbm, own),
         (gain_hbm, gain),
     )
-    for src, dst in ((wq_hbm, wq), (wkv_hbm, wkv)):
-        part = src.shape[0] // PIECES
-        pairs += tuple((src.at[pl.ds(i * part, part)], dst.at[pl.ds(i * part, part)]) for i in range(PIECES))
+    first = pl.ds(0, wide)
     copies = [pltpu.make_async_copy(src, dst, sems.at[i]) for i, (src, dst) in enumerate(pairs)]
     for copy in copies:
+        copy.start()
+    head_copies = [pltpu.make_async_copy(kv_hbm.at[r, first], kvbuf.at[r, first], ksem.at[r]) for r in range(rows)]
+    for copy in head_copies:
         copy.start()
 
     lane = lax.broadcasted_iota(jnp.int32, (rows, LANES), 1)
@@ -69,12 +76,29 @@
     for i in range(half):
         freq = jnp.where(lane[:1] % half == i, ROPE_BASE ** (-2.0 * i / HEAD), freq)
 
-    for copy in copies[:3]:
-        copy.wait()
+    copies[0].wait()
+    for r in range(rows):
+        spans[r] = lens[rep, r]
+
+        items[r] = r * per
+
+    def plan_row(r, n):
+        def plan_chunk(c, n):
+            items[n] = r * per + c
+            return n + 1
+
+        return lax.fori_loop(1, (spans[r] + SPAN - 1) // SPAN, plan_chunk, n)
+
+    total = lax.fori_loop(0, rows, plan_row, rows)
+    for u in range(UNROLL):
+        items[total + u] = rows * per
+    count[0] = total
+
+    copies[1].wait()
+    copies[2].wait()
     span = jnp.zeros((rows, LANES), jnp.int32)
     for r in range(rows):
         span = jnp.where(slot == r, lens[rep, r], span)
-        spans[r] = lens[rep, r]
     angle = span.astype(f32) * freq
     sine = jnp.sin(angle)
     cos_out[...] = jnp.cos(angle)
@@ -83,9 +107,8 @@
     n_experts = lax.axis_size("rep") * lax.axis_size("req")
     extra = table_out.shape[1]
     lane = lax.broadcasted_iota(jnp.int32, (rows, extra), 1)
-    slot = lax.broadcasted_iota(jnp.int32, (rows, extra), 0)
     ids, gates = jnp.transpose(ids_t[...]), jnp.transpose(gates_t[...])
-    table = jnp.where((lane == 2 * n_experts) & (slot == moved_slot[0]), 1.0, jnp.zeros((rows, extra), f32))
+    table = jnp.zeros((rows, extra), f32)
     for k in range(ids.shape[1]):
         chosen, weight = ids[:, k : k + 1], gates[:, k : k + 1]
         top = weight.astype(bf16).astype(f32)
@@ -93,19 +116,8 @@
         table = jnp.where(lane == chosen + n_experts, weight - top, table)
     table_out[...] = table.astype(bf16)
 
-    def plan_row(r, n):
-        def plan_chunk(c, n):
-            items[n] = r * per + c
-            return n + 1
-
-        return lax.fori_loop(0, (spans[r] + SPAN - 1) // SPAN, plan_chunk, n)
-
-    total = lax.fori_loop(0, rows, plan_row, 0)
-    for u in range(UNROLL):
-        items[total + u] = rows * per
-    count[0] = total
-    moved_out[0] = moved_slot[0]
-
+    for copy in head_copies:
+        copy.wait()
     for copy in copies[3:]:
         copy.wait()
 
@@ -122,37 +134,38 @@
     return [pltpu.with_memory_space_constraint(x, pltpu.VMEM) for x in arrays]
 
 
-def fetch(extra, lens, migrate, ids, gates, gain, own, wq, wkv, kv):
+def fetch(extra, lens, ids, gates, gain, own, wq, wkv, kv):
     rows = own.shape[0]
     wide = SPAN * (wkv.shape[1] // (2 * HEAD))
     per = kv.shape[1] // wide
-    outs = [(own.shape, bf16), (wq.shape, bf16), (wkv.shape, bf16), (gain.shape, f32)]
-    outs += [((rows, LANES), f32), ((rows, LANES), f32), ((rows, extra), bf16)]
-    scalars = [(rows,), (rows * per + UNROLL,), (1,), (1,)]
+    outs = [(own.shape, bf16), (gain.shape, f32)]
+    outs += [((rows, LANES), f32), ((rows, LANES), f32), ((rows, extra), bf16), (kv.shape, bf16)]
+    scalars = [(rows,), (rows * per + UNROLL,), (1,)]
     return pl.pallas_call(
         lambda *refs: fetch_kernel(wide, per, *refs),
         out_shape=tuple(pltpu.VMEM(shape, dtype) for shape, dtype in outs)
         + tuple(pltpu.SMEM(shape, jnp.int32) for shape in scalars),
-        in_specs=[hbm(), smem()] + [hbm()] * 6,
+        in_specs=[hbm()] * 6,
         out_specs=(vmem(),) * len(outs) + (smem(),) * len(scalars),
         scratch_shapes=[
             pltpu.SMEM(lens.shape, jnp.int32),
             pltpu.VMEM(ids.shape[::-1], jnp.int32),
             pltpu.VMEM(gates.shape[::-1], f32),
-            pltpu.SemaphoreType.DMA((5 + 2 * PIECES,)),
+            pltpu.SemaphoreType.DMA((5,)),
+            pltpu.SemaphoreType.DMA((rows,)),
         ],
         compiler_params=pltpu.CompilerParams(vmem_limit_bytes=8 * MIB),
         name="fetch",
-    )(*far(lens), migrate, *far(ids.T, gates.T, gain, own, wq, wkv))
+    )(*far(lens, ids.T, gates.T, gain, own, kv))
 
 
 def attention_kernel(n_parts, *refs):
     spans, items, count = refs[:3]
     refs = refs[3:]
     parts = refs[:n_parts]
-    (cos_ref, sin_ref, gain_ref, wq, wkv, wo_hbm, kv_hbm) = refs[n_parts : 7 + n_parts]
-    (tok_out, keep_out, send_out) = refs[7 + n_parts : 10 + n_parts]
-    (wo, kvbuf, qf, qb, kvn, mixes, sums, peaks, macc, lacc, oacc, ctx, wsem, ksem) = refs[10 + n_parts :]
+    (cos_ref, sin_ref, gain_ref, wq, wkv, _, wo_hbm, kv_hbm) = refs[n_parts : 8 + n_parts]
+    (tok_out, keep_out, send_out, kvbuf) = refs[8 + n_parts : 12 + n_parts]
+    (wo, qf, qb, kvn, mixes, sums, peaks, macc, lacc, oacc, ctx, wsem, ksem) = refs[12 + n_parts :]
     rows = tok_out.shape[0]
     n_query = wq.shape[1] // HEAD
     n_kv = wkv.shape[1] // (2 * HEAD)
@@ -161,16 +174,12 @@
     per = kv_hbm.shape[1] // wide
     tp = lax.axis_index("tp")
 
-    def kv_copy(r):
-        size = pl.multiple_of((spans[r] + SPAN - 1) // SPAN * wide, wide)
-        return pltpu.make_async_copy(
-            kv_hbm.at[r, pl.ds(0, size)], kvbuf.at[r, pl.ds(0, size)], ksem.at[r]
-        )
-
     total = count[0]
     blocks = (total + UNROLL - 1) // UNROLL
-    for r in range(rows // 2):
-        kv_copy(r).start()
+
+    for r in range(rows):
+        some, copy = rest_copy(kv_hbm, kvbuf, ksem, spans, wide, r)
+        pl.when(some)(copy.start)
     part = wo.shape[0] // PIECES
     wo_copies = [
         pltpu.make_async_copy(wo_hbm.at[pl.ds(i * part, part)], wo.at[pl.ds(i * part, part)], wsem.at[i])
@@ -212,8 +221,6 @@
         turned = turned * HEAD**-0.5
         qf[pl.ds(2 * k, rows, stride=QROWS), :] = jnp.where(low_half, turned, 0.0)
         qf[pl.ds(2 * k + 1, rows, stride=QROWS), :] = jnp.where(low_half, pltpu.roll(turned, HEAD, 1), 0.0)
-    for r in range(rows // 2, rows):
-        kv_copy(r).start()
     keyval = jnp.dot(normed, wkv[...], preferred_element_type=f32)
     for h in range(n_kv):
         v = keyval[:, h * LANES : (h + 1) * LANES]
@@ -241,11 +248,13 @@
         return r, c, kvbuf[kr, pl.ds(pl.multiple_of(c * wide, wide), wide), :]
 
     def arrive(r, carry):
-        kv_copy(r).wait()
+        some, copy = rest_copy(kv_hbm, kvbuf, ksem, spans, wide, r)
+        pl.when(some)(copy.wait)
         return carry
 
     def block(b, ready):
         last = jnp.minimum(items[b * UNROLL + UNROLL - 1] // per, rows - 1) + 1
+        last = jnp.where(b * UNROLL + UNROLL <= rows, 0, last)
         lax.fori_loop(ready, last, arrive, 0)
         got = [chunk(b * UNROLL + u) for u in range(UNROLL)]
         dots = [
@@ -266,9 +275,10 @@
             peaks[i] = tops[u]
         for (r, c, kv), top in zip(got, tops):
             macc[r] = jnp.maximum(macc[r], top)
-        return last
-
-    lax.fori_loop(0, blocks, block, 0)
+        return jnp.maximum(ready, last)
+
+    ready = lax.fori_loop(0, blocks, block, 0)
+    lax.fori_loop(ready, rows, arrive, 0)
 
     own = jnp.sum(qf[...] * kvn[...], axis=-1, keepdims=True)
     peak = jnp.maximum(macc[...].reshape(qf.shape), own)
@@ -299,7 +309,7 @@
     send_out[...] = partial.astype(bf16)
 
 
-def attention(plan, parts, cosine, sine, gain, wq, wkv, wo, kv):
+def attention(plan, parts, cosine, sine, gain, wq, wkv, kv_near, wo, kv):
     rows = parts[0].shape[0]
     width = wq.shape[0]
     n_kv = wkv.shape[1] // (2 * HEAD)
@@ -312,12 +322,13 @@
             pltpu.VMEM((rows, width), bf16),
             pltpu.VMEM((rows, width), f32),
             pltpu.VMEM((rows, width), bf16),
+            pltpu.VMEM(kv.shape, bf16),
         ),
-        in_specs=[smem()] * 3 + [vmem()] * (len(parts) + 5) + [hbm()] * 2,
-        out_specs=(vmem(), vmem(), vmem()),
+        in_specs=[smem()] * 3 + [vmem()] * (len(parts) + 6) + [hbm()] * 2,
+        out_specs=(vmem(), vmem(), vmem(), vmem()),
+        input_output_aliases={8 + len(parts): 3},
         scratch_shapes=[
             pltpu.VMEM(wo.shape, bf16),
-            pltpu.VMEM(kv.shape, bf16),
             pltpu.VMEM((many * QROWS, LANES), f32),
             pltpu.VMEM((many, QROWS, LANES), bf16),
             pltpu.VMEM((many * QROWS, LANES), f32),
@@ -331,12 +342,12 @@
             pltpu.SemaphoreType.DMA((PIECES,)),
             pltpu.SemaphoreType.DMA((rows,)),
         ],
-        compiler_params=pltpu.CompilerParams(vmem_limit_bytes=36 * MIB),
+        compiler_params=pltpu.CompilerParams(vmem_limit_bytes=16 * MIB),
         name="attention",
-    )(*close(*plan), *near(*parts, cosine, sine, gain, wq, wkv), *far(wo, kv))
-
-
-def expert_input_kernel(n_tp, tokens, keep, other, gain, table, payload, residual_out):
+    )(*close(*plan), *near(*parts, cosine, sine, gain, wq, wkv, kv_near), *far(wo, kv))
+
+
+def expert_input_kernel(n_tp, moved_slot, tokens, keep, other, gain, table, payload, residual_out):
     width = tokens.shape[1]
     tp = lax.axis_index("tp")
     residual = tokens[...].astype(f32) + keep[...] + other[...].astype(f32)
@@ -346,12 +357,58 @@
         mine = jnp.where(tp == t, residual[:, t * part : (t + 1) * part], mine)
     residual_out[...] = mine
     expert_in = normed_rows(residual, gain[...].reshape(1, -1))
+    lane = lax.broadcasted_iota(jnp.int32, table.shape, 1)
+    slot = lax.broadcasted_iota(jnp.int32, table.shape, 0)
+    n_experts = lax.axis_size("rep") * lax.axis_size("req")
+    moved = (lane == 2 * n_experts) & (slot == moved_slot[0])
+    marked = jnp.where(moved, 1.0, table[...].astype(f32)).astype(bf16)
     for q in range(payload.shape[0]):
         payload[q, :, :width] = expert_in
-        payload[q, :, width:] = table[...]
-
-
-def expert_input(n_tp, n_req, tokens, keep, other, gain, table):
+        payload[q, :, width:] = marked
+
+
+def stacked_kernel(*refs):
+    blocks, whole, tail = refs[:-2], refs[-2], refs[-1]
+    rows = blocks[0].shape[0]
+    for k, block in enumerate(blocks):
+        whole[k * rows : (k + 1) * rows] = block[...]
+        if k:
+            tail[(k - 1) * rows : k * rows] = block[...]
+
+
+def stacked(blocks):
+    rows, width = blocks[0].shape
+    return pl.pallas_call(
+        stacked_kernel,
+        out_shape=(
+            pltpu.VMEM((len(blocks) * rows, width), bf16),
+            pltpu.VMEM(((len(blocks) - 1) * rows, width), bf16),
+        ),
+        in_specs=[vmem()] * len(blocks),
+        out_specs=(vmem(), vmem()),
+        compiler_params=pltpu.CompilerParams(vmem_limit_bytes=8 * MIB),
+        name="stacked",
+    )(*near(*blocks))
+
+
+def joined_kernel(first, second, out):
+    rows = first.shape[0]
+    out[:rows] = first[...]
+    out[rows:] = second[...]
+
+
+def joined(first, second):
+    return pl.pallas_call(
+        joined_kernel,
+        out_shape=pltpu.VMEM((first.shape[0] + second.shape[0], first.shape[1]), bf16),
+        in_specs=[vmem()] * 2,
+        out_specs=vmem(),
+        compiler_params=pltpu.CompilerParams(vmem_limit_bytes=8 * MIB),
+        name="joined",
+    )(*near(first, second))
+
+
+def expert_input(n_tp, n_req, moved, tokens, keep, other, gain, table):
     rows, width = tokens.shape
     return pl.pallas_call(
         lambda *refs: expert_input_kernel(n_tp, *refs),
@@ -359,11 +416,11 @@
             pltpu.VMEM((n_req, rows, width + table.shape[1]), bf16),
             pltpu.VMEM((rows, width // n_tp), f32),
         ),
-        in_specs=[vmem()] * 5,
+        in_specs=[smem()] + [vmem()] * 5,
         out_specs=(vmem(), vmem()),
         compiler_params=pltpu.CompilerParams(vmem_limit_bytes=8 * MIB),
         name="expert_input",
-    )(*near(tokens, keep, other), gain, *near(table))
+    )(moved, *near(tokens, keep, other), gain, *near(table))
 
 
 def expert_rows(rows, gate_up, down):
@@ -382,20 +439,27 @@
 def own_expert(x, gate_up, down):
     return pl.pallas_call(
         own_expert_kernel,
-        out_shape=jax.ShapeDtypeStruct((x.shape[0], down.shape[1]), f32),
+        out_shape=pltpu.VMEM((x.shape[0], down.shape[1]), f32),
         in_specs=[vmem()] * 3,
         out_specs=vmem(),
         compiler_params=pltpu.CompilerParams(vmem_limit_bytes=32 * MIB),
+        cost_estimate=expert_cost(x.shape[0], gate_up, down),
         name="own_expert",
-    )(x, gate_up, down)
-
-
-def other_expert_kernel(x_own, x_other, y_own, gate_up, down, keep, send):
-    width = down.shape[1]
+    )(*near(x), gate_up, down)
+
+
+def expert_cost(count, gate_up, down):
+    return pl.CostEstimate(
+        flops=2 * count * (gate_up.size + down.size),
+        bytes_accessed=2 * (gate_up.size + down.size) + 10 * count * down.shape[1],
+        transcendentals=count * down.shape[0],
+    )
+
+
+def traded(width, x_own, x_other, from_own, from_other, keep, send):
     n_req = lax.axis_size("req")
     n_experts = lax.axis_size("rep") * n_req
     expert = lax.axis_index("rep") * n_req + lax.axis_index("req")
-    y_other = expert_rows(x_other[:, :width], gate_up[...], down[...])
     own_table = x_own[:, width:].astype(f32)
     other_table = x_other[:, width:].astype(f32)
     lane = lax.broadcasted_iota(jnp.int32, own_table.shape, 1)
@@ -403,67 +467,173 @@
     def picked(table, mask):
         return jnp.sum(jnp.where(mask, table, 0.0), axis=-1, keepdims=True)
 
-    mine = (lane == expert) | (lane == expert + n_experts)
-    own_gate, other_gate = picked(own_table, mine), picked(other_table, mine)
+    gated = (lane == expert) | (lane == expert + n_experts)
+    own_gate, other_gate = picked(own_table, gated), picked(other_table, gated)
     moved = picked(own_table, lane == 2 * n_experts) > 0.5
-    from_own = y_own[...] * jnp.where(moved, other_gate, own_gate)
-    from_other = y_other * jnp.where(moved, own_gate, other_gate)
+    from_own = from_own(jnp.where(moved, other_gate, own_gate))
+    from_other = from_other() * jnp.where(moved, own_gate, other_gate)
     keep[...] = jnp.where(moved, from_other, from_own)
     send[...] = jnp.where(moved, from_own, from_other).astype(bf16)
 
 
-def other_expert(x_own, x_other, y_own, gate_up, down):
-    return pl.pallas_call(
-        other_expert_kernel,
-        out_shape=(
-            jax.ShapeDtypeStruct(y_own.shape, f32),
-            jax.ShapeDtypeStruct(y_own.shape, bf16),
-        ),
+def home_expert_kernel(n_tp, place, x_own, x_other, residual, gate_up, down, keep, send, mine):
+    width = down.shape[1]
+    count = x_own.shape[0]
+    both = jnp.concatenate([x_own[:, :width], x_other[:, :width]], axis=0)
+    y = expert_rows(both, gate_up[...], down[...])
+    rows, part = residual.shape
+    tp = lax.axis_index("tp")
+    here = pl.ds(place() * rows, rows)
+
+    def from_own(gate):
+        mine[...] = y[:count] * gate
+        for t in range(n_tp):
+
+            @pl.when(tp == t)
+            def _():
+                mine[here, t * part : (t + 1) * part] += residual[...]
+
+        return mine[...]
+
+    traded(width, x_own, x_other, from_own, lambda: y[count:], keep, send)
+
+
+def home_expert(n_tp, place, x_own, x_other, residual, gate_up, down):
+    shape = (x_own.shape[0], down.shape[1])
+    return pl.pallas_call(
+        lambda *refs: home_expert_kernel(n_tp, place, *refs),
+        out_shape=(pltpu.VMEM(shape, f32), pltpu.VMEM(shape, bf16)),
         in_specs=[vmem()] * 5,
         out_specs=(vmem(), vmem()),
-        compiler_params=pltpu.CompilerParams(vmem_limit_bytes=40 * MIB),
+        scratch_shapes=[pltpu.VMEM(shape, f32)],
+        compiler_params=pltpu.CompilerParams(vmem_limit_bytes=40 * MIB if shape[0] > 256 else 16 * MIB),
+        cost_estimate=expert_cost(2 * shape[0], gate_up, down),
+        name="home_expert",
+    )(*near(x_own, x_other, residual), gate_up, down)
+
+
+def other_expert_kernel(x_own, x_other, y_own, gate_up, down, keep, send):
+    width = down.shape[1]
+
+    def from_other():
+        return expert_rows(x_other[:, :width], gate_up[...], down[...])
+
+    traded(width, x_own, x_other, lambda gate: y_own[...] * gate, from_other, keep, send)
+
+
+def other_expert(x_own, x_other, y_own, gate_up, down):
+    return pl.pallas_call(
+        other_expert_kernel,
+        out_shape=(pltpu.VMEM(y_own.shape, f32), pltpu.VMEM(y_own.shape, bf16)),
+        in_specs=[vmem()] * 5,
+        out_specs=(vmem(), vmem()),
+        compiler_params=pltpu.CompilerParams(vmem_limit_bytes=16 * MIB),
+        cost_estimate=expert_cost(y_own.shape[0], gate_up, down),
         name="other_expert",
-    )(x_own, x_other, y_own, gate_up, down)
-
-
-def pair_sum_kernel(n_tp, keep, recv, out):
-    n_req, _, rows, part = out.shape
-    total = (keep[...] + recv[...].astype(f32)).astype(bf16)
-    for q in range(n_req):
-        for t in range(n_tp):
-            out[q, t] = total[q * rows : (q + 1) * rows, t * part : (t + 1) * part]
-
-
-def pair_sum(n_tp, n_req, keep, recv):
-    rows, part = keep.shape[0] // n_req, keep.shape[1] // n_tp
-    return pl.pallas_call(
-        lambda *refs: pair_sum_kernel(n_tp, *refs),
-        out_shape=jax.ShapeDtypeStruct((n_req, n_tp, rows, part), bf16),
+    )(*near(x_own, x_other, y_own), gate_up, down)
+
+
+def pair_sum_kernel(n_tp, spots, *refs):
+    out = refs[-1]
+    _, _, rows, part = out.shape
+    for i, spot in enumerate(spots):
+        keep, recv = refs[2 * i], refs[2 * i + 1]
+        total = (keep[...] + recv[...].astype(f32)).astype(bf16)
+        for q in range(total.shape[0] // rows):
+            for t in range(n_tp):
+                out[spot(q), t] = total[q * rows : (q + 1) * rows, t * part : (t + 1) * part]
+
+
+def pair_sum(n_tp, n_req, rows, spots, *sums):
+    part = sums[0].shape[1] // n_tp
+    return pl.pallas_call(
+        lambda *refs: pair_sum_kernel(n_tp, spots, *refs),
+        out_shape=pltpu.VMEM((n_req, n_tp, rows, part), bf16),
+        in_specs=[vmem()] * len(sums),
+        out_specs=vmem(),
+        compiler_params=pltpu.CompilerParams(vmem_limit_bytes=16 * MIB),
+        name="pair_sum",
+    )(*near(*sums))
+
+
+def halves_kernel(keep, recv, mine, cross):
+    total = keep[...] + recv[...].astype(f32)
+    part = mine.shape[1]
+    low, high = total[:, :part], total[:, part:]
+    first = lax.axis_index("tp") == 0
+    mine[...] = jnp.where(first, low, high).astype(mine.dtype)
+    cross[...] = jnp.where(first, high, low).astype(bf16)
+
+
+def halves(keep, recv, kind):
+    shape = (keep.shape[0], keep.shape[1] // 2)
+    return pl.pallas_call(
+        halves_kernel,
+        out_shape=(pltpu.VMEM(shape, kind), pltpu.VMEM(shape, bf16)),
         in_specs=[vmem()] * 2,
+        out_specs=(vmem(), vmem()),
+        compiler_params=pltpu.CompilerParams(vmem_limit_bytes=8 * MIB),
+        name="halves",
+    )(*near(keep, recv))
+
+
+def square_sum_kernel(mine, *refs):
+    arrived, outs = refs[:3], refs[3:]
+    total = mine[...]
+    for piece in arrived:
+        total = total + piece[...].astype(f32)
+    rows = outs[0].shape[0]
+    for k, out in enumerate(outs):
+        out[...] = total[k * rows : (k + 1) * rows].astype(out.dtype)
+
+
+def square_sum(rows, mine, *arrived):
+    shape = (rows, mine.shape[1])
+    count = mine.shape[0] // rows
+    return pl.pallas_call(
+        square_sum_kernel,
+        out_shape=(pltpu.VMEM(shape, f32),) + (pltpu.VMEM(shape, bf16),) * (count - 1),
+        in_specs=[vmem()] * 4,
+        out_specs=(vmem(),) * count,
+        compiler_params=pltpu.CompilerParams(vmem_limit_bytes=8 * MIB),
+        name="square_sum",
+    )(*near(mine, *arrived))
+
+
+def line_sum_kernel(*refs):
+    total = refs[0][...]
+    for piece in refs[1:-1]:
+        total = total + piece[...].astype(f32)
+    refs[-1][...] = total.astype(bf16)
+
+
+def line_sum(mine, *arrived):
+    return pl.pallas_call(
+        line_sum_kernel,
+        out_shape=jax.ShapeDtypeStruct(mine.shape, bf16),
+        in_specs=[vmem()] * (1 + len(arrived)),
         out_specs=vmem(),
-        compiler_params=pltpu.CompilerParams(vmem_limit_bytes=32 * MIB),
-        name="pair_sum",
-    )(keep, recv)
-
-
-def final_kernel(moved_slot, pieces, own_residual, other_residual, out):
+        compiler_params=pltpu.CompilerParams(vmem_limit_bytes=8 * MIB),
+        name="line_sum",
+    )(*near(mine, *arrived))
+
+
+def final_kernel(pieces, out):
     total = pieces[0].astype(f32)
     for i in range(1, pieces.shape[0]):
         total = total + pieces[i].astype(f32)
-    slot = lax.broadcasted_iota(jnp.int32, total.shape, 0)
-    residual = jnp.where(slot == moved_slot[0], other_residual[...], own_residual[...])
-    out[...] = (residual + total).astype(bf16)
-
-
-def final(moved, pieces, own_residual, other_residual):
+    out[...] = total.astype(bf16)
+
+
+def final(pieces):
     return pl.pallas_call(
         final_kernel,
-        out_shape=jax.ShapeDtypeStruct(own_residual.shape, bf16),
-        in_specs=[smem()] + [vmem()] * 3,
+        out_shape=jax.ShapeDtypeStruct(pieces.shape[1:], bf16),
+        in_specs=[vmem()],
         out_specs=vmem(),
         compiler_params=pltpu.CompilerParams(vmem_limit_bytes=8 * MIB),
         name="final",
-    )(*close(moved), pieces, own_residual, other_residual)
+    )(*near(pieces))
 
 
 def shards(
@@ -490,10 +660,9 @@
     else:
         all_parts = lax.all_gather(hidden, "tp", axis=1, tiled=True)
     kv = kv_cache.reshape(rows, -1, LANES)
-    own, wq, wkv, gain, cosine, sine, table, *plan, moved = fetch(
+    own, gain, cosine, sine, table, kv_near, *plan = fetch(
         extra,
         lengths,
-        migrate,
         expert_ids,
         expert_gates,
         attn_gain,
@@ -503,25 +672,54 @@
         kv,
     )
     parts = [own, other_part] if n_tp == 2 else [all_parts]
-    tokens, keep, send = attention(plan, parts, cosine, sine, gain, wq, wkv, output_weight, kv)
+    tokens, keep, send, _ = attention(
+        plan, parts, cosine, sine, gain, w_query, key_value_weight, kv_near, output_weight, kv
+    )
+    gate_up = w_gateup[0].reshape(w_gateup.shape[1], -1)
+    down = w_down[0]
     if n_tp == 2:
         other = swapped(send, "tp")
+        gate_up, other = lax.optimization_barrier((gate_up, other))
     else:
         other = lax.psum(keep.astype(bf16), "tp").astype(f32) - keep
-    payload, residual = expert_input(n_tp, n_req, tokens, keep, other, moe_gain, table)
-    other_residual = swapped(residual, "rep")
+    by_permute = n_req == 8 and n_tp == 2
+    payload, residual = expert_input(n_tp, 1 if by_permute else n_req, migrate, tokens, keep, other, moe_gain, table)
+    if by_permute:
+        payload = payload[0]
+        steps = [[(q, q ^ 2 * k) for q in range(n_req)] for k in (1, 2, 3)]
+        beside = [lax.ppermute(payload, "req", step) for step in steps]
+        across = swapped(payload, "req")
+        home, tail = stacked([payload] + beside)
+        away = joined(across, swapped(tail, "req"))
+        home_other = swapped(home, "rep")
+        home_keep, home_send = home_expert(
+            n_tp, lambda: 0, home, home_other, residual, gate_up, down
+        )
+        home_recv = swapped(home_send, "rep")
+        away_other = swapped(away, "rep")
+        away_own = own_expert(away, gate_up, down)
+        away_keep, away_send = other_expert(away, away_other, away_own, gate_up, down)
+        away_recv = swapped(away_send, "rep")
+        home_mine, home_cross = halves(home_keep, home_recv, f32)
+        from_x = swapped(home_cross, "tp")
+        away_mine, away_cross = halves(away_keep, away_recv, bf16)
+        from_y = swapped(away_mine, "req")
+        corner = [(i, i ^ 3) for i in range(n_req * n_tp)]
+        from_corner = lax.ppermute(away_cross, ("req", "tp"), corner)
+        mine, *others = square_sum(rows, home_mine, from_x, from_y, from_corner)
+        line = [lax.ppermute(other, "req", step) for other, step in zip(others, steps)]
+        return line_sum(mine, *line)
     x_own = lax.all_to_all(payload, "req", split_axis=0, concat_axis=0, tiled=True)
     x_own = x_own.reshape(n_req * rows, -1)
     x_other = swapped(x_own, "rep")
-    gate_up = w_gateup[0].reshape(w_gateup.shape[1], -1)
-    down = w_down[0]
-    y_own = own_expert(x_own, gate_up, down)
-    mix_keep, mix_send = other_expert(x_own, x_other, y_own, gate_up, down)
+    mix_keep, mix_send = home_expert(
+        n_tp, lambda: lax.axis_index("req"), x_own, x_other, residual, gate_up, down
+    )
     mix_recv = swapped(mix_send, "rep")
-    pieces = pair_sum(n_tp, n_req, mix_keep, mix_recv)
+    pieces = pair_sum(n_tp, n_req, rows, (lambda q: q,), mix_keep, mix_recv)
     pieces = pieces.reshape(n_req * n_tp, rows, -1)
     pieces = lax.all_to_all(pieces, ("req", "tp"), split_axis=0, concat_axis=0, tiled=True)
-    return final(moved, pieces, residual, other_residual)
+    return final(pieces)
 
 
 def solution(mesh):

time: 58.4 us -> 53.2 us (0.911)
  blocking collectives: 18.1 us -> 0 us
  starting transfers between devices: 8.05 us -> 20.2 us
  local copies, waits for them, and re-layouts: 0.35 us -> 1.23 us
    all_to_all x1 -> x0, blocking collectives: 18.1 us -> none  [shards(): lax.all_to_all(payload, 'req', split_axis=0, concat_axis=0, tiled=True)]
    all_to_all x1 -> x0, waiting for transfers between devices: 11.8 us -> none  [shards(): lax.all_to_all(pieces, ('req', 'tp'), split_axis=0, concat_axis=0, tiled=...]
    ppermute x0 -> x7, starting transfers between devices: none -> 9.57 us  [the longest x3 4.44 us: shards(): beside = [lax.ppermute(payload, 'req', step) for step in steps]]
    ppermute x0 -> x7, waiting for transfers between devices: none -> 8.16 us  [the longest x3 4.67 us: shards(): beside = [lax.ppermute(payload, 'req', step) for step in steps]]
    ppermute x5 -> x10, starting transfers between devices: 4.5 us -> 10.6 us  [swapped(): lax.ppermute(value, axis, [(i, i ^ 1) for i in range(lax.axis_size(axis))])]
    ppermute x5 -> x10, waiting for transfers between devices: 6.5 us -> 10.1 us  [swapped(): lax.ppermute(value, axis, [(i, i ^ 1) for i in range(lax.axis_size(axis))])]
    all_to_all x1 -> x0, starting transfers between devices: 3.55 us -> none  [shards(): lax.all_to_all(pieces, ('req', 'tp'), split_axis=0, concat_axis=0, tiled=...]
    unnamed x7 -> x11, local copies, waits for them, and re-layouts: 0.35 us -> 1.23 us
  transfers between devices with their start and end apart: 6 -> 17, of which waited for: 5 -> 11; matrix products, arithmetic and copies ran while one was open for 1% -> 1% of each run, Pallas kernels for 5% -> 8%
where the time goes in v3:
time: 53.2 us; the launch traced here: 53.1 us
  starting transfers between devices  20.2 us (38%)
  waiting for transfers between devices  18.2 us (34%)
  Pallas kernels  12.7 us (24%)
  local copies, waits for them, and re-layouts  1.23 us (2%)
  between operations  0.78 us (1%)
    ppermute x10, starting transfers between devices, swapped(): lax.ppermute(value, axis, [(i, i ^ 1) for i in range(lax.axis_size(axis))])  10.6 us
    ppermute x10, waiting for transfers between devices, swapped(): lax.ppermute(value, axis, [(i, i ^ 1) for i in range(lax.axis_size(axis))])  10.1 us
    pallas_call x1, Pallas kernels, attention(): pl.pallas_call(lambda *refs: attention_kernel(len(parts), *refs), out_sha...  7.9 us
    ppermute x3, waiting for transfers between devices, shards(): beside = [lax.ppermute(payload, 'req', step) for step in steps]  4.67 us
    ppermute x3, starting transfers between devices, shards(): beside = [lax.ppermute(payload, 'req', step) for step in steps]  4.44 us
    ppermute x3, starting transfers between devices, shards(): lax.ppermute(other, 'req', step)  4.44 us
    ppermute x3, waiting for transfers between devices, shards(): lax.ppermute(other, 'req', step)  2.38 us
    pallas_call x1, Pallas kernels, fetch(): pl.pallas_call(lambda *refs: fetch_kernel(wide, per, *refs), out_shape=tu...  1.95 us
  transfers between devices with their start and end apart: 17, of which 11 were waited for; matrix products, arithmetic and copies ran while one was open for 1% of the time, Pallas kernels for 8%

profile of v3, /device:TPU:0, one launch (start us, length us, event | category | flops | bytes accessed | tf_op | source)
XLA Modules:
  0.0 53.1 jit_solution(10921769420750635239)
XLA Ops:
  0.0 2.9 %collective-permute-start = (bf16[16,768]{1,0:T(8,128)(2,1)}, bf16[16,768]{1,0:T(8,128)(2,1)S(1)}, u32[]{:S(2)}, u32[]{:S(2)}) collective-permute-start(bf16[16,768]{1,0:T(8,128)(2,1)} %refs_4_.2), channel_id=1, source_target_pairs={{0,1},{1,0},{2,3},{3,2},{4,5},{5,4},{6,7},{7,6},{8,9},{9,8},{10,11... | collective-permute-start | bytes 73736 | tf_op jit(solution)/shard_map/ppermute | solution.py:36
  2.9 1.9 %fetch.1 = (bf16[16,768]{1,0:T(8,128)(2,1)S(1)}, f32[1536]{0:T(1024)S(1)}, f32[16,128]{1,0:T(8,128)S(1)}, f32[16,128]{1,0:T(8,128)S(1)}, bf16[16,128]{1,0:T(8,12...) custom-call(s32[2,16]{1,0:T(2,128)} %refs_0_.2, ...), custom_call_target="tpu_custom_call" | custom-call | tf_op jit(solution)/shard_map/fetch/pallas_call | solution.py:144
  5.0 0.4 copy-done.1
  5.3 0.5 copy-done.2
  5.8 7.9 %attention.1 = (bf16[16,1536]{1,0:T(8,128)(2,1)S(1)}, f32[16,1536]{1,0:T(8,128)S(1)}, bf16[16,1536]{1,0:T(8,128)(2,1)S(1)}, bf16[16,4096,128]{2,1,0:T(8,128)(2,1)S(1)}) custom-call(s32[16]{0:T(128)S(4)} %get-tuple-element.35.refs_0_, s32[144]{0:T(256)S(4)} %get-tuple-element.36.refs_1_, ...), custom_call_target="tpu_custom_call", output_to_operand_aliasing={{3}: (10, {})} | custom-call | tf_op jit(solution)/shard_map/attention/pallas_call | solution.py:319
  13.7 1.3 %collective-permute-start.1 = (bf16[16,1536]{1,0:T(8,128)(2,1)S(1)}, bf16[16,1536]{1,0:T(8,128)(2,1)S(1)}, u32[]{:S(2)}, u32[]{:S(2)}) collective-permute-start(bf16[16,1536]{1,0:T(8,128)(2,1)S(1)} %get-tuple-element.45), channel_id=1, source_target_pairs={{0,1},{1,0},{2,3},{3,2},{4,5},{5,4},{6,7},{7,6},{8,9},{9,8},{10,11... | collective-permute-start | bytes 147464 | tf_op jit(solution)/shard_map/ppermute | solution.py:36
  15.0 0.4 copy.15
  16.0 1.9 %collective-permute-done.1.refs_3_ = bf16[16,1536]{1,0:T(8,128)(2,1)S(1)} collective-permute-done((bf16[16,1536]{1,0:T(8,128)(2,1)S(1)}, bf16[16,1536]{1,0:T(8,128)(2,1)S(1)}, u32[]{:S(2)}, u32[]{:S(2)}) %collective-permute-start.1) | collective-permute-done | bytes 49184 | tf_op jit(solution)/shard_map/ppermute | solution.py:36
  17.9 0.1 expert_input.1
  18.1 3.1 %collective-permute-start.3 = (bf16[16,1664]{1,0:T(8,128)(2,1)S(1)}, bf16[16,1664]{1,0:T(8,128)(2,1)S(1)}, u32[]{:S(2)}, u32[]{:S(2)}) collective-permute-start(bf16[16,1664]{1,0:T(8,128)(2,1)S(1)} %bitcast.15), channel_id=1, source_target_pairs={{0,8},{2,10},{4,12},{6,14},{8,0},{10,2},{12,4},{14,6},{1,9},{3,11}... | collective-permute-start | bytes 159752 | tf_op jit(solution)/shard_map/ppermute | solution.py:690
  21.2 1.3 %collective-permute-start.4 = (bf16[16,1664]{1,0:T(8,128)(2,1)S(1)}, bf16[16,1664]{1,0:T(8,128)(2,1)S(1)}, u32[]{:S(2)}, u32[]{:S(2)}) collective-permute-start(bf16[16,1664]{1,0:T(8,128)(2,1)S(1)} %bitcast.16), channel_id=1, source_target_pairs={{0,12},{2,14},{4,8},{6,10},{8,4},{10,6},{12,0},{14,2},{1,13},{3,15... | collective-permute-start | bytes 159752 | tf_op jit(solution)/shard_map/ppermute | solution.py:690
  22.5 1.2 %collective-permute-done.3.refs_2_ = bf16[16,1664]{1,0:T(8,128)(2,1)S(1)} collective-permute-done((bf16[16,1664]{1,0:T(8,128)(2,1)S(1)}, bf16[16,1664]{1,0:T(8,128)(2,1)S(1)}, u32[]{:S(2)}, u32[]{:S(2)}) %collective-permute-start.3) | collective-permute-done | bytes 53280 | tf_op jit(solution)/shard_map/ppermute | solution.py:690
  23.7 3.5 %collective-permute-done.4.refs_3_ = bf16[16,1664]{1,0:T(8,128)(2,1)S(1)} collective-permute-done((bf16[16,1664]{1,0:T(8,128)(2,1)S(1)}, bf16[16,1664]{1,0:T(8,128)(2,1)S(1)}, u32[]{:S(2)}, u32[]{:S(2)}) %collective-permute-start.4) | collective-permute-done | bytes 53280 | tf_op jit(solution)/shard_map/ppermute | solution.py:690
  27.2 2.6 %collective-permute-start.9 = (bf16[48,1664]{1,0:T(8,128)(2,1)S(1)}, bf16[48,1664]{1,0:T(8,128)(2,1)S(1)}, u32[]{:S(2)}, u32[]{:S(2)}) collective-permute-start(bf16[48,1664]{1,0:T(8,128)(2,1)S(1)} %get-tuple-element.56), channel_id=1, source_target_pairs={{0,2},{2,0},{4,6},{6,4},{8,10},{10,8},{12,14},{14,12},{1,3},{3,1},... | collective-permute-start | bytes 479240 | tf_op jit(solution)/shard_map/ppermute | solution.py:36
  29.8 4.1 %collective-permute-done.8.first = bf16[16,1664]{1,0:T(8,128)(2,1)S(1)} collective-permute-done((bf16[16,1664]{1,0:T(8,128)(2,1)S(1)}, bf16[16,1664]{1,0:T(8,128)(2,1)S(1)}, u32[]{:S(2)}, u32[]{:S(2)}) %collective-permute-start.8) | collective-permute-done | bytes 53280 | tf_op jit(solution)/shard_map/ppermute | solution.py:36
  34.0 0.6 %own_expert.1.y_own = f32[64,1536]{1,0:T(8,128)S(1)} custom-call(bf16[64,1664]{1,0:T(8,128)(2,1)S(1)} %joined.1.x.x_own, bf16[1536,512]{1,0:T(8,128)(2,1)S(1)} %bitcast.8, bf16[256,1536]{1,0:T(8,128)(2,1)S(1)} %bitcast.11), custom_call_target="tpu_custom_call" | custom-call | flops 150994944 | bytes 3342336 | tf_op jit(solution)/shard_map/own_expert/pallas_call | solution.py:440
  34.6 0.7 %home_expert.1 = (f32[64,1536]{1,0:T(8,128)S(1)}, bf16[64,1536]{1,0:T(8,128)(2,1)S(1)}) custom-call(bf16[64,1664]{1,0:T(8,128)(2,1)S(1)} %get-tuple-element.49.refs_0_, bf16[64,1664]{1,0:T(8,128)(2,1)S(1)} %collective-permute-done.5.refs_1_, f32[16,768]{1,0:T(8,128)S(1)} %get-tuple-element.50.refs_2_, bf16[1536,512]{1,0:T(8,128)(2,1)S(1)} %bitcast.9, ...), custom_call_target="tpu_custom_call" | custom-call | flops 301989888 | bytes 4325376 | tf_op jit(solution)/shard_map/home_expert/pallas_call | solution.py:503
  35.3 0.6 %collective-permute-start.6 = (bf16[64,1536]{1,0:T(8,128)(2,1)S(1)}, bf16[64,1536]{1,0:T(8,128)(2,1)S(1)}, u32[]{:S(2)}, u32[]{:S(2)}) collective-permute-start(bf16[64,1536]{1,0:T(8,128)(2,1)S(1)} %get-tuple-element.53), channel_id=1, source_target_pairs={{0,16},{16,0},{1,17},{17,1},{2,18},{18,2},{3,19},{19,3},{4,20},{20... | collective-permute-start | bytes 589832 | tf_op jit(solution)/shard_map/ppermute | solution.py:36
  35.9 0.6 %other_expert.1 = (f32[64,1536]{1,0:T(8,128)S(1)}, bf16[64,1536]{1,0:T(8,128)(2,1)S(1)}) custom-call(bf16[64,1664]{1,0:T(8,128)(2,1)S(1)} %joined.1.x.x_own, bf16[64,1664]{1,0:T(8,128)(2,1)S(1)} %collective-permute-done.10.x_other, f32[64,1536]{1,0:T(8,128)S(1)} %own_expert.1.y_own, bf16[1536,512]{1,0:T(8,128)(2,1)S(1)} %bitcast.10, ...), custom_call_target="tpu_custom_call" | custom-call | flops 150994944 | bytes 3342336 | tf_op jit(solution)/shard_map/other_expert/pallas_call | solution.py:525
  36.5 0.1 collective-permute-start.11
  36.6 0.4 collective-permute-done.6.recv
  37.0 1.3 %collective-permute-start.7 = (bf16[64,768]{1,0:T(8,128)(2,1)S(1)}, bf16[64,768]{1,0:T(8,128)(2,1)S(1)}, u32[]{:S(2)}, u32[]{:S(2)}) collective-permute-start(bf16[64,768]{1,0:T(8,128)(2,1)S(1)} %get-tuple-element.55), channel_id=1, source_target_pairs={{0,1},{1,0},{2,3},{3,2},{4,5},{5,4},{6,7},{7,6},{8,9},{9,8},{10,11... | collective-permute-start | bytes 294920 | tf_op jit(solution)/shard_map/ppermute | solution.py:36
  38.3 1.8 %collective-permute-start.12 = (bf16[64,768]{1,0:T(8,128)(2,1)S(1)}, bf16[64,768]{1,0:T(8,128)(2,1)S(1)}, u32[]{:S(2)}, u32[]{:S(2)}) collective-permute-start(bf16[64,768]{1,0:T(8,128)(2,1)S(1)} %get-tuple-element.59), channel_id=1, source_target_pairs={{0,2},{2,0},{4,6},{6,4},{8,10},{10,8},{12,14},{14,12},{1,3},{3,1},... | collective-permute-start | bytes 294920 | tf_op jit(solution)/shard_map/ppermute | solution.py:36
  40.1 0.7 %collective-permute-start.13 = (bf16[64,768]{1,0:T(8,128)(2,1)S(1)}, bf16[64,768]{1,0:T(8,128)(2,1)S(1)}, u32[]{:S(2)}, u32[]{:S(2)}) collective-permute-start(bf16[64,768]{1,0:T(8,128)(2,1)S(1)} %get-tuple-element.60), channel_id=1, source_target_pairs={{0,3},{1,2},{2,1},{3,0},{4,7},{5,6},{6,5},{7,4},{8,11},{9,10},{10,... | collective-permute-start | bytes 294920 | tf_op jit(solution)/shard_map/ppermute | solution.py:708
  40.8 1.4 %collective-permute-done.7.refs_0_ = bf16[64,768]{1,0:T(8,128)(2,1)S(1)} collective-permute-done((bf16[64,768]{1,0:T(8,128)(2,1)S(1)}, bf16[64,768]{1,0:T(8,128)(2,1)S(1)}, u32[]{:S(2)}, u32[]{:S(2)}) %collective-permute-start.7) | collective-permute-done | bytes 98336 | tf_op jit(solution)/shard_map/ppermute | solution.py:36
  42.1 2.4 %collective-permute-done.12.refs_1_ = bf16[64,768]{1,0:T(8,128)(2,1)S(1)} collective-permute-done((bf16[64,768]{1,0:T(8,128)(2,1)S(1)}, bf16[64,768]{1,0:T(8,128)(2,1)S(1)}, u32[]{:S(2)}, u32[]{:S(2)}) %collective-permute-start.12) | collective-permute-done | bytes 98336 | tf_op jit(solution)/shard_map/ppermute | solution.py:36
  44.5 1.1 %collective-permute-done.13.refs_2_ = bf16[64,768]{1,0:T(8,128)(2,1)S(1)} collective-permute-done((bf16[64,768]{1,0:T(8,128)(2,1)S(1)}, bf16[64,768]{1,0:T(8,128)(2,1)S(1)}, u32[]{:S(2)}, u32[]{:S(2)}) %collective-permute-start.13) | collective-permute-done | bytes 98336 | tf_op jit(solution)/shard_map/ppermute | solution.py:708
  45.7 1.1 %collective-permute-start.15 = (bf16[16,768]{1,0:T(8,128)(2,1)S(1)}, bf16[16,768]{1,0:T(8,128)(2,1)S(1)}, u32[]{:S(2)}, u32[]{:S(2)}) collective-permute-start(bf16[16,768]{1,0:T(8,128)(2,1)S(1)} %get-tuple-element.63), channel_id=1, source_target_pairs={{0,8},{2,10},{4,12},{6,14},{8,0},{10,2},{12,4},{14,6},{1,9},{3,11}... | collective-permute-start | bytes 73736 | tf_op jit(solution)/shard_map/ppermute | solution.py:710
  46.8 3.2 %collective-permute-start.16 = (bf16[16,768]{1,0:T(8,128)(2,1)S(1)}, bf16[16,768]{1,0:T(8,128)(2,1)S(1)}, u32[]{:S(2)}, u32[]{:S(2)}) collective-permute-start(bf16[16,768]{1,0:T(8,128)(2,1)S(1)} %get-tuple-element.64), channel_id=1, source_target_pairs={{0,12},{2,14},{4,8},{6,10},{8,4},{10,6},{12,0},{14,2},{1,13},{3,15... | collective-permute-start | bytes 73736 | tf_op jit(solution)/shard_map/ppermute | solution.py:710
  50.1 0.4 collective-permute-done.15.refs_2_
  50.5 2.0 %collective-permute-done.16.refs_3_ = bf16[16,768]{1,0:T(8,128)(2,1)S(1)} collective-permute-done((bf16[16,768]{1,0:T(8,128)(2,1)S(1)}, bf16[16,768]{1,0:T(8,128)(2,1)S(1)}, u32[]{:S(2)}, u32[]{:S(2)}) %collective-permute-start.16) | collective-permute-done | bytes 24608 | tf_op jit(solution)/shard_map/ppermute | solution.py:710
  52.5 0.6 %line_sum.1 = bf16[16,768]{1,0:T(8,128)(2,1)} custom-call(f32[16,768]{1,0:T(8,128)S(1)} %get-tuple-element.61.refs_0_, bf16[16,768]{1,0:T(8,128)(2,1)S(1)} %collective-permute-done.14.refs_1_, bf16[16,768]{1,0:T(8,128)(2,1)S(1)} %collective-permute-done.15.refs_2_, bf16[16,768]{1,0:T(8,128)(2,1)S(1)} %collective-permute-done.16.refs_3_), custom_call_target="tpu_custom_call" | custom-call | tf_op jit(solution)/shard_map/line_sum/pallas_call | solution.py:611
  (25 shorter events, 0.6 us)
Async XLA Ops:
  0.0 5.0 %collective-permute-start = (bf16[16,768]{1,0:T(8,128)(2,1)}, bf16[16,768]{1,0:T(8,128)(2,1)S(1)}, u32[]{:S(2)}, u32[]{:S(2)}) collective-permute-start(bf16[16,768]{1,0:T(8,128)(2,1)} %refs_4_.2), channel_id=1, source_target_pairs={{0,1},{1,0},{2,3},{3,2},{4,5},{5,4},{6,7},{7,6},{8,9},{9,8},{10,11... | collective-permute-start | bytes 73736 | tf_op jit(solution)/shard_map/ppermute | solution.py:36
  2.9 2.4 %copy-start.1 = (bf16[1536,768]{1,0:T(8,128)(2,1)S(1)}, bf16[1536,768]{1,0:T(8,128)(2,1)}, u32[]{:S(2)}) copy-start(bf16[1536,768]{1,0:T(8,128)(2,1)} %refs_8_.1) | copy-start | bytes 7077892
  2.9 2.9 %copy-start.2 = (bf16[1536,512]{1,0:T(8,128)(2,1)S(1)}, bf16[1536,512]{1,0:T(8,128)(2,1)}, u32[]{:S(2)}) copy-start(bf16[1536,512]{1,0:T(8,128)(2,1)} %refs_9_.1) | copy-start | bytes 4718596
  5.8 9.2 %copy-start.4 = (bf16[1,1536,2,256]{3,2,1,0:T(2,128)(2,1)S(1)}, bf16[1,1536,2,256]{3,2,1,0:T(2,128)(2,1)}, u32[]{:S(2)}) copy-start(bf16[1,1536,2,256]{3,2,1,0:T(2,128)(2,1)} %param.22) | copy-start | bytes 4718596
  13.7 4.2 %copy-start.3 = (f32[1536]{0:T(1024)S(1)}, f32[1536]{0:T(1024)}, u32[]{:S(2)}) copy-start(f32[1536]{0:T(1024)} %refs_4_.3) | copy-start | bytes 18436
  13.7 20.2 %copy-start = (bf16[1,256,1536]{2,1,0:T(8,128)(2,1)S(1)}, bf16[1,256,1536]{2,1,0:T(8,128)(2,1)}, u32[]{:S(2)}) copy-start(bf16[1,256,1536]{2,1,0:T(8,128)(2,1)} %param.23) | copy-start | bytes 2359300
  13.7 4.2 %collective-permute-start.1 = (bf16[16,1536]{1,0:T(8,128)(2,1)S(1)}, bf16[16,1536]{1,0:T(8,128)(2,1)S(1)}, u32[]{:S(2)}, u32[]{:S(2)}) collective-permute-start(bf16[16,1536]{1,0:T(8,128)(2,1)S(1)} %get-tuple-element.45), channel_id=1, source_target_pairs={{0,1},{1,0},{2,3},{3,2},{4,5},{5,4},{6,7},{7,6},{8,9},{9,8},{10,11... | collective-permute-start | bytes 147464 | tf_op jit(solution)/shard_map/ppermute | solution.py:36
  18.0 4.5 %collective-permute-start.2 = (bf16[16,1664]{1,0:T(8,128)(2,1)S(1)}, bf16[16,1664]{1,0:T(8,128)(2,1)S(1)}, u32[]{:S(2)}, u32[]{:S(2)}) collective-permute-start(bf16[16,1664]{1,0:T(8,128)(2,1)S(1)} %bitcast.14), channel_id=1, source_target_pairs={{0,4},{2,6},{4,0},{6,2},{8,12},{10,14},{12,8},{14,10},{1,5},{3,7},... | collective-permute-start | bytes 159752 | tf_op jit(solution)/shard_map/ppermute | solution.py:690
  18.1 5.6 %collective-permute-start.3 = (bf16[16,1664]{1,0:T(8,128)(2,1)S(1)}, bf16[16,1664]{1,0:T(8,128)(2,1)S(1)}, u32[]{:S(2)}, u32[]{:S(2)}) collective-permute-start(bf16[16,1664]{1,0:T(8,128)(2,1)S(1)} %bitcast.15), channel_id=1, source_target_pairs={{0,8},{2,10},{4,12},{6,14},{8,0},{10,2},{12,4},{14,6},{1,9},{3,11}... | collective-permute-start | bytes 159752 | tf_op jit(solution)/shard_map/ppermute | solution.py:690
  21.2 5.9 %collective-permute-start.4 = (bf16[16,1664]{1,0:T(8,128)(2,1)S(1)}, bf16[16,1664]{1,0:T(8,128)(2,1)S(1)}, u32[]{:S(2)}, u32[]{:S(2)}) collective-permute-start(bf16[16,1664]{1,0:T(8,128)(2,1)S(1)} %bitcast.16), channel_id=1, source_target_pairs={{0,12},{2,14},{4,8},{6,10},{8,4},{10,6},{12,0},{14,2},{1,13},{3,15... | collective-permute-start | bytes 159752 | tf_op jit(solution)/shard_map/ppermute | solution.py:690
  27.2 6.7 %collective-permute-start.9 = (bf16[48,1664]{1,0:T(8,128)(2,1)S(1)}, bf16[48,1664]{1,0:T(8,128)(2,1)S(1)}, u32[]{:S(2)}, u32[]{:S(2)}) collective-permute-start(bf16[48,1664]{1,0:T(8,128)(2,1)S(1)} %get-tuple-element.56), channel_id=1, source_target_pairs={{0,2},{2,0},{4,6},{6,4},{8,10},{10,8},{12,14},{14,12},{1,3},{3,1},... | collective-permute-start | bytes 479240 | tf_op jit(solution)/shard_map/ppermute | solution.py:36
  29.7 4.1 %collective-permute-start.8 = (bf16[16,1664]{1,0:T(8,128)(2,1)S(1)}, bf16[16,1664]{1,0:T(8,128)(2,1)S(1)}, u32[]{:S(2)}, u32[]{:S(2)}) collective-permute-start(bf16[16,1664]{1,0:T(8,128)(2,1)S(1)} %bitcast.18), channel_id=1, source_target_pairs={{0,2},{2,0},{4,6},{6,4},{8,10},{10,8},{12,14},{14,12},{1,3},{3,1},... | collective-permute-start | bytes 159752 | tf_op jit(solution)/shard_map/ppermute | solution.py:36
  29.8 4.8 %collective-permute-start.5 = (bf16[64,1664]{1,0:T(8,128)(2,1)S(1)}, bf16[64,1664]{1,0:T(8,128)(2,1)S(1)}, u32[]{:S(2)}, u32[]{:S(2)}) collective-permute-start(bf16[64,1664]{1,0:T(8,128)(2,1)S(1)} %get-tuple-element.49.refs_0_), channel_id=1, source_target_pairs={{0,16},{16,0},{1,17},{17,1},{2,18},{18,2},{3,19},{19,3},{4,20},{20... | collective-permute-start | bytes 638984 | tf_op jit(solution)/shard_map/ppermute | solution.py:36
  33.9 2.0 %collective-permute-start.10 = (bf16[64,1664]{1,0:T(8,128)(2,1)S(1)}, bf16[64,1664]{1,0:T(8,128)(2,1)S(1)}, u32[]{:S(2)}, u32[]{:S(2)}) collective-permute-start(bf16[64,1664]{1,0:T(8,128)(2,1)S(1)} %joined.1.x.x_own), channel_id=1, source_target_pairs={{0,16},{16,0},{1,17},{17,1},{2,18},{18,2},{3,19},{19,3},{4,20},{20... | collective-permute-start | bytes 638984 | tf_op jit(solution)/shard_map/ppermute | solution.py:36
  35.3 1.6 %collective-permute-start.6 = (bf16[64,1536]{1,0:T(8,128)(2,1)S(1)}, bf16[64,1536]{1,0:T(8,128)(2,1)S(1)}, u32[]{:S(2)}, u32[]{:S(2)}) collective-permute-start(bf16[64,1536]{1,0:T(8,128)(2,1)S(1)} %get-tuple-element.53), channel_id=1, source_target_pairs={{0,16},{16,0},{1,17},{17,1},{2,18},{18,2},{3,19},{19,3},{4,20},{20... | collective-permute-start | bytes 589832 | tf_op jit(solution)/shard_map/ppermute | solution.py:36
  36.5 1.8 %collective-permute-start.11 = (bf16[64,1536]{1,0:T(8,128)(2,1)S(1)}, bf16[64,1536]{1,0:T(8,128)(2,1)S(1)}, u32[]{:S(2)}, u32[]{:S(2)}) collective-permute-start(bf16[64,1536]{1,0:T(8,128)(2,1)S(1)} %get-tuple-element.58), channel_id=1, source_target_pairs={{0,16},{16,0},{1,17},{17,1},{2,18},{18,2},{3,19},{19,3},{4,20},{20... | collective-permute-start | bytes 589832 | tf_op jit(solution)/shard_map/ppermute | solution.py:36
  37.0 5.1 %collective-permute-start.7 = (bf16[64,768]{1,0:T(8,128)(2,1)S(1)}, bf16[64,768]{1,0:T(8,128)(2,1)S(1)}, u32[]{:S(2)}, u32[]{:S(2)}) collective-permute-start(bf16[64,768]{1,0:T(8,128)(2,1)S(1)} %get-tuple-element.55), channel_id=1, source_target_pairs={{0,1},{1,0},{2,3},{3,2},{4,5},{5,4},{6,7},{7,6},{8,9},{9,8},{10,11... | collective-permute-start | bytes 294920 | tf_op jit(solution)/shard_map/ppermute | solution.py:36
  38.3 6.2 %collective-permute-start.12 = (bf16[64,768]{1,0:T(8,128)(2,1)S(1)}, bf16[64,768]{1,0:T(8,128)(2,1)S(1)}, u32[]{:S(2)}, u32[]{:S(2)}) collective-permute-start(bf16[64,768]{1,0:T(8,128)(2,1)S(1)} %get-tuple-element.59), channel_id=1, source_target_pairs={{0,2},{2,0},{4,6},{6,4},{8,10},{10,8},{12,14},{14,12},{1,3},{3,1},... | collective-permute-start | bytes 294920 | tf_op jit(solution)/shard_map/ppermute | solution.py:36
  40.1 5.5 %collective-permute-start.13 = (bf16[64,768]{1,0:T(8,128)(2,1)S(1)}, bf16[64,768]{1,0:T(8,128)(2,1)S(1)}, u32[]{:S(2)}, u32[]{:S(2)}) collective-permute-start(bf16[64,768]{1,0:T(8,128)(2,1)S(1)} %get-tuple-element.60), channel_id=1, source_target_pairs={{0,3},{1,2},{2,1},{3,0},{4,7},{5,6},{6,5},{7,4},{8,11},{9,10},{10,... | collective-permute-start | bytes 294920 | tf_op jit(solution)/shard_map/ppermute | solution.py:708
  45.6 4.5 %collective-permute-start.14 = (bf16[16,768]{1,0:T(8,128)(2,1)S(1)}, bf16[16,768]{1,0:T(8,128)(2,1)S(1)}, u32[]{:S(2)}, u32[]{:S(2)}) collective-permute-start(bf16[16,768]{1,0:T(8,128)(2,1)S(1)} %get-tuple-element.62), channel_id=1, source_target_pairs={{0,4},{2,6},{4,0},{6,2},{8,12},{10,14},{12,8},{14,10},{1,5},{3,7},... | collective-permute-start | bytes 73736 | tf_op jit(solution)/shard_map/ppermute | solution.py:710
  45.7 4.8 %collective-permute-start.15 = (bf16[16,768]{1,0:T(8,128)(2,1)S(1)}, bf16[16,768]{1,0:T(8,128)(2,1)S(1)}, u32[]{:S(2)}, u32[]{:S(2)}) collective-permute-start(bf16[16,768]{1,0:T(8,128)(2,1)S(1)} %get-tuple-element.63), channel_id=1, source_target_pairs={{0,8},{2,10},{4,12},{6,14},{8,0},{10,2},{12,4},{14,6},{1,9},{3,11}... | collective-permute-start | bytes 73736 | tf_op jit(solution)/shard_map/ppermute | solution.py:710
  46.8 5.6 %collective-permute-start.16 = (bf16[16,768]{1,0:T(8,128)(2,1)S(1)}, bf16[16,768]{1,0:T(8,128)(2,1)S(1)}, u32[]{:S(2)}, u32[]{:S(2)}) collective-permute-start(bf16[16,768]{1,0:T(8,128)(2,1)S(1)} %get-tuple-element.64), channel_id=1, source_target_pairs={{0,12},{2,14},{4,8},{6,10},{8,4},{10,6},{12,0},{14,2},{1,13},{3,15... | collective-permute-start | bytes 73736 | tf_op jit(solution)/shard_map/ppermute | solution.py:710

commit v4 on v3

--- a/solution.py
+++ b/solution.py
@@ -13,6 +13,7 @@
 QROWS = 16
 SPAN = 128
 UNROLL = 16
+EARLY = 17
 PIECES = 4
 MIB = 1 << 20
 
@@ -50,7 +51,7 @@
 def fetch_kernel(wide, per, *refs):
     (lens_hbm, ids_hbm, gates_hbm, gain_hbm, own_hbm, kv_hbm) = refs[:6]
     (own, gain, cos_out, sin_out, table_out, kvbuf, spans, items, count) = refs[6:15]
-    lens, ids_t, gates_t, sems, ksem = refs[15:]
+    lens, ids_t, gates_t, sems, ksem, rsem = refs[15:]
     rows = own.shape[0]
     rep = lax.axis_index("rep")
 
@@ -82,17 +83,24 @@
 
         items[r] = r * per
 
-    def plan_row(r, n):
+    def plan_row(r, carry):
+        n, early = carry
+        some, copy = rest_copy(kv_hbm, kvbuf, rsem, spans, wide, r)
+        soon = n < EARLY
+        pl.when(some & soon)(copy.start)
+
         def plan_chunk(c, n):
             items[n] = r * per + c
             return n + 1
 
-        return lax.fori_loop(1, (spans[r] + SPAN - 1) // SPAN, plan_chunk, n)
-
-    total = lax.fori_loop(0, rows, plan_row, rows)
+        later = lax.fori_loop(1, (spans[r] + SPAN - 1) // SPAN, plan_chunk, n)
+        return later, jnp.where(soon, r + 1, early)
+
+    total, early = lax.fori_loop(0, rows, plan_row, (rows, 0))
     for u in range(UNROLL):
         items[total + u] = rows * per
     count[0] = total
+    count[1] = early
 
     copies[1].wait()
     copies[2].wait()
@@ -118,6 +126,13 @@
 
     for copy in head_copies:
         copy.wait()
+
+    def arrive(r, carry):
+        some, copy = rest_copy(kv_hbm, kvbuf, rsem, spans, wide, r)
+        pl.when(some)(copy.wait)
+        return carry
+
+    lax.fori_loop(0, early, arrive, 0)
     for copy in copies[3:]:
         copy.wait()
 
@@ -140,7 +155,7 @@
     per = kv.shape[1] // wide
     outs = [(own.shape, bf16), (gain.shape, f32)]
     outs += [((rows, LANES), f32), ((rows, LANES), f32), ((rows, extra), bf16), (kv.shape, bf16)]
-    scalars = [(rows,), (rows * per + UNROLL,), (1,)]
+    scalars = [(rows,), (rows * per + UNROLL,), (2,)]
     return pl.pallas_call(
         lambda *refs: fetch_kernel(wide, per, *refs),
         out_shape=tuple(pltpu.VMEM(shape, dtype) for shape, dtype in outs)
@@ -152,6 +167,7 @@
             pltpu.VMEM(ids.shape[::-1], jnp.int32),
             pltpu.VMEM(gates.shape[::-1], f32),
             pltpu.SemaphoreType.DMA((5,)),
+            pltpu.SemaphoreType.DMA((rows,)),
             pltpu.SemaphoreType.DMA((rows,)),
         ],
         compiler_params=pltpu.CompilerParams(vmem_limit_bytes=8 * MIB),
@@ -174,12 +190,15 @@
     per = kv_hbm.shape[1] // wide
     tp = lax.axis_index("tp")
 
-    total = count[0]
+    total, early = count[0], count[1]
     blocks = (total + UNROLL - 1) // UNROLL
 
-    for r in range(rows):
+    def begin(r, carry):
         some, copy = rest_copy(kv_hbm, kvbuf, ksem, spans, wide, r)
         pl.when(some)(copy.start)
+        return carry
+
+    lax.fori_loop(early, rows, begin, 0)
     part = wo.shape[0] // PIECES
     wo_copies = [
         pltpu.make_async_copy(wo_hbm.at[pl.ds(i * part, part)], wo.at[pl.ds(i * part, part)], wsem.at[i])
@@ -252,10 +271,22 @@
         pl.when(some)(copy.wait)
         return carry
 
+    def merge(base, row_of):
+        for u in range(UNROLL):
+            r = row_of(u)
+            before = macc[r]
+            after = jnp.maximum(before, peaks[base + u])
+            macc[r] = after
+            fade, weight = jnp.exp(before - after), jnp.exp(peaks[base + u] - after)
+            lacc[r] = fade * lacc[r] + weight * sums[base + u]
+            oacc[r] = fade * oacc[r] + weight * mixes[base + u]
+
     def block(b, ready):
         last = jnp.minimum(items[b * UNROLL + UNROLL - 1] // per, rows - 1) + 1
         last = jnp.where(b * UNROLL + UNROLL <= rows, 0, last)
         lax.fori_loop(ready, last, arrive, 0)
+        earlier = jnp.maximum(b - 1, 0) * UNROLL
+        merge(b * UNROLL, lambda u: jnp.where(b == 0, rows, items[earlier + u] // per))
         got = [chunk(b * UNROLL + u) for u in range(UNROLL)]
         dots = [
             lax.dot_general(qb[r], kv, (((1,), (1,)), ((), ())), preferred_element_type=f32) for r, c, kv in got
@@ -268,36 +299,27 @@
             top = jnp.max(folded(jnp.maximum, s), axis=-1, keepdims=True)
             tops.append(jnp.broadcast_to(top, (QROWS, LANES)))
             probs.append(jnp.exp(s - top))
-        for u, ((r, c, kv), p) in enumerate(zip(got, probs)):
-            i = b * UNROLL + u
-            mixes[i] = jnp.dot(p.astype(bf16), kv, preferred_element_type=f32)
+        for u, p in enumerate(probs):
+            i = (b + 1) * UNROLL + u
+            mixes[i] = jnp.dot(p.astype(bf16), got[u][2], preferred_element_type=f32)
             sums[i] = folded(jnp.add, p)
             peaks[i] = tops[u]
-        for (r, c, kv), top in zip(got, tops):
-            macc[r] = jnp.maximum(macc[r], top)
         return jnp.maximum(ready, last)
 
-    ready = lax.fori_loop(0, blocks, block, 0)
+    mixes[:UNROLL] = jnp.zeros((UNROLL, QROWS, LANES), f32)
+    sums[:UNROLL] = jnp.zeros((UNROLL, QROWS, LANES), f32)
+    peaks[:UNROLL] = jnp.full((UNROLL, QROWS, LANES), MASKED, f32)
+    ready = lax.fori_loop(0, blocks, block, early)
     lax.fori_loop(ready, rows, arrive, 0)
+    merge(blocks * UNROLL, lambda u: items[(blocks - 1) * UNROLL + u] // per)
 
     own = jnp.sum(qf[...] * kvn[...], axis=-1, keepdims=True)
-    peak = jnp.maximum(macc[...].reshape(qf.shape), own)
-    own_p = jnp.exp(own - peak)
-    macc[...] = peak.reshape(macc.shape)
-
-    def merge(b, carry):
-        for u in range(UNROLL):
-            i = b * UNROLL + u
-            r = items[i] // per
-            weight = jnp.exp(peaks[i] - macc[r])
-            lacc[r] += weight * sums[i]
-            oacc[r] += weight * mixes[i]
-        return carry
-
-    lax.fori_loop(0, blocks, merge, 0)
-
-    total_p = jnp.sum(lacc[...].reshape(qf.shape), axis=-1, keepdims=True) + own_p
-    qf[...] = (oacc[...].reshape(qf.shape) + own_p * kvn[...]) / total_p
+    before = macc[...].reshape(qf.shape)
+    peak = jnp.maximum(before, own)
+    own_p, fade = jnp.exp(own - peak), jnp.exp(before - peak)
+
+    total_p = jnp.sum(fade * lacc[...].reshape(qf.shape), axis=-1, keepdims=True) + own_p
+    qf[...] = (fade * oacc[...].reshape(qf.shape) + own_p * kvn[...]) / total_p
     for k in range(n_query // 2):
         a = qf[pl.ds(2 * k, rows, stride=QROWS), :]
         b = qf[pl.ds(2 * k + 1, rows, stride=QROWS), :]
@@ -314,7 +336,7 @@
     width = wq.shape[0]
     n_kv = wkv.shape[1] // (2 * HEAD)
     per = kv.shape[1] // (SPAN * n_kv)
-    slots = rows * per + UNROLL
+    slots = rows * per + 2 * UNROLL
     many = rows + 1
     return pl.pallas_call(
         lambda *refs: attention_kernel(len(parts), *refs),

time: 53.2 us -> 52.3 us (0.983)
  local copies, waits for them, and re-layouts: 1.23 us -> 0.39 us
  Pallas kernels: 12.7 us -> 13.4 us
    pallas_call x1, Pallas kernels: 1.95 us -> 3.09 us  [fetch(): pl.pallas_call(lambda *refs: fetch_kernel(wide, per, *refs), out_shape=tu...]
    ppermute x3, waiting for transfers between devices: 4.67 us -> 3.62 us  [shards(): beside = [lax.ppermute(payload, 'req', step) for step in steps]]
    unnamed x11, local copies, waits for them, and re-layouts: 1.23 us -> 0.39 us
    ppermute x3, waiting for transfers between devices: 2.38 us -> 2.95 us  [shards(): lax.ppermute(other, 'req', step)]
  transfers between devices with their start and end apart: 17 -> 17, of which waited for: 11 -> 10; matrix products, arithmetic and copies ran while one was open for 1% -> 1% of each run, Pallas kernels for 8% -> 10%
where the time goes in v4:
time: 52.3 us
  starting transfers between devices  19.8 us (38%)
  waiting for transfers between devices  17.9 us (34%)
  Pallas kernels  13.4 us (26%)
  between operations  0.81 us (2%)
    ppermute x10, waiting for transfers between devices, swapped(): lax.ppermute(value, axis, [(i, i ^ 1) for i in range(lax.axis_size(axis))])  10.2 us
    ppermute x10, starting transfers between devices, swapped(): lax.ppermute(value, axis, [(i, i ^ 1) for i in range(lax.axis_size(axis))])  10.1 us
    pallas_call x1, Pallas kernels, attention(): pl.pallas_call(lambda *refs: attention_kernel(len(parts), *refs), out_sha...  7.43 us
    ppermute x3, starting transfers between devices, shards(): lax.ppermute(other, 'req', step)  4.44 us
    ppermute x3, starting transfers between devices, shards(): beside = [lax.ppermute(payload, 'req', step) for step in steps]  4.44 us
    ppermute x3, waiting for transfers between devices, shards(): beside = [lax.ppermute(payload, 'req', step) for step in steps]  3.62 us
    pallas_call x1, Pallas kernels, fetch(): pl.pallas_call(lambda *refs: fetch_kernel(wide, per, *refs), out_shape=tu...  3.09 us
    ppermute x3, waiting for transfers between devices, shards(): lax.ppermute(other, 'req', step)  2.95 us
  transfers between devices with their start and end apart: 17, of which 10 were waited for; matrix products, arithmetic and copies ran while one was open for 1% of the time, Pallas kernels for 10%

profile of v4, /device:TPU:0, one launch (start us, length us, event | category | flops | bytes accessed | tf_op | source)
XLA Modules:
  0.0 52.3 jit_solution(4605162685310057399)
XLA Ops:
  0.0 2.9 %collective-permute-start = (bf16[16,768]{1,0:T(8,128)(2,1)}, bf16[16,768]{1,0:T(8,128)(2,1)S(1)}, u32[]{:S(2)}, u32[]{:S(2)}) collective-permute-start(bf16[16,768]{1,0:T(8,128)(2,1)} %refs_4_.2), channel_id=1, source_target_pairs={{0,1},{1,0},{2,3},{3,2},{4,5},{5,4},{6,7},{7,6},{8,9},{9,8},{10,11... | collective-permute-start | bytes 73736 | tf_op jit(solution)/shard_map/ppermute | solution.py:37
  2.9 3.1 %fetch.1 = (bf16[16,768]{1,0:T(8,128)(2,1)S(1)}, f32[1536]{0:T(1024)S(1)}, f32[16,128]{1,0:T(8,128)S(1)}, f32[16,128]{1,0:T(8,128)S(1)}, bf16[16,128]{1,0:T(8,12...) custom-call(s32[2,16]{1,0:T(2,128)} %refs_0_.2, ...), custom_call_target="tpu_custom_call" | custom-call | tf_op jit(solution)/shard_map/fetch/pallas_call | solution.py:159
  6.1 7.4 %attention.1 = (bf16[16,1536]{1,0:T(8,128)(2,1)S(1)}, f32[16,1536]{1,0:T(8,128)S(1)}, bf16[16,1536]{1,0:T(8,128)(2,1)S(1)}, bf16[16,4096,128]{2,1,0:T(8,128)(2,1)S(1)}) custom-call(s32[16]{0:T(128)S(4)} %get-tuple-element.35.refs_0_, s32[144]{0:T(256)S(4)} %get-tuple-element.36.refs_1_, ...), custom_call_target="tpu_custom_call", output_to_operand_aliasing={{3}: (10, {})} | custom-call | tf_op jit(solution)/shard_map/attention/pallas_call | solution.py:341
  13.6 1.0 %collective-permute-start.1 = (bf16[16,1536]{1,0:T(8,128)(2,1)S(1)}, bf16[16,1536]{1,0:T(8,128)(2,1)S(1)}, u32[]{:S(2)}, u32[]{:S(2)}) collective-permute-start(bf16[16,1536]{1,0:T(8,128)(2,1)S(1)} %get-tuple-element.45), channel_id=1, source_target_pairs={{0,1},{1,0},{2,3},{3,2},{4,5},{5,4},{6,7},{7,6},{8,9},{9,8},{10,11... | collective-permute-start | bytes 147464 | tf_op jit(solution)/shard_map/ppermute | solution.py:37
  14.5 0.4 copy.15
  15.5 2.2 %collective-permute-done.1.refs_3_ = bf16[16,1536]{1,0:T(8,128)(2,1)S(1)} collective-permute-done((bf16[16,1536]{1,0:T(8,128)(2,1)S(1)}, bf16[16,1536]{1,0:T(8,128)(2,1)S(1)}, u32[]{:S(2)}, u32[]{:S(2)}) %collective-permute-start.1) | collective-permute-done | bytes 49184 | tf_op jit(solution)/shard_map/ppermute | solution.py:37
  17.7 0.1 expert_input.1
  17.8 0.1 collective-permute-start.2
  17.9 2.0 %collective-permute-start.3 = (bf16[16,1664]{1,0:T(8,128)(2,1)S(1)}, bf16[16,1664]{1,0:T(8,128)(2,1)S(1)}, u32[]{:S(2)}, u32[]{:S(2)}) collective-permute-start(bf16[16,1664]{1,0:T(8,128)(2,1)S(1)} %bitcast.15), channel_id=1, source_target_pairs={{0,8},{2,10},{4,12},{6,14},{8,0},{10,2},{12,4},{14,6},{1,9},{3,11}... | collective-permute-start | bytes 159752 | tf_op jit(solution)/shard_map/ppermute | solution.py:712
  19.9 2.4 %collective-permute-start.4 = (bf16[16,1664]{1,0:T(8,128)(2,1)S(1)}, bf16[16,1664]{1,0:T(8,128)(2,1)S(1)}, u32[]{:S(2)}, u32[]{:S(2)}) collective-permute-start(bf16[16,1664]{1,0:T(8,128)(2,1)S(1)} %bitcast.16), channel_id=1, source_target_pairs={{0,12},{2,14},{4,8},{6,10},{8,4},{10,6},{12,0},{14,2},{1,13},{3,15... | collective-permute-start | bytes 159752 | tf_op jit(solution)/shard_map/ppermute | solution.py:712
  22.3 1.2 %collective-permute-done.3.refs_2_ = bf16[16,1664]{1,0:T(8,128)(2,1)S(1)} collective-permute-done((bf16[16,1664]{1,0:T(8,128)(2,1)S(1)}, bf16[16,1664]{1,0:T(8,128)(2,1)S(1)}, u32[]{:S(2)}, u32[]{:S(2)}) %collective-permute-start.3) | collective-permute-done | bytes 53280 | tf_op jit(solution)/shard_map/ppermute | solution.py:712
  23.4 2.5 %collective-permute-done.4.refs_3_ = bf16[16,1664]{1,0:T(8,128)(2,1)S(1)} collective-permute-done((bf16[16,1664]{1,0:T(8,128)(2,1)S(1)}, bf16[16,1664]{1,0:T(8,128)(2,1)S(1)}, u32[]{:S(2)}, u32[]{:S(2)}) %collective-permute-start.4) | collective-permute-done | bytes 53280 | tf_op jit(solution)/shard_map/ppermute | solution.py:712
  25.9 2.6 %collective-permute-start.9 = (bf16[48,1664]{1,0:T(8,128)(2,1)S(1)}, bf16[48,1664]{1,0:T(8,128)(2,1)S(1)}, u32[]{:S(2)}, u32[]{:S(2)}) collective-permute-start(bf16[48,1664]{1,0:T(8,128)(2,1)S(1)} %get-tuple-element.56), channel_id=1, source_target_pairs={{0,2},{2,0},{4,6},{6,4},{8,10},{10,8},{12,14},{14,12},{1,3},{3,1},... | collective-permute-start | bytes 479240 | tf_op jit(solution)/shard_map/ppermute | solution.py:37
  28.6 0.1 collective-permute-start.8
  28.6 4.1 %collective-permute-done.8.first = bf16[16,1664]{1,0:T(8,128)(2,1)S(1)} collective-permute-done((bf16[16,1664]{1,0:T(8,128)(2,1)S(1)}, bf16[16,1664]{1,0:T(8,128)(2,1)S(1)}, u32[]{:S(2)}, u32[]{:S(2)}) %collective-permute-start.8) | collective-permute-done | bytes 53280 | tf_op jit(solution)/shard_map/ppermute | solution.py:37
  32.8 0.6 %own_expert.1.y_own = f32[64,1536]{1,0:T(8,128)S(1)} custom-call(bf16[64,1664]{1,0:T(8,128)(2,1)S(1)} %joined.1.x.x_own, bf16[1536,512]{1,0:T(8,128)(2,1)S(1)} %bitcast.8, bf16[256,1536]{1,0:T(8,128)(2,1)S(1)} %bitcast.11), custom_call_target="tpu_custom_call" | custom-call | flops 150994944 | bytes 3342336 | tf_op jit(solution)/shard_map/own_expert/pallas_call | solution.py:462
  33.4 0.7 %home_expert.1 = (f32[64,1536]{1,0:T(8,128)S(1)}, bf16[64,1536]{1,0:T(8,128)(2,1)S(1)}) custom-call(bf16[64,1664]{1,0:T(8,128)(2,1)S(1)} %get-tuple-element.49.refs_0_, bf16[64,1664]{1,0:T(8,128)(2,1)S(1)} %collective-permute-done.5.refs_1_, f32[16,768]{1,0:T(8,128)S(1)} %get-tuple-element.50.refs_2_, bf16[1536,512]{1,0:T(8,128)(2,1)S(1)} %bitcast.9, ...), custom_call_target="tpu_custom_call" | custom-call | flops 301989888 | bytes 4325376 | tf_op jit(solution)/shard_map/home_expert/pallas_call | solution.py:525
  34.1 0.6 %collective-permute-start.6 = (bf16[64,1536]{1,0:T(8,128)(2,1)S(1)}, bf16[64,1536]{1,0:T(8,128)(2,1)S(1)}, u32[]{:S(2)}, u32[]{:S(2)}) collective-permute-start(bf16[64,1536]{1,0:T(8,128)(2,1)S(1)} %get-tuple-element.53), channel_id=1, source_target_pairs={{0,16},{16,0},{1,17},{17,1},{2,18},{18,2},{3,19},{19,3},{4,20},{20... | collective-permute-start | bytes 589832 | tf_op jit(solution)/shard_map/ppermute | solution.py:37
  34.7 0.6 %other_expert.1 = (f32[64,1536]{1,0:T(8,128)S(1)}, bf16[64,1536]{1,0:T(8,128)(2,1)S(1)}) custom-call(bf16[64,1664]{1,0:T(8,128)(2,1)S(1)} %joined.1.x.x_own, bf16[64,1664]{1,0:T(8,128)(2,1)S(1)} %collective-permute-done.10.x_other, f32[64,1536]{1,0:T(8,128)S(1)} %own_expert.1.y_own, bf16[1536,512]{1,0:T(8,128)(2,1)S(1)} %bitcast.10, ...), custom_call_target="tpu_custom_call" | custom-call | flops 150994944 | bytes 3342336 | tf_op jit(solution)/shard_map/other_expert/pallas_call | solution.py:547
  35.3 0.1 collective-permute-start.11
  35.4 0.4 collective-permute-done.6.recv
  35.8 1.0 %collective-permute-start.7 = (bf16[64,768]{1,0:T(8,128)(2,1)S(1)}, bf16[64,768]{1,0:T(8,128)(2,1)S(1)}, u32[]{:S(2)}, u32[]{:S(2)}) collective-permute-start(bf16[64,768]{1,0:T(8,128)(2,1)S(1)} %get-tuple-element.55), channel_id=1, source_target_pairs={{0,1},{1,0},{2,3},{3,2},{4,5},{5,4},{6,7},{7,6},{8,9},{9,8},{10,11... | collective-permute-start | bytes 294920 | tf_op jit(solution)/shard_map/ppermute | solution.py:37
  36.9 1.8 %collective-permute-start.12 = (bf16[64,768]{1,0:T(8,128)(2,1)S(1)}, bf16[64,768]{1,0:T(8,128)(2,1)S(1)}, u32[]{:S(2)}, u32[]{:S(2)}) collective-permute-start(bf16[64,768]{1,0:T(8,128)(2,1)S(1)} %get-tuple-element.59), channel_id=1, source_target_pairs={{0,2},{2,0},{4,6},{6,4},{8,10},{10,8},{12,14},{14,12},{1,3},{3,1},... | collective-permute-start | bytes 294920 | tf_op jit(solution)/shard_map/ppermute | solution.py:37
  38.7 0.8 %collective-permute-start.13 = (bf16[64,768]{1,0:T(8,128)(2,1)S(1)}, bf16[64,768]{1,0:T(8,128)(2,1)S(1)}, u32[]{:S(2)}, u32[]{:S(2)}) collective-permute-start(bf16[64,768]{1,0:T(8,128)(2,1)S(1)} %get-tuple-element.60), channel_id=1, source_target_pairs={{0,3},{1,2},{2,1},{3,0},{4,7},{5,6},{6,5},{7,4},{8,11},{9,10},{10,... | collective-permute-start | bytes 294920 | tf_op jit(solution)/shard_map/ppermute | solution.py:730
  39.5 1.4 %collective-permute-done.7.refs_0_ = bf16[64,768]{1,0:T(8,128)(2,1)S(1)} collective-permute-done((bf16[64,768]{1,0:T(8,128)(2,1)S(1)}, bf16[64,768]{1,0:T(8,128)(2,1)S(1)}, u32[]{:S(2)}, u32[]{:S(2)}) %collective-permute-start.7) | collective-permute-done | bytes 98336 | tf_op jit(solution)/shard_map/ppermute | solution.py:37
  41.0 2.2 %collective-permute-done.12.refs_1_ = bf16[64,768]{1,0:T(8,128)(2,1)S(1)} collective-permute-done((bf16[64,768]{1,0:T(8,128)(2,1)S(1)}, bf16[64,768]{1,0:T(8,128)(2,1)S(1)}, u32[]{:S(2)}, u32[]{:S(2)}) %collective-permute-start.12) | collective-permute-done | bytes 98336 | tf_op jit(solution)/shard_map/ppermute | solution.py:37
  43.1 1.1 %collective-permute-done.13.refs_2_ = bf16[64,768]{1,0:T(8,128)(2,1)S(1)} collective-permute-done((bf16[64,768]{1,0:T(8,128)(2,1)S(1)}, bf16[64,768]{1,0:T(8,128)(2,1)S(1)}, u32[]{:S(2)}, u32[]{:S(2)}) %collective-permute-start.13) | collective-permute-done | bytes 98336 | tf_op jit(solution)/shard_map/ppermute | solution.py:730
  44.3 1.7 %collective-permute-start.15 = (bf16[16,768]{1,0:T(8,128)(2,1)S(1)}, bf16[16,768]{1,0:T(8,128)(2,1)S(1)}, u32[]{:S(2)}, u32[]{:S(2)}) collective-permute-start(bf16[16,768]{1,0:T(8,128)(2,1)S(1)} %get-tuple-element.63), channel_id=1, source_target_pairs={{0,8},{2,10},{4,12},{6,14},{8,0},{10,2},{12,4},{14,6},{1,9},{3,11}... | collective-permute-start | bytes 73736 | tf_op jit(solution)/shard_map/ppermute | solution.py:732
  46.0 2.7 %collective-permute-start.16 = (bf16[16,768]{1,0:T(8,128)(2,1)S(1)}, bf16[16,768]{1,0:T(8,128)(2,1)S(1)}, u32[]{:S(2)}, u32[]{:S(2)}) collective-permute-start(bf16[16,768]{1,0:T(8,128)(2,1)S(1)} %get-tuple-element.64), channel_id=1, source_target_pairs={{0,12},{2,14},{4,8},{6,10},{8,4},{10,6},{12,0},{14,2},{1,13},{3,15... | collective-permute-start | bytes 73736 | tf_op jit(solution)/shard_map/ppermute | solution.py:732
  48.7 0.4 collective-permute-done.15.refs_2_
  49.1 2.5 %collective-permute-done.16.refs_3_ = bf16[16,768]{1,0:T(8,128)(2,1)S(1)} collective-permute-done((bf16[16,768]{1,0:T(8,128)(2,1)S(1)}, bf16[16,768]{1,0:T(8,128)(2,1)S(1)}, u32[]{:S(2)}, u32[]{:S(2)}) %collective-permute-start.16) | collective-permute-done | bytes 24608 | tf_op jit(solution)/shard_map/ppermute | solution.py:732
  51.7 0.6 %line_sum.1 = bf16[16,768]{1,0:T(8,128)(2,1)} custom-call(f32[16,768]{1,0:T(8,128)S(1)} %get-tuple-element.61.refs_0_, bf16[16,768]{1,0:T(8,128)(2,1)S(1)} %collective-permute-done.14.refs_1_, bf16[16,768]{1,0:T(8,128)(2,1)S(1)} %collective-permute-done.15.refs_2_, bf16[16,768]{1,0:T(8,128)(2,1)S(1)} %collective-permute-done.16.refs_3_), custom_call_target="tpu_custom_call" | custom-call | tf_op jit(solution)/shard_map/line_sum/pallas_call | solution.py:633
  (25 shorter events, 0.4 us)
Async XLA Ops:
  0.0 6.0 %collective-permute-start = (bf16[16,768]{1,0:T(8,128)(2,1)}, bf16[16,768]{1,0:T(8,128)(2,1)S(1)}, u32[]{:S(2)}, u32[]{:S(2)}) collective-permute-start(bf16[16,768]{1,0:T(8,128)(2,1)} %refs_4_.2), channel_id=1, source_target_pairs={{0,1},{1,0},{2,3},{3,2},{4,5},{5,4},{6,7},{7,6},{8,9},{9,8},{10,11... | collective-permute-start | bytes 73736 | tf_op jit(solution)/shard_map/ppermute | solution.py:37
  2.9 3.1 %copy-start.1 = (bf16[1536,768]{1,0:T(8,128)(2,1)S(1)}, bf16[1536,768]{1,0:T(8,128)(2,1)}, u32[]{:S(2)}) copy-start(bf16[1536,768]{1,0:T(8,128)(2,1)} %refs_8_.1) | copy-start | bytes 7077892
  2.9 3.1 %copy-start.2 = (bf16[1536,512]{1,0:T(8,128)(2,1)S(1)}, bf16[1536,512]{1,0:T(8,128)(2,1)}, u32[]{:S(2)}) copy-start(bf16[1536,512]{1,0:T(8,128)(2,1)} %refs_9_.1) | copy-start | bytes 4718596
  6.1 8.4 %copy-start.4 = (bf16[1,1536,2,256]{3,2,1,0:T(2,128)(2,1)S(1)}, bf16[1,1536,2,256]{3,2,1,0:T(2,128)(2,1)}, u32[]{:S(2)}) copy-start(bf16[1,1536,2,256]{3,2,1,0:T(2,128)(2,1)} %param.22) | copy-start | bytes 4718596
  13.5 4.2 %copy-start.3 = (f32[1536]{0:T(1024)S(1)}, f32[1536]{0:T(1024)}, u32[]{:S(2)}) copy-start(f32[1536]{0:T(1024)} %refs_4_.3) | copy-start | bytes 18436
  13.5 19.3 %copy-start = (bf16[1,256,1536]{2,1,0:T(8,128)(2,1)S(1)}, bf16[1,256,1536]{2,1,0:T(8,128)(2,1)}, u32[]{:S(2)}) copy-start(bf16[1,256,1536]{2,1,0:T(8,128)(2,1)} %param.23) | copy-start | bytes 2359300
  13.6 4.2 %collective-permute-start.1 = (bf16[16,1536]{1,0:T(8,128)(2,1)S(1)}, bf16[16,1536]{1,0:T(8,128)(2,1)S(1)}, u32[]{:S(2)}, u32[]{:S(2)}) collective-permute-start(bf16[16,1536]{1,0:T(8,128)(2,1)S(1)} %get-tuple-element.45), channel_id=1, source_target_pairs={{0,1},{1,0},{2,3},{3,2},{4,5},{5,4},{6,7},{7,6},{8,9},{9,8},{10,11... | collective-permute-start | bytes 147464 | tf_op jit(solution)/shard_map/ppermute | solution.py:37
  17.8 4.5 %collective-permute-start.2 = (bf16[16,1664]{1,0:T(8,128)(2,1)S(1)}, bf16[16,1664]{1,0:T(8,128)(2,1)S(1)}, u32[]{:S(2)}, u32[]{:S(2)}) collective-permute-start(bf16[16,1664]{1,0:T(8,128)(2,1)S(1)} %bitcast.14), channel_id=1, source_target_pairs={{0,4},{2,6},{4,0},{6,2},{8,12},{10,14},{12,8},{14,10},{1,5},{3,7},... | collective-permute-start | bytes 159752 | tf_op jit(solution)/shard_map/ppermute | solution.py:712
  17.9 5.5 %collective-permute-start.3 = (bf16[16,1664]{1,0:T(8,128)(2,1)S(1)}, bf16[16,1664]{1,0:T(8,128)(2,1)S(1)}, u32[]{:S(2)}, u32[]{:S(2)}) collective-permute-start(bf16[16,1664]{1,0:T(8,128)(2,1)S(1)} %bitcast.15), channel_id=1, source_target_pairs={{0,8},{2,10},{4,12},{6,14},{8,0},{10,2},{12,4},{14,6},{1,9},{3,11}... | collective-permute-start | bytes 159752 | tf_op jit(solution)/shard_map/ppermute | solution.py:712
  19.9 6.0 %collective-permute-start.4 = (bf16[16,1664]{1,0:T(8,128)(2,1)S(1)}, bf16[16,1664]{1,0:T(8,128)(2,1)S(1)}, u32[]{:S(2)}, u32[]{:S(2)}) collective-permute-start(bf16[16,1664]{1,0:T(8,128)(2,1)S(1)} %bitcast.16), channel_id=1, source_target_pairs={{0,12},{2,14},{4,8},{6,10},{8,4},{10,6},{12,0},{14,2},{1,13},{3,15... | collective-permute-start | bytes 159752 | tf_op jit(solution)/shard_map/ppermute | solution.py:712
  25.9 6.8 %collective-permute-start.9 = (bf16[48,1664]{1,0:T(8,128)(2,1)S(1)}, bf16[48,1664]{1,0:T(8,128)(2,1)S(1)}, u32[]{:S(2)}, u32[]{:S(2)}) collective-permute-start(bf16[48,1664]{1,0:T(8,128)(2,1)S(1)} %get-tuple-element.56), channel_id=1, source_target_pairs={{0,2},{2,0},{4,6},{6,4},{8,10},{10,8},{12,14},{14,12},{1,3},{3,1},... | collective-permute-start | bytes 479240 | tf_op jit(solution)/shard_map/ppermute | solution.py:37
  28.6 4.1 %collective-permute-start.8 = (bf16[16,1664]{1,0:T(8,128)(2,1)S(1)}, bf16[16,1664]{1,0:T(8,128)(2,1)S(1)}, u32[]{:S(2)}, u32[]{:S(2)}) collective-permute-start(bf16[16,1664]{1,0:T(8,128)(2,1)S(1)} %bitcast.18), channel_id=1, source_target_pairs={{0,2},{2,0},{4,6},{6,4},{8,10},{10,8},{12,14},{14,12},{1,3},{3,1},... | collective-permute-start | bytes 159752 | tf_op jit(solution)/shard_map/ppermute | solution.py:37
  28.6 4.8 %collective-permute-start.5 = (bf16[64,1664]{1,0:T(8,128)(2,1)S(1)}, bf16[64,1664]{1,0:T(8,128)(2,1)S(1)}, u32[]{:S(2)}, u32[]{:S(2)}) collective-permute-start(bf16[64,1664]{1,0:T(8,128)(2,1)S(1)} %get-tuple-element.49.refs_0_), channel_id=1, source_target_pairs={{0,16},{16,0},{1,17},{17,1},{2,18},{18,2},{3,19},{19,3},{4,20},{20... | collective-permute-start | bytes 638984 | tf_op jit(solution)/shard_map/ppermute | solution.py:37
  32.7 2.0 %collective-permute-start.10 = (bf16[64,1664]{1,0:T(8,128)(2,1)S(1)}, bf16[64,1664]{1,0:T(8,128)(2,1)S(1)}, u32[]{:S(2)}, u32[]{:S(2)}) collective-permute-start(bf16[64,1664]{1,0:T(8,128)(2,1)S(1)} %joined.1.x.x_own), channel_id=1, source_target_pairs={{0,16},{16,0},{1,17},{17,1},{2,18},{18,2},{3,19},{19,3},{4,20},{20... | collective-permute-start | bytes 638984 | tf_op jit(solution)/shard_map/ppermute | solution.py:37
  34.1 1.6 %collective-permute-start.6 = (bf16[64,1536]{1,0:T(8,128)(2,1)S(1)}, bf16[64,1536]{1,0:T(8,128)(2,1)S(1)}, u32[]{:S(2)}, u32[]{:S(2)}) collective-permute-start(bf16[64,1536]{1,0:T(8,128)(2,1)S(1)} %get-tuple-element.53), channel_id=1, source_target_pairs={{0,16},{16,0},{1,17},{17,1},{2,18},{18,2},{3,19},{19,3},{4,20},{20... | collective-permute-start | bytes 589832 | tf_op jit(solution)/shard_map/ppermute | solution.py:37
  35.3 1.5 %collective-permute-start.11 = (bf16[64,1536]{1,0:T(8,128)(2,1)S(1)}, bf16[64,1536]{1,0:T(8,128)(2,1)S(1)}, u32[]{:S(2)}, u32[]{:S(2)}) collective-permute-start(bf16[64,1536]{1,0:T(8,128)(2,1)S(1)} %get-tuple-element.58), channel_id=1, source_target_pairs={{0,16},{16,0},{1,17},{17,1},{2,18},{18,2},{3,19},{19,3},{4,20},{20... | collective-permute-start | bytes 589832 | tf_op jit(solution)/shard_map/ppermute | solution.py:37
  35.8 5.1 %collective-permute-start.7 = (bf16[64,768]{1,0:T(8,128)(2,1)S(1)}, bf16[64,768]{1,0:T(8,128)(2,1)S(1)}, u32[]{:S(2)}, u32[]{:S(2)}) collective-permute-start(bf16[64,768]{1,0:T(8,128)(2,1)S(1)} %get-tuple-element.55), channel_id=1, source_target_pairs={{0,1},{1,0},{2,3},{3,2},{4,5},{5,4},{6,7},{7,6},{8,9},{9,8},{10,11... | collective-permute-start | bytes 294920 | tf_op jit(solution)/shard_map/ppermute | solution.py:37
  36.9 6.2 %collective-permute-start.12 = (bf16[64,768]{1,0:T(8,128)(2,1)S(1)}, bf16[64,768]{1,0:T(8,128)(2,1)S(1)}, u32[]{:S(2)}, u32[]{:S(2)}) collective-permute-start(bf16[64,768]{1,0:T(8,128)(2,1)S(1)} %get-tuple-element.59), channel_id=1, source_target_pairs={{0,2},{2,0},{4,6},{6,4},{8,10},{10,8},{12,14},{14,12},{1,3},{3,1},... | collective-permute-start | bytes 294920 | tf_op jit(solution)/shard_map/ppermute | solution.py:37
  38.7 5.6 %collective-permute-start.13 = (bf16[64,768]{1,0:T(8,128)(2,1)S(1)}, bf16[64,768]{1,0:T(8,128)(2,1)S(1)}, u32[]{:S(2)}, u32[]{:S(2)}) collective-permute-start(bf16[64,768]{1,0:T(8,128)(2,1)S(1)} %get-tuple-element.60), channel_id=1, source_target_pairs={{0,3},{1,2},{2,1},{3,0},{4,7},{5,6},{6,5},{7,4},{8,11},{9,10},{10,... | collective-permute-start | bytes 294920 | tf_op jit(solution)/shard_map/ppermute | solution.py:730
  44.3 4.5 %collective-permute-start.14 = (bf16[16,768]{1,0:T(8,128)(2,1)S(1)}, bf16[16,768]{1,0:T(8,128)(2,1)S(1)}, u32[]{:S(2)}, u32[]{:S(2)}) collective-permute-start(bf16[16,768]{1,0:T(8,128)(2,1)S(1)} %get-tuple-element.62), channel_id=1, source_target_pairs={{0,4},{2,6},{4,0},{6,2},{8,12},{10,14},{12,8},{14,10},{1,5},{3,7},... | collective-permute-start | bytes 73736 | tf_op jit(solution)/shard_map/ppermute | solution.py:732
  44.3 4.8 %collective-permute-start.15 = (bf16[16,768]{1,0:T(8,128)(2,1)S(1)}, bf16[16,768]{1,0:T(8,128)(2,1)S(1)}, u32[]{:S(2)}, u32[]{:S(2)}) collective-permute-start(bf16[16,768]{1,0:T(8,128)(2,1)S(1)} %get-tuple-element.63), channel_id=1, source_target_pairs={{0,8},{2,10},{4,12},{6,14},{8,0},{10,2},{12,4},{14,6},{1,9},{3,11}... | collective-permute-start | bytes 73736 | tf_op jit(solution)/shard_map/ppermute | solution.py:732
  46.0 5.6 %collective-permute-start.16 = (bf16[16,768]{1,0:T(8,128)(2,1)S(1)}, bf16[16,768]{1,0:T(8,128)(2,1)S(1)}, u32[]{:S(2)}, u32[]{:S(2)}) collective-permute-start(bf16[16,768]{1,0:T(8,128)(2,1)S(1)} %get-tuple-element.64), channel_id=1, source_target_pairs={{0,12},{2,14},{4,8},{6,10},{8,4},{10,6},{12,0},{14,2},{1,13},{3,15... | collective-permute-start | bytes 73736 | tf_op jit(solution)/shard_map/ppermute | solution.py:732

commit v5 on v4

--- a/solution.py
+++ b/solution.py
@@ -453,23 +453,6 @@
     return jnp.dot(active, down, preferred_element_type=f32)
 
 
-def own_expert_kernel(x, gate_up, down, y):
-    width = down.shape[1]
-    y[...] = expert_rows(x[:, :width], gate_up[...], down[...])
-
-
-def own_expert(x, gate_up, down):
-    return pl.pallas_call(
-        own_expert_kernel,
-        out_shape=pltpu.VMEM((x.shape[0], down.shape[1]), f32),
-        in_specs=[vmem()] * 3,
-        out_specs=vmem(),
-        compiler_params=pltpu.CompilerParams(vmem_limit_bytes=32 * MIB),
-        cost_estimate=expert_cost(x.shape[0], gate_up, down),
-        name="own_expert",
-    )(*near(x), gate_up, down)
-
-
 def expert_cost(count, gate_up, down):
     return pl.CostEstimate(
         flops=2 * count * (gate_up.size + down.size),
@@ -498,11 +481,15 @@
     send[...] = jnp.where(moved, from_own, from_other).astype(bf16)
 
 
-def home_expert_kernel(n_tp, place, x_own, x_other, residual, gate_up, down, keep, send, mine):
+def home_expert_kernel(n_tp, place, n_more, x_own, x_other, residual, gate_up, down, *refs):
+    more, (keep, send), rest = refs[:n_more], refs[n_more : n_more + 2], refs[n_more + 2 :]
+    mine = rest[-1]
     width = down.shape[1]
     count = x_own.shape[0]
-    both = jnp.concatenate([x_own[:, :width], x_other[:, :width]], axis=0)
-    y = expert_rows(both, gate_up[...], down[...])
+    rows_of = [x_own[:, :width], x_other[:, :width]] + [x[:, :width] for x in more]
+    y = expert_rows(jnp.concatenate(rows_of, axis=0), gate_up[...], down[...])
+    for i, out in enumerate(rest[:-1]):
+        out[...] = y[(2 + i) * count : (3 + i) * count]
     rows, part = residual.shape
     tp = lax.axis_index("tp")
     here = pl.ds(place() * rows, rows)
@@ -517,21 +504,21 @@
 
         return mine[...]
 
-    traded(width, x_own, x_other, from_own, lambda: y[count:], keep, send)
-
-
-def home_expert(n_tp, place, x_own, x_other, residual, gate_up, down):
+    traded(width, x_own, x_other, from_own, lambda: y[count : 2 * count], keep, send)
+
+
+def home_expert(n_tp, place, x_own, x_other, residual, gate_up, down, *more):
     shape = (x_own.shape[0], down.shape[1])
     return pl.pallas_call(
-        lambda *refs: home_expert_kernel(n_tp, place, *refs),
-        out_shape=(pltpu.VMEM(shape, f32), pltpu.VMEM(shape, bf16)),
-        in_specs=[vmem()] * 5,
-        out_specs=(vmem(), vmem()),
+        lambda *refs: home_expert_kernel(n_tp, place, len(more), *refs),
+        out_shape=(pltpu.VMEM(shape, f32), pltpu.VMEM(shape, bf16)) + (pltpu.VMEM(shape, f32),) * len(more),
+        in_specs=[vmem()] * (5 + len(more)),
+        out_specs=(vmem(),) * (2 + len(more)),
         scratch_shapes=[pltpu.VMEM(shape, f32)],
         compiler_params=pltpu.CompilerParams(vmem_limit_bytes=40 * MIB if shape[0] > 256 else 16 * MIB),
         cost_estimate=expert_cost(2 * shape[0], gate_up, down),
         name="home_expert",
-    )(*near(x_own, x_other, residual), gate_up, down)
+    )(*near(x_own, x_other, residual), gate_up, down, *near(*more))
 
 
 def other_expert_kernel(x_own, x_other, y_own, gate_up, down, keep, send):
@@ -714,12 +701,11 @@
         home, tail = stacked([payload] + beside)
         away = joined(across, swapped(tail, "req"))
         home_other = swapped(home, "rep")
-        home_keep, home_send = home_expert(
-            n_tp, lambda: 0, home, home_other, residual, gate_up, down
+        home_keep, home_send, away_own = home_expert(
+            n_tp, lambda: 0, home, home_other, residual, gate_up, down, away
         )
         home_recv = swapped(home_send, "rep")
         away_other = swapped(away, "rep")
-        away_own = own_expert(away, gate_up, down)
         away_keep, away_send = other_expert(away, away_other, away_own, gate_up, down)
         away_recv = swapped(away_send, "rep")
         home_mine, home_cross = halves(home_keep, home_recv, f32)

time: 52.3 us -> 52.1 us (level)
  Pallas kernels: 13.4 us -> 11.9 us
  starting transfers between devices: 19.8 us -> 20.9 us
    ppermute x10, starting transfers between devices: 10.1 us -> 11.3 us  [swapped(): lax.ppermute(value, axis, [(i, i ^ 1) for i in range(lax.axis_size(axis))])]
    pallas_call x1, Pallas kernels: 7.43 us -> 6.43 us  [attention(): pl.pallas_call(lambda *refs: attention_kernel(len(parts), *refs), out_sha...]
    ppermute x3, waiting for transfers between devices: 3.62 us -> 4.47 us  [shards(): beside = [lax.ppermute(payload, 'req', step) for step in steps]]
    ppermute x3, waiting for transfers between devices: 2.95 us -> 2.37 us  [shards(): lax.ppermute(other, 'req', step)]
    pallas_call x2 -> x1, Pallas kernels: 1.31 us -> 0.85 us  [home_expert(): pl.pallas_call(lambda *refs: home_expert_kernel(n_tp, place, len(more), *...]
  transfers between devices with their start and end apart: 17 -> 17, of which waited for: 10 -> 11; matrix products, arithmetic and copies ran while one was open for 1% -> 1% of each run, Pallas kernels for 10% -> 9%
where the time goes in v5:
time: 52.1 us; the launch traced here: 52.2 us
  starting transfers between devices  20.9 us (40%)
  waiting for transfers between devices  18.2 us (35%)
  Pallas kernels  11.9 us (23%)
  between operations  0.8 us (2%)
    ppermute x10, starting transfers between devices, swapped(): lax.ppermute(value, axis, [(i, i ^ 1) for i in range(lax.axis_size(axis))])  11.3 us
    ppermute x10, waiting for transfers between devices, swapped(): lax.ppermute(value, axis, [(i, i ^ 1) for i in range(lax.axis_size(axis))])  10.3 us
    pallas_call x1, Pallas kernels, attention(): pl.pallas_call(lambda *refs: attention_kernel(len(parts), *refs), out_sha...  6.43 us
    ppermute x3, waiting for transfers between devices, shards(): beside = [lax.ppermute(payload, 'req', step) for step in steps]  4.47 us
    ppermute x3, starting transfers between devices, shards(): beside = [lax.ppermute(payload, 'req', step) for step in steps]  4.45 us
    ppermute x3, starting transfers between devices, shards(): lax.ppermute(other, 'req', step)  4.44 us
    pallas_call x1, Pallas kernels, fetch(): pl.pallas_call(lambda *refs: fetch_kernel(wide, per, *refs), out_shape=tu...  3.09 us
    ppermute x3, waiting for transfers between devices, shards(): lax.ppermute(other, 'req', step)  2.37 us
  transfers between devices with their start and end apart: 17, of which 11 were waited for; matrix products, arithmetic and copies ran while one was open for 1% of the time, Pallas kernels for 9%

profile of v5, /device:TPU:0, one launch (start us, length us, event | category | flops | bytes accessed | tf_op | source)
XLA Modules:
  0.0 52.2 jit_solution(18276124962784435986)
XLA Ops:
  0.0 2.9 %collective-permute-start = (bf16[16,768]{1,0:T(8,128)(2,1)}, bf16[16,768]{1,0:T(8,128)(2,1)S(1)}, u32[]{:S(2)}, u32[]{:S(2)}) collective-permute-start(bf16[16,768]{1,0:T(8,128)(2,1)} %refs_4_.2), channel_id=1, source_target_pairs={{0,1},{1,0},{2,3},{3,2},{4,5},{5,4},{6,7},{7,6},{8,9},{9,8},{10,11... | collective-permute-start | bytes 73736 | tf_op jit(solution)/shard_map/ppermute | solution.py:37
  2.9 3.1 %fetch.1 = (bf16[16,768]{1,0:T(8,128)(2,1)S(1)}, f32[1536]{0:T(1024)S(1)}, f32[16,128]{1,0:T(8,128)S(1)}, f32[16,128]{1,0:T(8,128)S(1)}, bf16[16,128]{1,0:T(8,12...) custom-call(s32[2,16]{1,0:T(2,128)} %refs_0_.2, ...), custom_call_target="tpu_custom_call" | custom-call | tf_op jit(solution)/shard_map/fetch/pallas_call | solution.py:159
  6.1 6.4 %attention.1 = (bf16[16,1536]{1,0:T(8,128)(2,1)S(1)}, f32[16,1536]{1,0:T(8,128)S(1)}, bf16[16,1536]{1,0:T(8,128)(2,1)S(1)}, bf16[16,4096,128]{2,1,0:T(8,128)(2,1)S(1)}) custom-call(s32[16]{0:T(128)S(4)} %get-tuple-element.36.refs_0_, s32[144]{0:T(256)S(4)} %get-tuple-element.37.refs_1_, ...), custom_call_target="tpu_custom_call", output_to_operand_aliasing={{3}: (10, {})} | custom-call | tf_op jit(solution)/shard_map/attention/pallas_call | solution.py:341
  12.5 1.0 %collective-permute-start.1 = (bf16[16,1536]{1,0:T(8,128)(2,1)S(1)}, bf16[16,1536]{1,0:T(8,128)(2,1)S(1)}, u32[]{:S(2)}, u32[]{:S(2)}) collective-permute-start(bf16[16,1536]{1,0:T(8,128)(2,1)S(1)} %get-tuple-element.46), channel_id=1, source_target_pairs={{0,1},{1,0},{2,3},{3,2},{4,5},{5,4},{6,7},{7,6},{8,9},{9,8},{10,11... | collective-permute-start | bytes 147464 | tf_op jit(solution)/shard_map/ppermute | solution.py:37
  13.5 0.3 copy.15
  14.5 2.3 %collective-permute-done.1.refs_3_ = bf16[16,1536]{1,0:T(8,128)(2,1)S(1)} collective-permute-done((bf16[16,1536]{1,0:T(8,128)(2,1)S(1)}, bf16[16,1536]{1,0:T(8,128)(2,1)S(1)}, u32[]{:S(2)}, u32[]{:S(2)}) %collective-permute-start.1) | collective-permute-done | bytes 49184 | tf_op jit(solution)/shard_map/ppermute | solution.py:37
  16.8 0.1 expert_input.1
  16.9 1.6 %collective-permute-start.2 = (bf16[16,1664]{1,0:T(8,128)(2,1)S(1)}, bf16[16,1664]{1,0:T(8,128)(2,1)S(1)}, u32[]{:S(2)}, u32[]{:S(2)}) collective-permute-start(bf16[16,1664]{1,0:T(8,128)(2,1)S(1)} %bitcast.12), channel_id=1, source_target_pairs={{0,4},{2,6},{4,0},{6,2},{8,12},{10,14},{12,8},{14,10},{1,5},{3,7},... | collective-permute-start | bytes 159752 | tf_op jit(solution)/shard_map/ppermute | solution.py:699
  18.5 1.3 %collective-permute-start.3 = (bf16[16,1664]{1,0:T(8,128)(2,1)S(1)}, bf16[16,1664]{1,0:T(8,128)(2,1)S(1)}, u32[]{:S(2)}, u32[]{:S(2)}) collective-permute-start(bf16[16,1664]{1,0:T(8,128)(2,1)S(1)} %bitcast.13), channel_id=1, source_target_pairs={{0,8},{2,10},{4,12},{6,14},{8,0},{10,2},{12,4},{14,6},{1,9},{3,11}... | collective-permute-start | bytes 159752 | tf_op jit(solution)/shard_map/ppermute | solution.py:699
  19.8 1.6 %collective-permute-start.4 = (bf16[16,1664]{1,0:T(8,128)(2,1)S(1)}, bf16[16,1664]{1,0:T(8,128)(2,1)S(1)}, u32[]{:S(2)}, u32[]{:S(2)}) collective-permute-start(bf16[16,1664]{1,0:T(8,128)(2,1)S(1)} %bitcast.14), channel_id=1, source_target_pairs={{0,12},{2,14},{4,8},{6,10},{8,4},{10,6},{12,0},{14,2},{1,13},{3,15... | collective-permute-start | bytes 159752 | tf_op jit(solution)/shard_map/ppermute | solution.py:699
  21.3 0.1 collective-permute-done.2.refs_1_
  21.5 3.7 %collective-permute-done.3.refs_2_ = bf16[16,1664]{1,0:T(8,128)(2,1)S(1)} collective-permute-done((bf16[16,1664]{1,0:T(8,128)(2,1)S(1)}, bf16[16,1664]{1,0:T(8,128)(2,1)S(1)}, u32[]{:S(2)}, u32[]{:S(2)}) %collective-permute-start.3) | collective-permute-done | bytes 53280 | tf_op jit(solution)/shard_map/ppermute | solution.py:699
  25.2 0.6 %collective-permute-done.4.refs_3_ = bf16[16,1664]{1,0:T(8,128)(2,1)S(1)} collective-permute-done((bf16[16,1664]{1,0:T(8,128)(2,1)S(1)}, bf16[16,1664]{1,0:T(8,128)(2,1)S(1)}, u32[]{:S(2)}, u32[]{:S(2)}) %collective-permute-start.4) | collective-permute-done | bytes 53280 | tf_op jit(solution)/shard_map/ppermute | solution.py:699
  25.9 3.5 %collective-permute-start.7 = (bf16[48,1664]{1,0:T(8,128)(2,1)S(1)}, bf16[48,1664]{1,0:T(8,128)(2,1)S(1)}, u32[]{:S(2)}, u32[]{:S(2)}) collective-permute-start(bf16[48,1664]{1,0:T(8,128)(2,1)S(1)} %get-tuple-element.53), channel_id=1, source_target_pairs={{0,2},{2,0},{4,6},{6,4},{8,10},{10,8},{12,14},{14,12},{1,3},{3,1},... | collective-permute-start | bytes 479240 | tf_op jit(solution)/shard_map/ppermute | solution.py:37
  29.4 0.1 collective-permute-start.6
  29.5 4.1 %collective-permute-done.6.first = bf16[16,1664]{1,0:T(8,128)(2,1)S(1)} collective-permute-done((bf16[16,1664]{1,0:T(8,128)(2,1)S(1)}, bf16[16,1664]{1,0:T(8,128)(2,1)S(1)}, u32[]{:S(2)}, u32[]{:S(2)}) %collective-permute-start.6) | collective-permute-done | bytes 53280 | tf_op jit(solution)/shard_map/ppermute | solution.py:37
  33.6 0.9 %home_expert.1 = (f32[64,1536]{1,0:T(8,128)S(1)}, bf16[64,1536]{1,0:T(8,128)(2,1)S(1)}, f32[64,1536]{1,0:T(8,128)S(1)}) custom-call(bf16[64,1664]{1,0:T(8,128)(2,1)S(1)} %get-tuple-element.50.refs_0_, bf16[64,1664]{1,0:T(8,128)(2,1)S(1)} %collective-permute-done.5.refs_1_, f32[16,768]{1,0:T(8,128)S(1)} %get-tuple-element.51.refs_2_, ...), custom_call_target="tpu_custom_call" | custom-call | flops 301989888 | bytes 4325376 | tf_op jit(solution)/shard_map/home_expert/pallas_call | solution.py:512
  34.5 0.5 %collective-permute-start.8 = (bf16[64,1536]{1,0:T(8,128)(2,1)S(1)}, bf16[64,1536]{1,0:T(8,128)(2,1)S(1)}, u32[]{:S(2)}, u32[]{:S(2)}) collective-permute-start(bf16[64,1536]{1,0:T(8,128)(2,1)S(1)} %get-tuple-element.55), channel_id=1, source_target_pairs={{0,16},{16,0},{1,17},{17,1},{2,18},{18,2},{3,19},{19,3},{4,20},{20... | collective-permute-start | bytes 589832 | tf_op jit(solution)/shard_map/ppermute | solution.py:37
  35.1 0.6 %other_expert.1 = (f32[64,1536]{1,0:T(8,128)S(1)}, bf16[64,1536]{1,0:T(8,128)(2,1)S(1)}) custom-call(bf16[64,1664]{1,0:T(8,128)(2,1)S(1)} %joined.1.refs_5_.x_own, bf16[64,1664]{1,0:T(8,128)(2,1)S(1)} %collective-permute-done.10.x_other, f32[64,1536]{1,0:T(8,128)S(1)} %get-tuple-element.58.y_own, bf16[1536,512]{1,0:T(8,128)(2,1)S(1)} %bitcast.9, ...), custom_call_target="tpu_custom_call" | custom-call | flops 150994944 | bytes 3342336 | tf_op jit(solution)/shard_map/other_expert/pallas_call | solution.py:534
  35.7 0.2 collective-permute-start.11
  35.9 0.2 collective-permute-done.8.recv
  36.2 1.2 %collective-permute-start.9 = (bf16[64,768]{1,0:T(8,128)(2,1)S(1)}, bf16[64,768]{1,0:T(8,128)(2,1)S(1)}, u32[]{:S(2)}, u32[]{:S(2)}) collective-permute-start(bf16[64,768]{1,0:T(8,128)(2,1)S(1)} %get-tuple-element.57), channel_id=1, source_target_pairs={{0,1},{1,0},{2,3},{3,2},{4,5},{5,4},{6,7},{7,6},{8,9},{9,8},{10,11... | collective-permute-start | bytes 294920 | tf_op jit(solution)/shard_map/ppermute | solution.py:37
  37.4 1.8 %collective-permute-start.12 = (bf16[64,768]{1,0:T(8,128)(2,1)S(1)}, bf16[64,768]{1,0:T(8,128)(2,1)S(1)}, u32[]{:S(2)}, u32[]{:S(2)}) collective-permute-start(bf16[64,768]{1,0:T(8,128)(2,1)S(1)} %get-tuple-element.61), channel_id=1, source_target_pairs={{0,2},{2,0},{4,6},{6,4},{8,10},{10,8},{12,14},{14,12},{1,3},{3,1},... | collective-permute-start | bytes 294920 | tf_op jit(solution)/shard_map/ppermute | solution.py:37
  39.2 0.7 %collective-permute-start.13 = (bf16[64,768]{1,0:T(8,128)(2,1)S(1)}, bf16[64,768]{1,0:T(8,128)(2,1)S(1)}, u32[]{:S(2)}, u32[]{:S(2)}) collective-permute-start(bf16[64,768]{1,0:T(8,128)(2,1)S(1)} %get-tuple-element.62), channel_id=1, source_target_pairs={{0,3},{1,2},{2,1},{3,0},{4,7},{5,6},{6,5},{7,4},{8,11},{9,10},{10,... | collective-permute-start | bytes 294920 | tf_op jit(solution)/shard_map/ppermute | solution.py:716
  39.9 1.4 %collective-permute-done.9.refs_0_ = bf16[64,768]{1,0:T(8,128)(2,1)S(1)} collective-permute-done((bf16[64,768]{1,0:T(8,128)(2,1)S(1)}, bf16[64,768]{1,0:T(8,128)(2,1)S(1)}, u32[]{:S(2)}, u32[]{:S(2)}) %collective-permute-start.9) | collective-permute-done | bytes 98336 | tf_op jit(solution)/shard_map/ppermute | solution.py:37
  41.3 2.3 %collective-permute-done.12.refs_1_ = bf16[64,768]{1,0:T(8,128)(2,1)S(1)} collective-permute-done((bf16[64,768]{1,0:T(8,128)(2,1)S(1)}, bf16[64,768]{1,0:T(8,128)(2,1)S(1)}, u32[]{:S(2)}, u32[]{:S(2)}) %collective-permute-start.12) | collective-permute-done | bytes 98336 | tf_op jit(solution)/shard_map/ppermute | solution.py:37
  43.6 1.1 %collective-permute-done.13.refs_2_ = bf16[64,768]{1,0:T(8,128)(2,1)S(1)} collective-permute-done((bf16[64,768]{1,0:T(8,128)(2,1)S(1)}, bf16[64,768]{1,0:T(8,128)(2,1)S(1)}, u32[]{:S(2)}, u32[]{:S(2)}) %collective-permute-start.13) | collective-permute-done | bytes 98336 | tf_op jit(solution)/shard_map/ppermute | solution.py:716
  44.8 1.1 %collective-permute-start.15 = (bf16[16,768]{1,0:T(8,128)(2,1)S(1)}, bf16[16,768]{1,0:T(8,128)(2,1)S(1)}, u32[]{:S(2)}, u32[]{:S(2)}) collective-permute-start(bf16[16,768]{1,0:T(8,128)(2,1)S(1)} %get-tuple-element.65), channel_id=1, source_target_pairs={{0,8},{2,10},{4,12},{6,14},{8,0},{10,2},{12,4},{14,6},{1,9},{3,11}... | collective-permute-start | bytes 73736 | tf_op jit(solution)/shard_map/ppermute | solution.py:718
  46.0 3.3 %collective-permute-start.16 = (bf16[16,768]{1,0:T(8,128)(2,1)S(1)}, bf16[16,768]{1,0:T(8,128)(2,1)S(1)}, u32[]{:S(2)}, u32[]{:S(2)}) collective-permute-start(bf16[16,768]{1,0:T(8,128)(2,1)S(1)} %get-tuple-element.66), channel_id=1, source_target_pairs={{0,12},{2,14},{4,8},{6,10},{8,4},{10,6},{12,0},{14,2},{1,13},{3,15... | collective-permute-start | bytes 73736 | tf_op jit(solution)/shard_map/ppermute | solution.py:718
  49.2 0.4 collective-permute-done.15.refs_2_
  49.6 2.0 %collective-permute-done.16.refs_3_ = bf16[16,768]{1,0:T(8,128)(2,1)S(1)} collective-permute-done((bf16[16,768]{1,0:T(8,128)(2,1)S(1)}, bf16[16,768]{1,0:T(8,128)(2,1)S(1)}, u32[]{:S(2)}, u32[]{:S(2)}) %collective-permute-start.16) | collective-permute-done | bytes 24608 | tf_op jit(solution)/shard_map/ppermute | solution.py:718
  51.6 0.6 %line_sum.1 = bf16[16,768]{1,0:T(8,128)(2,1)} custom-call(f32[16,768]{1,0:T(8,128)S(1)} %get-tuple-element.63.refs_0_, bf16[16,768]{1,0:T(8,128)(2,1)S(1)} %collective-permute-done.14.refs_1_, bf16[16,768]{1,0:T(8,128)(2,1)S(1)} %collective-permute-done.15.refs_2_, bf16[16,768]{1,0:T(8,128)(2,1)S(1)} %collective-permute-done.16.refs_3_), custom_call_target="tpu_custom_call" | custom-call | tf_op jit(solution)/shard_map/line_sum/pallas_call | solution.py:620
  (24 shorter events, 0.4 us)
Async XLA Ops:
  0.0 6.0 %collective-permute-start = (bf16[16,768]{1,0:T(8,128)(2,1)}, bf16[16,768]{1,0:T(8,128)(2,1)S(1)}, u32[]{:S(2)}, u32[]{:S(2)}) collective-permute-start(bf16[16,768]{1,0:T(8,128)(2,1)} %refs_4_.2), channel_id=1, source_target_pairs={{0,1},{1,0},{2,3},{3,2},{4,5},{5,4},{6,7},{7,6},{8,9},{9,8},{10,11... | collective-permute-start | bytes 73736 | tf_op jit(solution)/shard_map/ppermute | solution.py:37
  2.9 3.1 %copy-start.1 = (bf16[1536,768]{1,0:T(8,128)(2,1)S(1)}, bf16[1536,768]{1,0:T(8,128)(2,1)}, u32[]{:S(2)}) copy-start(bf16[1536,768]{1,0:T(8,128)(2,1)} %refs_8_.1) | copy-start | bytes 7077892
  2.9 3.1 %copy-start.2 = (bf16[1536,512]{1,0:T(8,128)(2,1)S(1)}, bf16[1536,512]{1,0:T(8,128)(2,1)}, u32[]{:S(2)}) copy-start(bf16[1536,512]{1,0:T(8,128)(2,1)} %refs_9_.1) | copy-start | bytes 4718596
  6.1 7.4 %copy-start.4 = (bf16[1,1536,2,256]{3,2,1,0:T(2,128)(2,1)S(1)}, bf16[1,1536,2,256]{3,2,1,0:T(2,128)(2,1)}, u32[]{:S(2)}) copy-start(bf16[1,1536,2,256]{3,2,1,0:T(2,128)(2,1)} %param.22) | copy-start | bytes 4718596
  12.5 4.2 %copy-start.3 = (f32[1536]{0:T(1024)S(1)}, f32[1536]{0:T(1024)}, u32[]{:S(2)}) copy-start(f32[1536]{0:T(1024)} %refs_4_.3) | copy-start | bytes 18436
  12.5 21.1 %copy-start = (bf16[1,256,1536]{2,1,0:T(8,128)(2,1)S(1)}, bf16[1,256,1536]{2,1,0:T(8,128)(2,1)}, u32[]{:S(2)}) copy-start(bf16[1,256,1536]{2,1,0:T(8,128)(2,1)} %param.23) | copy-start | bytes 2359300
  12.5 4.2 %collective-permute-start.1 = (bf16[16,1536]{1,0:T(8,128)(2,1)S(1)}, bf16[16,1536]{1,0:T(8,128)(2,1)S(1)}, u32[]{:S(2)}, u32[]{:S(2)}) collective-permute-start(bf16[16,1536]{1,0:T(8,128)(2,1)S(1)} %get-tuple-element.46), channel_id=1, source_target_pairs={{0,1},{1,0},{2,3},{3,2},{4,5},{5,4},{6,7},{7,6},{8,9},{9,8},{10,11... | collective-permute-start | bytes 147464 | tf_op jit(solution)/shard_map/ppermute | solution.py:37
  16.9 4.6 %collective-permute-start.2 = (bf16[16,1664]{1,0:T(8,128)(2,1)S(1)}, bf16[16,1664]{1,0:T(8,128)(2,1)S(1)}, u32[]{:S(2)}, u32[]{:S(2)}) collective-permute-start(bf16[16,1664]{1,0:T(8,128)(2,1)S(1)} %bitcast.12), channel_id=1, source_target_pairs={{0,4},{2,6},{4,0},{6,2},{8,12},{10,14},{12,8},{14,10},{1,5},{3,7},... | collective-permute-start | bytes 159752 | tf_op jit(solution)/shard_map/ppermute | solution.py:699
  18.5 6.7 %collective-permute-start.3 = (bf16[16,1664]{1,0:T(8,128)(2,1)S(1)}, bf16[16,1664]{1,0:T(8,128)(2,1)S(1)}, u32[]{:S(2)}, u32[]{:S(2)}) collective-permute-start(bf16[16,1664]{1,0:T(8,128)(2,1)S(1)} %bitcast.13), channel_id=1, source_target_pairs={{0,8},{2,10},{4,12},{6,14},{8,0},{10,2},{12,4},{14,6},{1,9},{3,11}... | collective-permute-start | bytes 159752 | tf_op jit(solution)/shard_map/ppermute | solution.py:699
  19.8 6.0 %collective-permute-start.4 = (bf16[16,1664]{1,0:T(8,128)(2,1)S(1)}, bf16[16,1664]{1,0:T(8,128)(2,1)S(1)}, u32[]{:S(2)}, u32[]{:S(2)}) collective-permute-start(bf16[16,1664]{1,0:T(8,128)(2,1)S(1)} %bitcast.14), channel_id=1, source_target_pairs={{0,12},{2,14},{4,8},{6,10},{8,4},{10,6},{12,0},{14,2},{1,13},{3,15... | collective-permute-start | bytes 159752 | tf_op jit(solution)/shard_map/ppermute | solution.py:699
  25.9 7.7 %collective-permute-start.7 = (bf16[48,1664]{1,0:T(8,128)(2,1)S(1)}, bf16[48,1664]{1,0:T(8,128)(2,1)S(1)}, u32[]{:S(2)}, u32[]{:S(2)}) collective-permute-start(bf16[48,1664]{1,0:T(8,128)(2,1)S(1)} %get-tuple-element.53), channel_id=1, source_target_pairs={{0,2},{2,0},{4,6},{6,4},{8,10},{10,8},{12,14},{14,12},{1,3},{3,1},... | collective-permute-start | bytes 479240 | tf_op jit(solution)/shard_map/ppermute | solution.py:37
  29.4 4.1 %collective-permute-start.6 = (bf16[16,1664]{1,0:T(8,128)(2,1)S(1)}, bf16[16,1664]{1,0:T(8,128)(2,1)S(1)}, u32[]{:S(2)}, u32[]{:S(2)}) collective-permute-start(bf16[16,1664]{1,0:T(8,128)(2,1)S(1)} %bitcast.16), channel_id=1, source_target_pairs={{0,2},{2,0},{4,6},{6,4},{8,10},{10,8},{12,14},{14,12},{1,3},{3,1},... | collective-permute-start | bytes 159752 | tf_op jit(solution)/shard_map/ppermute | solution.py:37
  29.5 4.2 %collective-permute-start.5 = (bf16[64,1664]{1,0:T(8,128)(2,1)S(1)}, bf16[64,1664]{1,0:T(8,128)(2,1)S(1)}, u32[]{:S(2)}, u32[]{:S(2)}) collective-permute-start(bf16[64,1664]{1,0:T(8,128)(2,1)S(1)} %get-tuple-element.50.refs_0_), channel_id=1, source_target_pairs={{0,16},{16,0},{1,17},{17,1},{2,18},{18,2},{3,19},{19,3},{4,20},{20... | collective-permute-start | bytes 638984 | tf_op jit(solution)/shard_map/ppermute | solution.py:37
  33.5 1.5 %collective-permute-start.10 = (bf16[64,1664]{1,0:T(8,128)(2,1)S(1)}, bf16[64,1664]{1,0:T(8,128)(2,1)S(1)}, u32[]{:S(2)}, u32[]{:S(2)}) collective-permute-start(bf16[64,1664]{1,0:T(8,128)(2,1)S(1)} %joined.1.refs_5_.x_own), channel_id=1, source_target_pairs={{0,16},{16,0},{1,17},{17,1},{2,18},{18,2},{3,19},{19,3},{4,20},{20... | collective-permute-start | bytes 638984 | tf_op jit(solution)/shard_map/ppermute | solution.py:37
  34.5 1.6 %collective-permute-start.8 = (bf16[64,1536]{1,0:T(8,128)(2,1)S(1)}, bf16[64,1536]{1,0:T(8,128)(2,1)S(1)}, u32[]{:S(2)}, u32[]{:S(2)}) collective-permute-start(bf16[64,1536]{1,0:T(8,128)(2,1)S(1)} %get-tuple-element.55), channel_id=1, source_target_pairs={{0,16},{16,0},{1,17},{17,1},{2,18},{18,2},{3,19},{19,3},{4,20},{20... | collective-permute-start | bytes 589832 | tf_op jit(solution)/shard_map/ppermute | solution.py:37
  35.7 1.7 %collective-permute-start.11 = (bf16[64,1536]{1,0:T(8,128)(2,1)S(1)}, bf16[64,1536]{1,0:T(8,128)(2,1)S(1)}, u32[]{:S(2)}, u32[]{:S(2)}) collective-permute-start(bf16[64,1536]{1,0:T(8,128)(2,1)S(1)} %get-tuple-element.60), channel_id=1, source_target_pairs={{0,16},{16,0},{1,17},{17,1},{2,18},{18,2},{3,19},{19,3},{4,20},{20... | collective-permute-start | bytes 589832 | tf_op jit(solution)/shard_map/ppermute | solution.py:37
  36.2 5.1 %collective-permute-start.9 = (bf16[64,768]{1,0:T(8,128)(2,1)S(1)}, bf16[64,768]{1,0:T(8,128)(2,1)S(1)}, u32[]{:S(2)}, u32[]{:S(2)}) collective-permute-start(bf16[64,768]{1,0:T(8,128)(2,1)S(1)} %get-tuple-element.57), channel_id=1, source_target_pairs={{0,1},{1,0},{2,3},{3,2},{4,5},{5,4},{6,7},{7,6},{8,9},{9,8},{10,11... | collective-permute-start | bytes 294920 | tf_op jit(solution)/shard_map/ppermute | solution.py:37
  37.4 6.2 %collective-permute-start.12 = (bf16[64,768]{1,0:T(8,128)(2,1)S(1)}, bf16[64,768]{1,0:T(8,128)(2,1)S(1)}, u32[]{:S(2)}, u32[]{:S(2)}) collective-permute-start(bf16[64,768]{1,0:T(8,128)(2,1)S(1)} %get-tuple-element.61), channel_id=1, source_target_pairs={{0,2},{2,0},{4,6},{6,4},{8,10},{10,8},{12,14},{14,12},{1,3},{3,1},... | collective-permute-start | bytes 294920 | tf_op jit(solution)/shard_map/ppermute | solution.py:37
  39.2 5.5 %collective-permute-start.13 = (bf16[64,768]{1,0:T(8,128)(2,1)S(1)}, bf16[64,768]{1,0:T(8,128)(2,1)S(1)}, u32[]{:S(2)}, u32[]{:S(2)}) collective-permute-start(bf16[64,768]{1,0:T(8,128)(2,1)S(1)} %get-tuple-element.62), channel_id=1, source_target_pairs={{0,3},{1,2},{2,1},{3,0},{4,7},{5,6},{6,5},{7,4},{8,11},{9,10},{10,... | collective-permute-start | bytes 294920 | tf_op jit(solution)/shard_map/ppermute | solution.py:716
  44.8 4.5 %collective-permute-start.14 = (bf16[16,768]{1,0:T(8,128)(2,1)S(1)}, bf16[16,768]{1,0:T(8,128)(2,1)S(1)}, u32[]{:S(2)}, u32[]{:S(2)}) collective-permute-start(bf16[16,768]{1,0:T(8,128)(2,1)S(1)} %get-tuple-element.64), channel_id=1, source_target_pairs={{0,4},{2,6},{4,0},{6,2},{8,12},{10,14},{12,8},{14,10},{1,5},{3,7},... | collective-permute-start | bytes 73736 | tf_op jit(solution)/shard_map/ppermute | solution.py:718
  44.8 4.8 %collective-permute-start.15 = (bf16[16,768]{1,0:T(8,128)(2,1)S(1)}, bf16[16,768]{1,0:T(8,128)(2,1)S(1)}, u32[]{:S(2)}, u32[]{:S(2)}) collective-permute-start(bf16[16,768]{1,0:T(8,128)(2,1)S(1)} %get-tuple-element.65), channel_id=1, source_target_pairs={{0,8},{2,10},{4,12},{6,14},{8,0},{10,2},{12,4},{14,6},{1,9},{3,11}... | collective-permute-start | bytes 73736 | tf_op jit(solution)/shard_map/ppermute | solution.py:718
  46.0 5.6 %collective-permute-start.16 = (bf16[16,768]{1,0:T(8,128)(2,1)S(1)}, bf16[16,768]{1,0:T(8,128)(2,1)S(1)}, u32[]{:S(2)}, u32[]{:S(2)}) collective-permute-start(bf16[16,768]{1,0:T(8,128)(2,1)S(1)} %get-tuple-element.66), channel_id=1, source_target_pairs={{0,12},{2,14},{4,8},{6,10},{8,4},{10,6},{12,0},{14,2},{1,13},{3,15... | collective-permute-start | bytes 73736 | tf_op jit(solution)/shard_map/ppermute | solution.py:718

commit v6 on v5

--- a/solution.py
+++ b/solution.py
@@ -695,7 +695,7 @@
     payload, residual = expert_input(n_tp, 1 if by_permute else n_req, migrate, tokens, keep, other, moe_gain, table)
     if by_permute:
         payload = payload[0]
-        steps = [[(q, q ^ 2 * k) for q in range(n_req)] for k in (1, 2, 3)]
+        steps = [[(q, q ^ 2 * k) for q in range(n_req)] for k in (3, 2, 1)]
         beside = [lax.ppermute(payload, "req", step) for step in steps]
         across = swapped(payload, "req")
         home, tail = stacked([payload] + beside)

time: 52.1 us -> 50.5 us (0.969)
  waiting for transfers between devices: 18.2 us -> 17.2 us
  starting transfers between devices: 20.9 us -> 20 us
    ppermute x10, starting transfers between devices: 11.3 us -> 8.62 us  [swapped(): lax.ppermute(value, axis, [(i, i ^ 1) for i in range(lax.axis_size(axis))])]
    ppermute x1, starting transfers between devices: 0.71 us -> 1.91 us  [shards(): from_corner = lax.ppermute(away_cross, ('req', 'tp'), corner)]
    ppermute x1, waiting for transfers between devices: 1.11 us -> 0.01 us  [shards(): from_corner = lax.ppermute(away_cross, ('req', 'tp'), corner)]
    ppermute x3, starting transfers between devices: 4.45 us -> 5.03 us  [shards(): beside = [lax.ppermute(payload, 'req', step) for step in steps]]
  transfers between devices with their start and end apart: 17 -> 17, of which waited for: 11 -> 10; matrix products, arithmetic and copies ran while one was open for 1% -> 1% of each run, Pallas kernels for 9% -> 9%
where the time goes in v6:
time: 50.5 us; the launch traced here: 50.3 us
  starting transfers between devices  20 us (40%)
  waiting for transfers between devices  17.2 us (34%)
  Pallas kernels  11.9 us (24%)
  between operations  0.8 us (2%)
    ppermute x10, waiting for transfers between devices, swapped(): lax.ppermute(value, axis, [(i, i ^ 1) for i in range(lax.axis_size(axis))])  10.8 us
    ppermute x10, starting transfers between devices, swapped(): lax.ppermute(value, axis, [(i, i ^ 1) for i in range(lax.axis_size(axis))])  8.62 us
    pallas_call x1, Pallas kernels, attention(): pl.pallas_call(lambda *refs: attention_kernel(len(parts), *refs), out_sha...  6.43 us
    ppermute x3, starting transfers between devices, shards(): beside = [lax.ppermute(payload, 'req', step) for step in steps]  5.03 us
    ppermute x3, starting transfers between devices, shards(): lax.ppermute(other, 'req', step)  4.45 us
    ppermute x3, waiting for transfers between devices, shards(): beside = [lax.ppermute(payload, 'req', step) for step in steps]  4.39 us
    pallas_call x1, Pallas kernels, fetch(): pl.pallas_call(lambda *refs: fetch_kernel(wide, per, *refs), out_shape=tu...  3.09 us
    ppermute x3, waiting for transfers between devices, shards(): lax.ppermute(other, 'req', step)  2.07 us
  transfers between devices with their start and end apart: 17, of which 10 were waited for; matrix products, arithmetic and copies ran while one was open for 1% of the time, Pallas kernels for 9%

profile of v6, /device:TPU:0, one launch (start us, length us, event | category | flops | bytes accessed | tf_op | source)
XLA Modules:
  0.0 50.3 jit_solution(323552720576689660)
XLA Ops:
  0.0 2.9 %collective-permute-start = (bf16[16,768]{1,0:T(8,128)(2,1)}, bf16[16,768]{1,0:T(8,128)(2,1)S(1)}, u32[]{:S(2)}, u32[]{:S(2)}) collective-permute-start(bf16[16,768]{1,0:T(8,128)(2,1)} %refs_4_.2), channel_id=1, source_target_pairs={{0,1},{1,0},{2,3},{3,2},{4,5},{5,4},{6,7},{7,6},{8,9},{9,8},{10,11... | collective-permute-start | bytes 73736 | tf_op jit(solution)/shard_map/ppermute | solution.py:37
  2.9 3.1 %fetch.1 = (bf16[16,768]{1,0:T(8,128)(2,1)S(1)}, f32[1536]{0:T(1024)S(1)}, f32[16,128]{1,0:T(8,128)S(1)}, f32[16,128]{1,0:T(8,128)S(1)}, bf16[16,128]{1,0:T(8,12...) custom-call(s32[2,16]{1,0:T(2,128)} %refs_0_.2, ...), custom_call_target="tpu_custom_call" | custom-call | tf_op jit(solution)/shard_map/fetch/pallas_call | solution.py:159
  6.1 6.4 %attention.1 = (bf16[16,1536]{1,0:T(8,128)(2,1)S(1)}, f32[16,1536]{1,0:T(8,128)S(1)}, bf16[16,1536]{1,0:T(8,128)(2,1)S(1)}, bf16[16,4096,128]{2,1,0:T(8,128)(2,1)S(1)}) custom-call(s32[16]{0:T(128)S(4)} %get-tuple-element.36.refs_0_, s32[144]{0:T(256)S(4)} %get-tuple-element.37.refs_1_, ...), custom_call_target="tpu_custom_call", output_to_operand_aliasing={{3}: (10, {})} | custom-call | tf_op jit(solution)/shard_map/attention/pallas_call | solution.py:341
  12.5 1.0 %collective-permute-start.1 = (bf16[16,1536]{1,0:T(8,128)(2,1)S(1)}, bf16[16,1536]{1,0:T(8,128)(2,1)S(1)}, u32[]{:S(2)}, u32[]{:S(2)}) collective-permute-start(bf16[16,1536]{1,0:T(8,128)(2,1)S(1)} %get-tuple-element.46), channel_id=1, source_target_pairs={{0,1},{1,0},{2,3},{3,2},{4,5},{5,4},{6,7},{7,6},{8,9},{9,8},{10,11... | collective-permute-start | bytes 147464 | tf_op jit(solution)/shard_map/ppermute | solution.py:37
  13.5 0.3 copy.15
  14.5 2.2 %collective-permute-done.1.refs_3_ = bf16[16,1536]{1,0:T(8,128)(2,1)S(1)} collective-permute-done((bf16[16,1536]{1,0:T(8,128)(2,1)S(1)}, bf16[16,1536]{1,0:T(8,128)(2,1)S(1)}, u32[]{:S(2)}, u32[]{:S(2)}) %collective-permute-start.1) | collective-permute-done | bytes 49184 | tf_op jit(solution)/shard_map/ppermute | solution.py:37
  16.7 0.1 expert_input.1
  16.8 4.4 %collective-permute-start.2 = (bf16[16,1664]{1,0:T(8,128)(2,1)S(1)}, bf16[16,1664]{1,0:T(8,128)(2,1)S(1)}, u32[]{:S(2)}, u32[]{:S(2)}) collective-permute-start(bf16[16,1664]{1,0:T(8,128)(2,1)S(1)} %bitcast.12), channel_id=1, source_target_pairs={{0,12},{2,14},{4,8},{6,10},{8,4},{10,6},{12,0},{14,2},{1,13},{3,15... | collective-permute-start | bytes 159752 | tf_op jit(solution)/shard_map/ppermute | solution.py:699
  21.2 0.6 %collective-permute-start.4 = (bf16[16,1664]{1,0:T(8,128)(2,1)S(1)}, bf16[16,1664]{1,0:T(8,128)(2,1)S(1)}, u32[]{:S(2)}, u32[]{:S(2)}) collective-permute-start(bf16[16,1664]{1,0:T(8,128)(2,1)S(1)} %bitcast.14), channel_id=1, source_target_pairs={{0,4},{2,6},{4,0},{6,2},{8,12},{10,14},{12,8},{14,10},{1,5},{3,7},... | collective-permute-start | bytes 159752 | tf_op jit(solution)/shard_map/ppermute | solution.py:699
  21.9 1.7 %collective-permute-done.2.refs_1_ = bf16[16,1664]{1,0:T(8,128)(2,1)S(1)} collective-permute-done((bf16[16,1664]{1,0:T(8,128)(2,1)S(1)}, bf16[16,1664]{1,0:T(8,128)(2,1)S(1)}, u32[]{:S(2)}, u32[]{:S(2)}) %collective-permute-start.2) | collective-permute-done | bytes 53280 | tf_op jit(solution)/shard_map/ppermute | solution.py:699
  23.6 2.7 %collective-permute-done.3.refs_2_ = bf16[16,1664]{1,0:T(8,128)(2,1)S(1)} collective-permute-done((bf16[16,1664]{1,0:T(8,128)(2,1)S(1)}, bf16[16,1664]{1,0:T(8,128)(2,1)S(1)}, u32[]{:S(2)}, u32[]{:S(2)}) %collective-permute-start.3) | collective-permute-done | bytes 53280 | tf_op jit(solution)/shard_map/ppermute | solution.py:699
  26.3 0.8 %collective-permute-start.7 = (bf16[48,1664]{1,0:T(8,128)(2,1)S(1)}, bf16[48,1664]{1,0:T(8,128)(2,1)S(1)}, u32[]{:S(2)}, u32[]{:S(2)}) collective-permute-start(bf16[48,1664]{1,0:T(8,128)(2,1)S(1)} %get-tuple-element.53), channel_id=1, source_target_pairs={{0,2},{2,0},{4,6},{6,4},{8,10},{10,8},{12,14},{14,12},{1,3},{3,1},... | collective-permute-start | bytes 479240 | tf_op jit(solution)/shard_map/ppermute | solution.py:37
  27.0 1.3 %collective-permute-start.6 = (bf16[16,1664]{1,0:T(8,128)(2,1)S(1)}, bf16[16,1664]{1,0:T(8,128)(2,1)S(1)}, u32[]{:S(2)}, u32[]{:S(2)}) collective-permute-start(bf16[16,1664]{1,0:T(8,128)(2,1)S(1)} %bitcast.16), channel_id=1, source_target_pairs={{0,2},{2,0},{4,6},{6,4},{8,10},{10,8},{12,14},{14,12},{1,3},{3,1},... | collective-permute-start | bytes 159752 | tf_op jit(solution)/shard_map/ppermute | solution.py:37
  28.4 3.8 %collective-permute-done.6.first = bf16[16,1664]{1,0:T(8,128)(2,1)S(1)} collective-permute-done((bf16[16,1664]{1,0:T(8,128)(2,1)S(1)}, bf16[16,1664]{1,0:T(8,128)(2,1)S(1)}, u32[]{:S(2)}, u32[]{:S(2)}) %collective-permute-start.6) | collective-permute-done | bytes 53280 | tf_op jit(solution)/shard_map/ppermute | solution.py:37
  32.2 0.1 collective-permute-start.10
  32.3 0.8 %home_expert.1 = (f32[64,1536]{1,0:T(8,128)S(1)}, bf16[64,1536]{1,0:T(8,128)(2,1)S(1)}, f32[64,1536]{1,0:T(8,128)S(1)}) custom-call(bf16[64,1664]{1,0:T(8,128)(2,1)S(1)} %get-tuple-element.50.refs_0_, bf16[64,1664]{1,0:T(8,128)(2,1)S(1)} %collective-permute-done.5.refs_1_, f32[16,768]{1,0:T(8,128)S(1)} %get-tuple-element.51.refs_2_, ...), custom_call_target="tpu_custom_call" | custom-call | flops 301989888 | bytes 4325376 | tf_op jit(solution)/shard_map/home_expert/pallas_call | solution.py:512
  33.2 0.5 %collective-permute-start.8 = (bf16[64,1536]{1,0:T(8,128)(2,1)S(1)}, bf16[64,1536]{1,0:T(8,128)(2,1)S(1)}, u32[]{:S(2)}, u32[]{:S(2)}) collective-permute-start(bf16[64,1536]{1,0:T(8,128)(2,1)S(1)} %get-tuple-element.55), channel_id=1, source_target_pairs={{0,16},{16,0},{1,17},{17,1},{2,18},{18,2},{3,19},{19,3},{4,20},{20... | collective-permute-start | bytes 589832 | tf_op jit(solution)/shard_map/ppermute | solution.py:37
  33.8 0.6 %other_expert.1 = (f32[64,1536]{1,0:T(8,128)S(1)}, bf16[64,1536]{1,0:T(8,128)(2,1)S(1)}) custom-call(bf16[64,1664]{1,0:T(8,128)(2,1)S(1)} %joined.1.refs_5_.x_own, bf16[64,1664]{1,0:T(8,128)(2,1)S(1)} %collective-permute-done.10.x_other, f32[64,1536]{1,0:T(8,128)S(1)} %get-tuple-element.58.y_own, bf16[1536,512]{1,0:T(8,128)(2,1)S(1)} %bitcast.9, ...), custom_call_target="tpu_custom_call" | custom-call | flops 150994944 | bytes 3342336 | tf_op jit(solution)/shard_map/other_expert/pallas_call | solution.py:534
  34.4 0.2 collective-permute-start.11
  34.6 0.2 collective-permute-done.8.recv
  34.8 1.2 %collective-permute-start.9 = (bf16[64,768]{1,0:T(8,128)(2,1)S(1)}, bf16[64,768]{1,0:T(8,128)(2,1)S(1)}, u32[]{:S(2)}, u32[]{:S(2)}) collective-permute-start(bf16[64,768]{1,0:T(8,128)(2,1)S(1)} %get-tuple-element.57), channel_id=1, source_target_pairs={{0,1},{1,0},{2,3},{3,2},{4,5},{5,4},{6,7},{7,6},{8,9},{9,8},{10,11... | collective-permute-start | bytes 294920 | tf_op jit(solution)/shard_map/ppermute | solution.py:37
  36.1 0.6 %collective-permute-start.12 = (bf16[64,768]{1,0:T(8,128)(2,1)S(1)}, bf16[64,768]{1,0:T(8,128)(2,1)S(1)}, u32[]{:S(2)}, u32[]{:S(2)}) collective-permute-start(bf16[64,768]{1,0:T(8,128)(2,1)S(1)} %get-tuple-element.61), channel_id=1, source_target_pairs={{0,2},{2,0},{4,6},{6,4},{8,10},{10,8},{12,14},{14,12},{1,3},{3,1},... | collective-permute-start | bytes 294920 | tf_op jit(solution)/shard_map/ppermute | solution.py:37
  36.7 1.9 %collective-permute-start.13 = (bf16[64,768]{1,0:T(8,128)(2,1)S(1)}, bf16[64,768]{1,0:T(8,128)(2,1)S(1)}, u32[]{:S(2)}, u32[]{:S(2)}) collective-permute-start(bf16[64,768]{1,0:T(8,128)(2,1)S(1)} %get-tuple-element.62), channel_id=1, source_target_pairs={{0,3},{1,2},{2,1},{3,0},{4,7},{5,6},{6,5},{7,4},{8,11},{9,10},{10,... | collective-permute-start | bytes 294920 | tf_op jit(solution)/shard_map/ppermute | solution.py:716
  38.6 1.3 %collective-permute-done.9.refs_0_ = bf16[64,768]{1,0:T(8,128)(2,1)S(1)} collective-permute-done((bf16[64,768]{1,0:T(8,128)(2,1)S(1)}, bf16[64,768]{1,0:T(8,128)(2,1)S(1)}, u32[]{:S(2)}, u32[]{:S(2)}) %collective-permute-start.9) | collective-permute-done | bytes 98336 | tf_op jit(solution)/shard_map/ppermute | solution.py:37
  40.0 3.1 %collective-permute-done.12.refs_1_ = bf16[64,768]{1,0:T(8,128)(2,1)S(1)} collective-permute-done((bf16[64,768]{1,0:T(8,128)(2,1)S(1)}, bf16[64,768]{1,0:T(8,128)(2,1)S(1)}, u32[]{:S(2)}, u32[]{:S(2)}) %collective-permute-start.12) | collective-permute-done | bytes 98336 | tf_op jit(solution)/shard_map/ppermute | solution.py:37
  43.1 1.5 %collective-permute-start.14 = (bf16[16,768]{1,0:T(8,128)(2,1)S(1)}, bf16[16,768]{1,0:T(8,128)(2,1)S(1)}, u32[]{:S(2)}, u32[]{:S(2)}) collective-permute-start(bf16[16,768]{1,0:T(8,128)(2,1)S(1)} %get-tuple-element.64), channel_id=1, source_target_pairs={{0,12},{2,14},{4,8},{6,10},{8,4},{10,6},{12,0},{14,2},{1,13},{3,15... | collective-permute-start | bytes 73736 | tf_op jit(solution)/shard_map/ppermute | solution.py:718
  44.7 0.6 %collective-permute-start.15 = (bf16[16,768]{1,0:T(8,128)(2,1)S(1)}, bf16[16,768]{1,0:T(8,128)(2,1)S(1)}, u32[]{:S(2)}, u32[]{:S(2)}) collective-permute-start(bf16[16,768]{1,0:T(8,128)(2,1)S(1)} %get-tuple-element.65), channel_id=1, source_target_pairs={{0,8},{2,10},{4,12},{6,14},{8,0},{10,2},{12,4},{14,6},{1,9},{3,11}... | collective-permute-start | bytes 73736 | tf_op jit(solution)/shard_map/ppermute | solution.py:718
  45.3 2.3 %collective-permute-start.16 = (bf16[16,768]{1,0:T(8,128)(2,1)S(1)}, bf16[16,768]{1,0:T(8,128)(2,1)S(1)}, u32[]{:S(2)}, u32[]{:S(2)}) collective-permute-start(bf16[16,768]{1,0:T(8,128)(2,1)S(1)} %get-tuple-element.66), channel_id=1, source_target_pairs={{0,4},{2,6},{4,0},{6,2},{8,12},{10,14},{12,8},{14,10},{1,5},{3,7},... | collective-permute-start | bytes 73736 | tf_op jit(solution)/shard_map/ppermute | solution.py:718
  47.6 1.2 %collective-permute-done.14.refs_1_ = bf16[16,768]{1,0:T(8,128)(2,1)S(1)} collective-permute-done((bf16[16,768]{1,0:T(8,128)(2,1)S(1)}, bf16[16,768]{1,0:T(8,128)(2,1)S(1)}, u32[]{:S(2)}, u32[]{:S(2)}) %collective-permute-start.14) | collective-permute-done | bytes 24608 | tf_op jit(solution)/shard_map/ppermute | solution.py:718
  48.8 0.6 %collective-permute-done.15.refs_2_ = bf16[16,768]{1,0:T(8,128)(2,1)S(1)} collective-permute-done((bf16[16,768]{1,0:T(8,128)(2,1)S(1)}, bf16[16,768]{1,0:T(8,128)(2,1)S(1)}, u32[]{:S(2)}, u32[]{:S(2)}) %collective-permute-start.15) | collective-permute-done | bytes 24608 | tf_op jit(solution)/shard_map/ppermute | solution.py:718
  49.4 0.2 collective-permute-done.16.refs_3_
  49.7 0.6 %line_sum.1 = bf16[16,768]{1,0:T(8,128)(2,1)} custom-call(f32[16,768]{1,0:T(8,128)S(1)} %get-tuple-element.63.refs_0_, bf16[16,768]{1,0:T(8,128)(2,1)S(1)} %collective-permute-done.14.refs_1_, bf16[16,768]{1,0:T(8,128)(2,1)S(1)} %collective-permute-done.15.refs_2_, bf16[16,768]{1,0:T(8,128)(2,1)S(1)} %collective-permute-done.16.refs_3_), custom_call_target="tpu_custom_call" | custom-call | tf_op jit(solution)/shard_map/line_sum/pallas_call | solution.py:620
  (24 shorter events, 0.3 us)
Async XLA Ops:
  0.0 6.0 %collective-permute-start = (bf16[16,768]{1,0:T(8,128)(2,1)}, bf16[16,768]{1,0:T(8,128)(2,1)S(1)}, u32[]{:S(2)}, u32[]{:S(2)}) collective-permute-start(bf16[16,768]{1,0:T(8,128)(2,1)} %refs_4_.2), channel_id=1, source_target_pairs={{0,1},{1,0},{2,3},{3,2},{4,5},{5,4},{6,7},{7,6},{8,9},{9,8},{10,11... | collective-permute-start | bytes 73736 | tf_op jit(solution)/shard_map/ppermute | solution.py:37
  2.9 3.1 %copy-start.1 = (bf16[1536,768]{1,0:T(8,128)(2,1)S(1)}, bf16[1536,768]{1,0:T(8,128)(2,1)}, u32[]{:S(2)}) copy-start(bf16[1536,768]{1,0:T(8,128)(2,1)} %refs_8_.1) | copy-start | bytes 7077892
  2.9 3.1 %copy-start.2 = (bf16[1536,512]{1,0:T(8,128)(2,1)S(1)}, bf16[1536,512]{1,0:T(8,128)(2,1)}, u32[]{:S(2)}) copy-start(bf16[1536,512]{1,0:T(8,128)(2,1)} %refs_9_.1) | copy-start | bytes 4718596
  6.1 7.4 %copy-start.4 = (bf16[1,1536,2,256]{3,2,1,0:T(2,128)(2,1)S(1)}, bf16[1,1536,2,256]{3,2,1,0:T(2,128)(2,1)}, u32[]{:S(2)}) copy-start(bf16[1,1536,2,256]{3,2,1,0:T(2,128)(2,1)} %param.22) | copy-start | bytes 4718596
  12.5 4.2 %copy-start.3 = (f32[1536]{0:T(1024)S(1)}, f32[1536]{0:T(1024)}, u32[]{:S(2)}) copy-start(f32[1536]{0:T(1024)} %refs_4_.3) | copy-start | bytes 18436
  12.5 19.8 %copy-start = (bf16[1,256,1536]{2,1,0:T(8,128)(2,1)S(1)}, bf16[1,256,1536]{2,1,0:T(8,128)(2,1)}, u32[]{:S(2)}) copy-start(bf16[1,256,1536]{2,1,0:T(8,128)(2,1)} %param.23) | copy-start | bytes 2359300
  12.5 4.2 %collective-permute-start.1 = (bf16[16,1536]{1,0:T(8,128)(2,1)S(1)}, bf16[16,1536]{1,0:T(8,128)(2,1)S(1)}, u32[]{:S(2)}, u32[]{:S(2)}) collective-permute-start(bf16[16,1536]{1,0:T(8,128)(2,1)S(1)} %get-tuple-element.46), channel_id=1, source_target_pairs={{0,1},{1,0},{2,3},{3,2},{4,5},{5,4},{6,7},{7,6},{8,9},{9,8},{10,11... | collective-permute-start | bytes 147464 | tf_op jit(solution)/shard_map/ppermute | solution.py:37
  16.8 6.7 %collective-permute-start.2 = (bf16[16,1664]{1,0:T(8,128)(2,1)S(1)}, bf16[16,1664]{1,0:T(8,128)(2,1)S(1)}, u32[]{:S(2)}, u32[]{:S(2)}) collective-permute-start(bf16[16,1664]{1,0:T(8,128)(2,1)S(1)} %bitcast.12), channel_id=1, source_target_pairs={{0,12},{2,14},{4,8},{6,10},{8,4},{10,6},{12,0},{14,2},{1,13},{3,15... | collective-permute-start | bytes 159752 | tf_op jit(solution)/shard_map/ppermute | solution.py:699
  21.2 5.0 %collective-permute-start.3 = (bf16[16,1664]{1,0:T(8,128)(2,1)S(1)}, bf16[16,1664]{1,0:T(8,128)(2,1)S(1)}, u32[]{:S(2)}, u32[]{:S(2)}) collective-permute-start(bf16[16,1664]{1,0:T(8,128)(2,1)S(1)} %bitcast.13), channel_id=1, source_target_pairs={{0,8},{2,10},{4,12},{6,14},{8,0},{10,2},{12,4},{14,6},{1,9},{3,11}... | collective-permute-start | bytes 159752 | tf_op jit(solution)/shard_map/ppermute | solution.py:699
  21.2 5.0 %collective-permute-start.4 = (bf16[16,1664]{1,0:T(8,128)(2,1)S(1)}, bf16[16,1664]{1,0:T(8,128)(2,1)S(1)}, u32[]{:S(2)}, u32[]{:S(2)}) collective-permute-start(bf16[16,1664]{1,0:T(8,128)(2,1)S(1)} %bitcast.14), channel_id=1, source_target_pairs={{0,4},{2,6},{4,0},{6,2},{8,12},{10,14},{12,8},{14,10},{1,5},{3,7},... | collective-permute-start | bytes 159752 | tf_op jit(solution)/shard_map/ppermute | solution.py:699
  26.3 5.9 %collective-permute-start.7 = (bf16[48,1664]{1,0:T(8,128)(2,1)S(1)}, bf16[48,1664]{1,0:T(8,128)(2,1)S(1)}, u32[]{:S(2)}, u32[]{:S(2)}) collective-permute-start(bf16[48,1664]{1,0:T(8,128)(2,1)S(1)} %get-tuple-element.53), channel_id=1, source_target_pairs={{0,2},{2,0},{4,6},{6,4},{8,10},{10,8},{12,14},{14,12},{1,3},{3,1},... | collective-permute-start | bytes 479240 | tf_op jit(solution)/shard_map/ppermute | solution.py:37
  27.0 5.2 %collective-permute-start.6 = (bf16[16,1664]{1,0:T(8,128)(2,1)S(1)}, bf16[16,1664]{1,0:T(8,128)(2,1)S(1)}, u32[]{:S(2)}, u32[]{:S(2)}) collective-permute-start(bf16[16,1664]{1,0:T(8,128)(2,1)S(1)} %bitcast.16), channel_id=1, source_target_pairs={{0,2},{2,0},{4,6},{6,4},{8,10},{10,8},{12,14},{14,12},{1,3},{3,1},... | collective-permute-start | bytes 159752 | tf_op jit(solution)/shard_map/ppermute | solution.py:37
  28.4 3.9 %collective-permute-start.5 = (bf16[64,1664]{1,0:T(8,128)(2,1)S(1)}, bf16[64,1664]{1,0:T(8,128)(2,1)S(1)}, u32[]{:S(2)}, u32[]{:S(2)}) collective-permute-start(bf16[64,1664]{1,0:T(8,128)(2,1)S(1)} %get-tuple-element.50.refs_0_), channel_id=1, source_target_pairs={{0,16},{16,0},{1,17},{17,1},{2,18},{18,2},{3,19},{19,3},{4,20},{20... | collective-permute-start | bytes 638984 | tf_op jit(solution)/shard_map/ppermute | solution.py:37
  32.2 1.5 %collective-permute-start.10 = (bf16[64,1664]{1,0:T(8,128)(2,1)S(1)}, bf16[64,1664]{1,0:T(8,128)(2,1)S(1)}, u32[]{:S(2)}, u32[]{:S(2)}) collective-permute-start(bf16[64,1664]{1,0:T(8,128)(2,1)S(1)} %joined.1.refs_5_.x_own), channel_id=1, source_target_pairs={{0,16},{16,0},{1,17},{17,1},{2,18},{18,2},{3,19},{19,3},{4,20},{20... | collective-permute-start | bytes 638984 | tf_op jit(solution)/shard_map/ppermute | solution.py:37
  33.2 1.6 %collective-permute-start.8 = (bf16[64,1536]{1,0:T(8,128)(2,1)S(1)}, bf16[64,1536]{1,0:T(8,128)(2,1)S(1)}, u32[]{:S(2)}, u32[]{:S(2)}) collective-permute-start(bf16[64,1536]{1,0:T(8,128)(2,1)S(1)} %get-tuple-element.55), channel_id=1, source_target_pairs={{0,16},{16,0},{1,17},{17,1},{2,18},{18,2},{3,19},{19,3},{4,20},{20... | collective-permute-start | bytes 589832 | tf_op jit(solution)/shard_map/ppermute | solution.py:37
  34.4 1.7 %collective-permute-start.11 = (bf16[64,1536]{1,0:T(8,128)(2,1)S(1)}, bf16[64,1536]{1,0:T(8,128)(2,1)S(1)}, u32[]{:S(2)}, u32[]{:S(2)}) collective-permute-start(bf16[64,1536]{1,0:T(8,128)(2,1)S(1)} %get-tuple-element.60), channel_id=1, source_target_pairs={{0,16},{16,0},{1,17},{17,1},{2,18},{18,2},{3,19},{19,3},{4,20},{20... | collective-permute-start | bytes 589832 | tf_op jit(solution)/shard_map/ppermute | solution.py:37
  34.8 5.1 %collective-permute-start.9 = (bf16[64,768]{1,0:T(8,128)(2,1)S(1)}, bf16[64,768]{1,0:T(8,128)(2,1)S(1)}, u32[]{:S(2)}, u32[]{:S(2)}) collective-permute-start(bf16[64,768]{1,0:T(8,128)(2,1)S(1)} %get-tuple-element.57), channel_id=1, source_target_pairs={{0,1},{1,0},{2,3},{3,2},{4,5},{5,4},{6,7},{7,6},{8,9},{9,8},{10,11... | collective-permute-start | bytes 294920 | tf_op jit(solution)/shard_map/ppermute | solution.py:37
  36.1 6.9 %collective-permute-start.12 = (bf16[64,768]{1,0:T(8,128)(2,1)S(1)}, bf16[64,768]{1,0:T(8,128)(2,1)S(1)}, u32[]{:S(2)}, u32[]{:S(2)}) collective-permute-start(bf16[64,768]{1,0:T(8,128)(2,1)S(1)} %get-tuple-element.61), channel_id=1, source_target_pairs={{0,2},{2,0},{4,6},{6,4},{8,10},{10,8},{12,14},{14,12},{1,3},{3,1},... | collective-permute-start | bytes 294920 | tf_op jit(solution)/shard_map/ppermute | solution.py:37
  36.7 6.4 %collective-permute-start.13 = (bf16[64,768]{1,0:T(8,128)(2,1)S(1)}, bf16[64,768]{1,0:T(8,128)(2,1)S(1)}, u32[]{:S(2)}, u32[]{:S(2)}) collective-permute-start(bf16[64,768]{1,0:T(8,128)(2,1)S(1)} %get-tuple-element.62), channel_id=1, source_target_pairs={{0,3},{1,2},{2,1},{3,0},{4,7},{5,6},{6,5},{7,4},{8,11},{9,10},{10,... | collective-permute-start | bytes 294920 | tf_op jit(solution)/shard_map/ppermute | solution.py:716
  43.1 5.7 %collective-permute-start.14 = (bf16[16,768]{1,0:T(8,128)(2,1)S(1)}, bf16[16,768]{1,0:T(8,128)(2,1)S(1)}, u32[]{:S(2)}, u32[]{:S(2)}) collective-permute-start(bf16[16,768]{1,0:T(8,128)(2,1)S(1)} %get-tuple-element.64), channel_id=1, source_target_pairs={{0,12},{2,14},{4,8},{6,10},{8,4},{10,6},{12,0},{14,2},{1,13},{3,15... | collective-permute-start | bytes 73736 | tf_op jit(solution)/shard_map/ppermute | solution.py:718
  44.7 4.8 %collective-permute-start.15 = (bf16[16,768]{1,0:T(8,128)(2,1)S(1)}, bf16[16,768]{1,0:T(8,128)(2,1)S(1)}, u32[]{:S(2)}, u32[]{:S(2)}) collective-permute-start(bf16[16,768]{1,0:T(8,128)(2,1)S(1)} %get-tuple-element.65), channel_id=1, source_target_pairs={{0,8},{2,10},{4,12},{6,14},{8,0},{10,2},{12,4},{14,6},{1,9},{3,11}... | collective-permute-start | bytes 73736 | tf_op jit(solution)/shard_map/ppermute | solution.py:718
  45.3 4.4 %collective-permute-start.16 = (bf16[16,768]{1,0:T(8,128)(2,1)S(1)}, bf16[16,768]{1,0:T(8,128)(2,1)S(1)}, u32[]{:S(2)}, u32[]{:S(2)}) collective-permute-start(bf16[16,768]{1,0:T(8,128)(2,1)S(1)} %get-tuple-element.66), channel_id=1, source_target_pairs={{0,4},{2,6},{4,0},{6,2},{8,12},{10,14},{12,8},{14,10},{1,5},{3,7},... | collective-permute-start | bytes 73736 | tf_op jit(solution)/shard_map/ppermute | solution.py:718

commit v7 on v6

--- a/solution.py
+++ b/solution.py
@@ -285,8 +285,6 @@
         last = jnp.minimum(items[b * UNROLL + UNROLL - 1] // per, rows - 1) + 1
         last = jnp.where(b * UNROLL + UNROLL <= rows, 0, last)
         lax.fori_loop(ready, last, arrive, 0)
-        earlier = jnp.maximum(b - 1, 0) * UNROLL
-        merge(b * UNROLL, lambda u: jnp.where(b == 0, rows, items[earlier + u] // per))
         got = [chunk(b * UNROLL + u) for u in range(UNROLL)]
         dots = [
             lax.dot_general(qb[r], kv, (((1,), (1,)), ((), ())), preferred_element_type=f32) for r, c, kv in got
@@ -299,6 +297,8 @@
             top = jnp.max(folded(jnp.maximum, s), axis=-1, keepdims=True)
             tops.append(jnp.broadcast_to(top, (QROWS, LANES)))
             probs.append(jnp.exp(s - top))
+        earlier = jnp.maximum(b - 1, 0) * UNROLL
+        merge(b * UNROLL, lambda u: jnp.where(b == 0, rows, items[earlier + u] // per))
         for u, p in enumerate(probs):
             i = (b + 1) * UNROLL + u
             mixes[i] = jnp.dot(p.astype(bf16), got[u][2], preferred_element_type=f32)

time: 50.5 us -> 50.6 us (level)
    ppermute x10, starting transfers between devices: 8.62 us -> 10.7 us  [swapped(): lax.ppermute(value, axis, [(i, i ^ 1) for i in range(lax.axis_size(axis))])]
    ppermute x1, starting transfers between devices: 1.91 us -> 0.82 us  [shards(): from_corner = lax.ppermute(away_cross, ('req', 'tp'), corner)]
    ppermute x1, waiting for transfers between devices: 0.01 us -> 1.06 us  [shards(): from_corner = lax.ppermute(away_cross, ('req', 'tp'), corner)]
    ppermute x3, waiting for transfers between devices: 4.39 us -> 3.66 us  [shards(): beside = [lax.ppermute(payload, 'req', step) for step in steps]]
    ppermute x3, starting transfers between devices: 5.03 us -> 4.45 us  [shards(): beside = [lax.ppermute(payload, 'req', step) for step in steps]]
    ppermute x10, waiting for transfers between devices: 10.8 us -> 10.2 us  [swapped(): lax.ppermute(value, axis, [(i, i ^ 1) for i in range(lax.axis_size(axis))])]
  transfers between devices with their start and end apart: 17 -> 17, of which waited for: 10 -> 13; matrix products, arithmetic and copies ran while one was open for 1% -> 1% of each run, Pallas kernels for 9% -> 9%
where the time goes in v7:
time: 50.6 us; the launch traced here: 50.5 us
  starting transfers between devices  20.4 us (40%)
  waiting for transfers between devices  17 us (34%)
  Pallas kernels  11.9 us (24%)
  between operations  0.79 us (2%)
    ppermute x10, starting transfers between devices, swapped(): lax.ppermute(value, axis, [(i, i ^ 1) for i in range(lax.axis_size(axis))])  10.7 us
    ppermute x10, waiting for transfers between devices, swapped(): lax.ppermute(value, axis, [(i, i ^ 1) for i in range(lax.axis_size(axis))])  10.2 us
    pallas_call x1, Pallas kernels, attention(): pl.pallas_call(lambda *refs: attention_kernel(len(parts), *refs), out_sha...  6.42 us
    ppermute x3, starting transfers between devices, shards(): beside = [lax.ppermute(payload, 'req', step) for step in steps]  4.45 us
    ppermute x3, starting transfers between devices, shards(): lax.ppermute(other, 'req', step)  4.45 us
    ppermute x3, waiting for transfers between devices, shards(): beside = [lax.ppermute(payload, 'req', step) for step in steps]  3.66 us
    pallas_call x1, Pallas kernels, fetch(): pl.pallas_call(lambda *refs: fetch_kernel(wide, per, *refs), out_shape=tu...  3.09 us
    ppermute x3, waiting for transfers between devices, shards(): lax.ppermute(other, 'req', step)  2.07 us
  transfers between devices with their start and end apart: 17, of which 13 were waited for; matrix products, arithmetic and copies ran while one was open for 1% of the time, Pallas kernels for 9%

profile of v7, /device:TPU:0, one launch (start us, length us, event | category | flops | bytes accessed | tf_op | source)
XLA Modules:
  0.0 50.5 jit_solution(4440714871783304289)
XLA Ops:
  0.0 2.9 %collective-permute-start = (bf16[16,768]{1,0:T(8,128)(2,1)}, bf16[16,768]{1,0:T(8,128)(2,1)S(1)}, u32[]{:S(2)}, u32[]{:S(2)}) collective-permute-start(bf16[16,768]{1,0:T(8,128)(2,1)} %refs_4_.2), channel_id=1, source_target_pairs={{0,1},{1,0},{2,3},{3,2},{4,5},{5,4},{6,7},{7,6},{8,9},{9,8},{10,11... | collective-permute-start | bytes 73736 | tf_op jit(solution)/shard_map/ppermute | solution.py:37
  2.9 3.1 %fetch.1 = (bf16[16,768]{1,0:T(8,128)(2,1)S(1)}, f32[1536]{0:T(1024)S(1)}, f32[16,128]{1,0:T(8,128)S(1)}, f32[16,128]{1,0:T(8,128)S(1)}, bf16[16,128]{1,0:T(8,12...) custom-call(s32[2,16]{1,0:T(2,128)} %refs_0_.2, ...), custom_call_target="tpu_custom_call" | custom-call | tf_op jit(solution)/shard_map/fetch/pallas_call | solution.py:159
  6.1 6.4 %attention.1 = (bf16[16,1536]{1,0:T(8,128)(2,1)S(1)}, f32[16,1536]{1,0:T(8,128)S(1)}, bf16[16,1536]{1,0:T(8,128)(2,1)S(1)}, bf16[16,4096,128]{2,1,0:T(8,128)(2,1)S(1)}) custom-call(s32[16]{0:T(128)S(4)} %get-tuple-element.36.refs_0_, s32[144]{0:T(256)S(4)} %get-tuple-element.37.refs_1_, ...), custom_call_target="tpu_custom_call", output_to_operand_aliasing={{3}: (10, {})} | custom-call | tf_op jit(solution)/shard_map/attention/pallas_call | solution.py:341
  12.5 1.0 %collective-permute-start.1 = (bf16[16,1536]{1,0:T(8,128)(2,1)S(1)}, bf16[16,1536]{1,0:T(8,128)(2,1)S(1)}, u32[]{:S(2)}, u32[]{:S(2)}) collective-permute-start(bf16[16,1536]{1,0:T(8,128)(2,1)S(1)} %get-tuple-element.46), channel_id=1, source_target_pairs={{0,1},{1,0},{2,3},{3,2},{4,5},{5,4},{6,7},{7,6},{8,9},{9,8},{10,11... | collective-permute-start | bytes 147464 | tf_op jit(solution)/shard_map/ppermute | solution.py:37
  13.5 0.3 copy.15
  14.5 2.2 %collective-permute-done.1.refs_3_ = bf16[16,1536]{1,0:T(8,128)(2,1)S(1)} collective-permute-done((bf16[16,1536]{1,0:T(8,128)(2,1)S(1)}, bf16[16,1536]{1,0:T(8,128)(2,1)S(1)}, u32[]{:S(2)}, u32[]{:S(2)}) %collective-permute-start.1) | collective-permute-done | bytes 49184 | tf_op jit(solution)/shard_map/ppermute | solution.py:37
  16.8 2.5 %collective-permute-start.2 = (bf16[16,1664]{1,0:T(8,128)(2,1)S(1)}, bf16[16,1664]{1,0:T(8,128)(2,1)S(1)}, u32[]{:S(2)}, u32[]{:S(2)}) collective-permute-start(bf16[16,1664]{1,0:T(8,128)(2,1)S(1)} %bitcast.12), channel_id=1, source_target_pairs={{0,12},{2,14},{4,8},{6,10},{8,4},{10,6},{12,0},{14,2},{1,13},{3,15... | collective-permute-start | bytes 159752 | tf_op jit(solution)/shard_map/ppermute | solution.py:699
  19.3 1.2 %collective-permute-start.3 = (bf16[16,1664]{1,0:T(8,128)(2,1)S(1)}, bf16[16,1664]{1,0:T(8,128)(2,1)S(1)}, u32[]{:S(2)}, u32[]{:S(2)}) collective-permute-start(bf16[16,1664]{1,0:T(8,128)(2,1)S(1)} %bitcast.13), channel_id=1, source_target_pairs={{0,8},{2,10},{4,12},{6,14},{8,0},{10,2},{12,4},{14,6},{1,9},{3,11}... | collective-permute-start | bytes 159752 | tf_op jit(solution)/shard_map/ppermute | solution.py:699
  20.6 0.7 %collective-permute-start.4 = (bf16[16,1664]{1,0:T(8,128)(2,1)S(1)}, bf16[16,1664]{1,0:T(8,128)(2,1)S(1)}, u32[]{:S(2)}, u32[]{:S(2)}) collective-permute-start(bf16[16,1664]{1,0:T(8,128)(2,1)S(1)} %bitcast.14), channel_id=1, source_target_pairs={{0,4},{2,6},{4,0},{6,2},{8,12},{10,14},{12,8},{14,10},{1,5},{3,7},... | collective-permute-start | bytes 159752 | tf_op jit(solution)/shard_map/ppermute | solution.py:699
  21.3 1.6 %collective-permute-done.2.refs_1_ = bf16[16,1664]{1,0:T(8,128)(2,1)S(1)} collective-permute-done((bf16[16,1664]{1,0:T(8,128)(2,1)S(1)}, bf16[16,1664]{1,0:T(8,128)(2,1)S(1)}, u32[]{:S(2)}, u32[]{:S(2)}) %collective-permute-start.2) | collective-permute-done | bytes 53280 | tf_op jit(solution)/shard_map/ppermute | solution.py:699
  22.9 1.5 %collective-permute-done.3.refs_2_ = bf16[16,1664]{1,0:T(8,128)(2,1)S(1)} collective-permute-done((bf16[16,1664]{1,0:T(8,128)(2,1)S(1)}, bf16[16,1664]{1,0:T(8,128)(2,1)S(1)}, u32[]{:S(2)}, u32[]{:S(2)}) %collective-permute-start.3) | collective-permute-done | bytes 53280 | tf_op jit(solution)/shard_map/ppermute | solution.py:699
  24.4 0.5 %collective-permute-done.4.refs_3_ = bf16[16,1664]{1,0:T(8,128)(2,1)S(1)} collective-permute-done((bf16[16,1664]{1,0:T(8,128)(2,1)S(1)}, bf16[16,1664]{1,0:T(8,128)(2,1)S(1)}, u32[]{:S(2)}, u32[]{:S(2)}) %collective-permute-start.4) | collective-permute-done | bytes 53280 | tf_op jit(solution)/shard_map/ppermute | solution.py:699
  25.0 3.2 %collective-permute-start.7 = (bf16[48,1664]{1,0:T(8,128)(2,1)S(1)}, bf16[48,1664]{1,0:T(8,128)(2,1)S(1)}, u32[]{:S(2)}, u32[]{:S(2)}) collective-permute-start(bf16[48,1664]{1,0:T(8,128)(2,1)S(1)} %get-tuple-element.53), channel_id=1, source_target_pairs={{0,2},{2,0},{4,6},{6,4},{8,10},{10,8},{12,14},{14,12},{1,3},{3,1},... | collective-permute-start | bytes 479240 | tf_op jit(solution)/shard_map/ppermute | solution.py:37
  28.2 4.1 %collective-permute-done.6.first = bf16[16,1664]{1,0:T(8,128)(2,1)S(1)} collective-permute-done((bf16[16,1664]{1,0:T(8,128)(2,1)S(1)}, bf16[16,1664]{1,0:T(8,128)(2,1)S(1)}, u32[]{:S(2)}, u32[]{:S(2)}) %collective-permute-start.6) | collective-permute-done | bytes 53280 | tf_op jit(solution)/shard_map/ppermute | solution.py:37
  32.4 0.8 %home_expert.1 = (f32[64,1536]{1,0:T(8,128)S(1)}, bf16[64,1536]{1,0:T(8,128)(2,1)S(1)}, f32[64,1536]{1,0:T(8,128)S(1)}) custom-call(bf16[64,1664]{1,0:T(8,128)(2,1)S(1)} %get-tuple-element.50.refs_0_, bf16[64,1664]{1,0:T(8,128)(2,1)S(1)} %collective-permute-done.5.refs_1_, f32[16,768]{1,0:T(8,128)S(1)} %get-tuple-element.51.refs_2_, ...), custom_call_target="tpu_custom_call" | custom-call | flops 301989888 | bytes 4325376 | tf_op jit(solution)/shard_map/home_expert/pallas_call | solution.py:512
  33.3 0.5 %collective-permute-start.8 = (bf16[64,1536]{1,0:T(8,128)(2,1)S(1)}, bf16[64,1536]{1,0:T(8,128)(2,1)S(1)}, u32[]{:S(2)}, u32[]{:S(2)}) collective-permute-start(bf16[64,1536]{1,0:T(8,128)(2,1)S(1)} %get-tuple-element.55), channel_id=1, source_target_pairs={{0,16},{16,0},{1,17},{17,1},{2,18},{18,2},{3,19},{19,3},{4,20},{20... | collective-permute-start | bytes 589832 | tf_op jit(solution)/shard_map/ppermute | solution.py:37
  33.8 0.6 %other_expert.1 = (f32[64,1536]{1,0:T(8,128)S(1)}, bf16[64,1536]{1,0:T(8,128)(2,1)S(1)}) custom-call(bf16[64,1664]{1,0:T(8,128)(2,1)S(1)} %joined.1.refs_5_.x_own, bf16[64,1664]{1,0:T(8,128)(2,1)S(1)} %collective-permute-done.10.x_other, f32[64,1536]{1,0:T(8,128)S(1)} %get-tuple-element.58.y_own, bf16[1536,512]{1,0:T(8,128)(2,1)S(1)} %bitcast.9, ...), custom_call_target="tpu_custom_call" | custom-call | flops 150994944 | bytes 3342336 | tf_op jit(solution)/shard_map/other_expert/pallas_call | solution.py:534
  34.5 0.2 collective-permute-start.11
  34.7 0.2 collective-permute-done.8.recv
  34.9 1.0 %collective-permute-start.9 = (bf16[64,768]{1,0:T(8,128)(2,1)S(1)}, bf16[64,768]{1,0:T(8,128)(2,1)S(1)}, u32[]{:S(2)}, u32[]{:S(2)}) collective-permute-start(bf16[64,768]{1,0:T(8,128)(2,1)S(1)} %get-tuple-element.57), channel_id=1, source_target_pairs={{0,1},{1,0},{2,3},{3,2},{4,5},{5,4},{6,7},{7,6},{8,9},{9,8},{10,11... | collective-permute-start | bytes 294920 | tf_op jit(solution)/shard_map/ppermute | solution.py:37
  36.0 1.8 %collective-permute-start.12 = (bf16[64,768]{1,0:T(8,128)(2,1)S(1)}, bf16[64,768]{1,0:T(8,128)(2,1)S(1)}, u32[]{:S(2)}, u32[]{:S(2)}) collective-permute-start(bf16[64,768]{1,0:T(8,128)(2,1)S(1)} %get-tuple-element.61), channel_id=1, source_target_pairs={{0,2},{2,0},{4,6},{6,4},{8,10},{10,8},{12,14},{14,12},{1,3},{3,1},... | collective-permute-start | bytes 294920 | tf_op jit(solution)/shard_map/ppermute | solution.py:37
  37.8 0.8 %collective-permute-start.13 = (bf16[64,768]{1,0:T(8,128)(2,1)S(1)}, bf16[64,768]{1,0:T(8,128)(2,1)S(1)}, u32[]{:S(2)}, u32[]{:S(2)}) collective-permute-start(bf16[64,768]{1,0:T(8,128)(2,1)S(1)} %get-tuple-element.62), channel_id=1, source_target_pairs={{0,3},{1,2},{2,1},{3,0},{4,7},{5,6},{6,5},{7,4},{8,11},{9,10},{10,... | collective-permute-start | bytes 294920 | tf_op jit(solution)/shard_map/ppermute | solution.py:716
  38.6 1.4 %collective-permute-done.9.refs_0_ = bf16[64,768]{1,0:T(8,128)(2,1)S(1)} collective-permute-done((bf16[64,768]{1,0:T(8,128)(2,1)S(1)}, bf16[64,768]{1,0:T(8,128)(2,1)S(1)}, u32[]{:S(2)}, u32[]{:S(2)}) %collective-permute-start.9) | collective-permute-done | bytes 98336 | tf_op jit(solution)/shard_map/ppermute | solution.py:37
  40.1 2.2 %collective-permute-done.12.refs_1_ = bf16[64,768]{1,0:T(8,128)(2,1)S(1)} collective-permute-done((bf16[64,768]{1,0:T(8,128)(2,1)S(1)}, bf16[64,768]{1,0:T(8,128)(2,1)S(1)}, u32[]{:S(2)}, u32[]{:S(2)}) %collective-permute-start.12) | collective-permute-done | bytes 98336 | tf_op jit(solution)/shard_map/ppermute | solution.py:37
  42.3 1.1 %collective-permute-done.13.refs_2_ = bf16[64,768]{1,0:T(8,128)(2,1)S(1)} collective-permute-done((bf16[64,768]{1,0:T(8,128)(2,1)S(1)}, bf16[64,768]{1,0:T(8,128)(2,1)S(1)}, u32[]{:S(2)}, u32[]{:S(2)}) %collective-permute-start.13) | collective-permute-done | bytes 98336 | tf_op jit(solution)/shard_map/ppermute | solution.py:716
  43.4 1.5 %collective-permute-start.14 = (bf16[16,768]{1,0:T(8,128)(2,1)S(1)}, bf16[16,768]{1,0:T(8,128)(2,1)S(1)}, u32[]{:S(2)}, u32[]{:S(2)}) collective-permute-start(bf16[16,768]{1,0:T(8,128)(2,1)S(1)} %get-tuple-element.64), channel_id=1, source_target_pairs={{0,12},{2,14},{4,8},{6,10},{8,4},{10,6},{12,0},{14,2},{1,13},{3,15... | collective-permute-start | bytes 73736 | tf_op jit(solution)/shard_map/ppermute | solution.py:718
  44.9 0.6 %collective-permute-start.15 = (bf16[16,768]{1,0:T(8,128)(2,1)S(1)}, bf16[16,768]{1,0:T(8,128)(2,1)S(1)}, u32[]{:S(2)}, u32[]{:S(2)}) collective-permute-start(bf16[16,768]{1,0:T(8,128)(2,1)S(1)} %get-tuple-element.65), channel_id=1, source_target_pairs={{0,8},{2,10},{4,12},{6,14},{8,0},{10,2},{12,4},{14,6},{1,9},{3,11}... | collective-permute-start | bytes 73736 | tf_op jit(solution)/shard_map/ppermute | solution.py:718
  45.5 2.3 %collective-permute-start.16 = (bf16[16,768]{1,0:T(8,128)(2,1)S(1)}, bf16[16,768]{1,0:T(8,128)(2,1)S(1)}, u32[]{:S(2)}, u32[]{:S(2)}) collective-permute-start(bf16[16,768]{1,0:T(8,128)(2,1)S(1)} %get-tuple-element.66), channel_id=1, source_target_pairs={{0,4},{2,6},{4,0},{6,2},{8,12},{10,14},{12,8},{14,10},{1,5},{3,7},... | collective-permute-start | bytes 73736 | tf_op jit(solution)/shard_map/ppermute | solution.py:718
  47.8 1.2 %collective-permute-done.14.refs_1_ = bf16[16,768]{1,0:T(8,128)(2,1)S(1)} collective-permute-done((bf16[16,768]{1,0:T(8,128)(2,1)S(1)}, bf16[16,768]{1,0:T(8,128)(2,1)S(1)}, u32[]{:S(2)}, u32[]{:S(2)}) %collective-permute-start.14) | collective-permute-done | bytes 24608 | tf_op jit(solution)/shard_map/ppermute | solution.py:718
  49.1 0.7 %collective-permute-done.15.refs_2_ = bf16[16,768]{1,0:T(8,128)(2,1)S(1)} collective-permute-done((bf16[16,768]{1,0:T(8,128)(2,1)S(1)}, bf16[16,768]{1,0:T(8,128)(2,1)S(1)}, u32[]{:S(2)}, u32[]{:S(2)}) %collective-permute-start.15) | collective-permute-done | bytes 24608 | tf_op jit(solution)/shard_map/ppermute | solution.py:718
  49.7 0.2 collective-permute-done.16.refs_3_
  49.9 0.6 %line_sum.1 = bf16[16,768]{1,0:T(8,128)(2,1)} custom-call(f32[16,768]{1,0:T(8,128)S(1)} %get-tuple-element.63.refs_0_, bf16[16,768]{1,0:T(8,128)(2,1)S(1)} %collective-permute-done.14.refs_1_, bf16[16,768]{1,0:T(8,128)(2,1)S(1)} %collective-permute-done.15.refs_2_, bf16[16,768]{1,0:T(8,128)(2,1)S(1)} %collective-permute-done.16.refs_3_), custom_call_target="tpu_custom_call" | custom-call | tf_op jit(solution)/shard_map/line_sum/pallas_call | solution.py:620
  (24 shorter events, 0.6 us)
Async XLA Ops:
  0.0 6.0 %collective-permute-start = (bf16[16,768]{1,0:T(8,128)(2,1)}, bf16[16,768]{1,0:T(8,128)(2,1)S(1)}, u32[]{:S(2)}, u32[]{:S(2)}) collective-permute-start(bf16[16,768]{1,0:T(8,128)(2,1)} %refs_4_.2), channel_id=1, source_target_pairs={{0,1},{1,0},{2,3},{3,2},{4,5},{5,4},{6,7},{7,6},{8,9},{9,8},{10,11... | collective-permute-start | bytes 73736 | tf_op jit(solution)/shard_map/ppermute | solution.py:37
  2.9 3.1 %copy-start.1 = (bf16[1536,768]{1,0:T(8,128)(2,1)S(1)}, bf16[1536,768]{1,0:T(8,128)(2,1)}, u32[]{:S(2)}) copy-start(bf16[1536,768]{1,0:T(8,128)(2,1)} %refs_8_.1) | copy-start | bytes 7077892
  2.9 3.1 %copy-start.2 = (bf16[1536,512]{1,0:T(8,128)(2,1)S(1)}, bf16[1536,512]{1,0:T(8,128)(2,1)}, u32[]{:S(2)}) copy-start(bf16[1536,512]{1,0:T(8,128)(2,1)} %refs_9_.1) | copy-start | bytes 4718596
  6.1 7.4 %copy-start.4 = (bf16[1,1536,2,256]{3,2,1,0:T(2,128)(2,1)S(1)}, bf16[1,1536,2,256]{3,2,1,0:T(2,128)(2,1)}, u32[]{:S(2)}) copy-start(bf16[1,1536,2,256]{3,2,1,0:T(2,128)(2,1)} %param.22) | copy-start | bytes 4718596
  12.5 4.2 %copy-start.3 = (f32[1536]{0:T(1024)S(1)}, f32[1536]{0:T(1024)}, u32[]{:S(2)}) copy-start(f32[1536]{0:T(1024)} %refs_4_.3) | copy-start | bytes 18436
  12.5 19.9 %copy-start = (bf16[1,256,1536]{2,1,0:T(8,128)(2,1)S(1)}, bf16[1,256,1536]{2,1,0:T(8,128)(2,1)}, u32[]{:S(2)}) copy-start(bf16[1,256,1536]{2,1,0:T(8,128)(2,1)} %param.23) | copy-start | bytes 2359300
  12.5 4.2 %collective-permute-start.1 = (bf16[16,1536]{1,0:T(8,128)(2,1)S(1)}, bf16[16,1536]{1,0:T(8,128)(2,1)S(1)}, u32[]{:S(2)}, u32[]{:S(2)}) collective-permute-start(bf16[16,1536]{1,0:T(8,128)(2,1)S(1)} %get-tuple-element.46), channel_id=1, source_target_pairs={{0,1},{1,0},{2,3},{3,2},{4,5},{5,4},{6,7},{7,6},{8,9},{9,8},{10,11... | collective-permute-start | bytes 147464 | tf_op jit(solution)/shard_map/ppermute | solution.py:37
  16.8 6.1 %collective-permute-start.2 = (bf16[16,1664]{1,0:T(8,128)(2,1)S(1)}, bf16[16,1664]{1,0:T(8,128)(2,1)S(1)}, u32[]{:S(2)}, u32[]{:S(2)}) collective-permute-start(bf16[16,1664]{1,0:T(8,128)(2,1)S(1)} %bitcast.12), channel_id=1, source_target_pairs={{0,12},{2,14},{4,8},{6,10},{8,4},{10,6},{12,0},{14,2},{1,13},{3,15... | collective-permute-start | bytes 159752 | tf_op jit(solution)/shard_map/ppermute | solution.py:699
  19.3 5.1 %collective-permute-start.3 = (bf16[16,1664]{1,0:T(8,128)(2,1)S(1)}, bf16[16,1664]{1,0:T(8,128)(2,1)S(1)}, u32[]{:S(2)}, u32[]{:S(2)}) collective-permute-start(bf16[16,1664]{1,0:T(8,128)(2,1)S(1)} %bitcast.13), channel_id=1, source_target_pairs={{0,8},{2,10},{4,12},{6,14},{8,0},{10,2},{12,4},{14,6},{1,9},{3,11}... | collective-permute-start | bytes 159752 | tf_op jit(solution)/shard_map/ppermute | solution.py:699
  20.6 4.4 %collective-permute-start.4 = (bf16[16,1664]{1,0:T(8,128)(2,1)S(1)}, bf16[16,1664]{1,0:T(8,128)(2,1)S(1)}, u32[]{:S(2)}, u32[]{:S(2)}) collective-permute-start(bf16[16,1664]{1,0:T(8,128)(2,1)S(1)} %bitcast.14), channel_id=1, source_target_pairs={{0,4},{2,6},{4,0},{6,2},{8,12},{10,14},{12,8},{14,10},{1,5},{3,7},... | collective-permute-start | bytes 159752 | tf_op jit(solution)/shard_map/ppermute | solution.py:699
  25.0 7.3 %collective-permute-start.7 = (bf16[48,1664]{1,0:T(8,128)(2,1)S(1)}, bf16[48,1664]{1,0:T(8,128)(2,1)S(1)}, u32[]{:S(2)}, u32[]{:S(2)}) collective-permute-start(bf16[48,1664]{1,0:T(8,128)(2,1)S(1)} %get-tuple-element.53), channel_id=1, source_target_pairs={{0,2},{2,0},{4,6},{6,4},{8,10},{10,8},{12,14},{14,12},{1,3},{3,1},... | collective-permute-start | bytes 479240 | tf_op jit(solution)/shard_map/ppermute | solution.py:37
  28.1 4.1 %collective-permute-start.6 = (bf16[16,1664]{1,0:T(8,128)(2,1)S(1)}, bf16[16,1664]{1,0:T(8,128)(2,1)S(1)}, u32[]{:S(2)}, u32[]{:S(2)}) collective-permute-start(bf16[16,1664]{1,0:T(8,128)(2,1)S(1)} %bitcast.16), channel_id=1, source_target_pairs={{0,2},{2,0},{4,6},{6,4},{8,10},{10,8},{12,14},{14,12},{1,3},{3,1},... | collective-permute-start | bytes 159752 | tf_op jit(solution)/shard_map/ppermute | solution.py:37
  28.2 4.2 %collective-permute-start.5 = (bf16[64,1664]{1,0:T(8,128)(2,1)S(1)}, bf16[64,1664]{1,0:T(8,128)(2,1)S(1)}, u32[]{:S(2)}, u32[]{:S(2)}) collective-permute-start(bf16[64,1664]{1,0:T(8,128)(2,1)S(1)} %get-tuple-element.50.refs_0_), channel_id=1, source_target_pairs={{0,16},{16,0},{1,17},{17,1},{2,18},{18,2},{3,19},{19,3},{4,20},{20... | collective-permute-start | bytes 638984 | tf_op jit(solution)/shard_map/ppermute | solution.py:37
  32.3 1.5 %collective-permute-start.10 = (bf16[64,1664]{1,0:T(8,128)(2,1)S(1)}, bf16[64,1664]{1,0:T(8,128)(2,1)S(1)}, u32[]{:S(2)}, u32[]{:S(2)}) collective-permute-start(bf16[64,1664]{1,0:T(8,128)(2,1)S(1)} %joined.1.refs_5_.x_own), channel_id=1, source_target_pairs={{0,16},{16,0},{1,17},{17,1},{2,18},{18,2},{3,19},{19,3},{4,20},{20... | collective-permute-start | bytes 638984 | tf_op jit(solution)/shard_map/ppermute | solution.py:37
  33.3 1.6 %collective-permute-start.8 = (bf16[64,1536]{1,0:T(8,128)(2,1)S(1)}, bf16[64,1536]{1,0:T(8,128)(2,1)S(1)}, u32[]{:S(2)}, u32[]{:S(2)}) collective-permute-start(bf16[64,1536]{1,0:T(8,128)(2,1)S(1)} %get-tuple-element.55), channel_id=1, source_target_pairs={{0,16},{16,0},{1,17},{17,1},{2,18},{18,2},{3,19},{19,3},{4,20},{20... | collective-permute-start | bytes 589832 | tf_op jit(solution)/shard_map/ppermute | solution.py:37
  34.5 1.5 %collective-permute-start.11 = (bf16[64,1536]{1,0:T(8,128)(2,1)S(1)}, bf16[64,1536]{1,0:T(8,128)(2,1)S(1)}, u32[]{:S(2)}, u32[]{:S(2)}) collective-permute-start(bf16[64,1536]{1,0:T(8,128)(2,1)S(1)} %get-tuple-element.60), channel_id=1, source_target_pairs={{0,16},{16,0},{1,17},{17,1},{2,18},{18,2},{3,19},{19,3},{4,20},{20... | collective-permute-start | bytes 589832 | tf_op jit(solution)/shard_map/ppermute | solution.py:37
  34.9 5.1 %collective-permute-start.9 = (bf16[64,768]{1,0:T(8,128)(2,1)S(1)}, bf16[64,768]{1,0:T(8,128)(2,1)S(1)}, u32[]{:S(2)}, u32[]{:S(2)}) collective-permute-start(bf16[64,768]{1,0:T(8,128)(2,1)S(1)} %get-tuple-element.57), channel_id=1, source_target_pairs={{0,1},{1,0},{2,3},{3,2},{4,5},{5,4},{6,7},{7,6},{8,9},{9,8},{10,11... | collective-permute-start | bytes 294920 | tf_op jit(solution)/shard_map/ppermute | solution.py:37
  36.0 6.2 %collective-permute-start.12 = (bf16[64,768]{1,0:T(8,128)(2,1)S(1)}, bf16[64,768]{1,0:T(8,128)(2,1)S(1)}, u32[]{:S(2)}, u32[]{:S(2)}) collective-permute-start(bf16[64,768]{1,0:T(8,128)(2,1)S(1)} %get-tuple-element.61), channel_id=1, source_target_pairs={{0,2},{2,0},{4,6},{6,4},{8,10},{10,8},{12,14},{14,12},{1,3},{3,1},... | collective-permute-start | bytes 294920 | tf_op jit(solution)/shard_map/ppermute | solution.py:37
  37.8 5.5 %collective-permute-start.13 = (bf16[64,768]{1,0:T(8,128)(2,1)S(1)}, bf16[64,768]{1,0:T(8,128)(2,1)S(1)}, u32[]{:S(2)}, u32[]{:S(2)}) collective-permute-start(bf16[64,768]{1,0:T(8,128)(2,1)S(1)} %get-tuple-element.62), channel_id=1, source_target_pairs={{0,3},{1,2},{2,1},{3,0},{4,7},{5,6},{6,5},{7,4},{8,11},{9,10},{10,... | collective-permute-start | bytes 294920 | tf_op jit(solution)/shard_map/ppermute | solution.py:716
  43.4 5.7 %collective-permute-start.14 = (bf16[16,768]{1,0:T(8,128)(2,1)S(1)}, bf16[16,768]{1,0:T(8,128)(2,1)S(1)}, u32[]{:S(2)}, u32[]{:S(2)}) collective-permute-start(bf16[16,768]{1,0:T(8,128)(2,1)S(1)} %get-tuple-element.64), channel_id=1, source_target_pairs={{0,12},{2,14},{4,8},{6,10},{8,4},{10,6},{12,0},{14,2},{1,13},{3,15... | collective-permute-start | bytes 73736 | tf_op jit(solution)/shard_map/ppermute | solution.py:718
  44.9 4.8 %collective-permute-start.15 = (bf16[16,768]{1,0:T(8,128)(2,1)S(1)}, bf16[16,768]{1,0:T(8,128)(2,1)S(1)}, u32[]{:S(2)}, u32[]{:S(2)}) collective-permute-start(bf16[16,768]{1,0:T(8,128)(2,1)S(1)} %get-tuple-element.65), channel_id=1, source_target_pairs={{0,8},{2,10},{4,12},{6,14},{8,0},{10,2},{12,4},{14,6},{1,9},{3,11}... | collective-permute-start | bytes 73736 | tf_op jit(solution)/shard_map/ppermute | solution.py:718
  45.5 4.4 %collective-permute-start.16 = (bf16[16,768]{1,0:T(8,128)(2,1)S(1)}, bf16[16,768]{1,0:T(8,128)(2,1)S(1)}, u32[]{:S(2)}, u32[]{:S(2)}) collective-permute-start(bf16[16,768]{1,0:T(8,128)(2,1)S(1)} %get-tuple-element.66), channel_id=1, source_target_pairs={{0,4},{2,6},{4,0},{6,2},{8,12},{10,14},{12,8},{14,10},{1,5},{3,7},... | collective-permute-start | bytes 73736 | tf_op jit(solution)/shard_map/ppermute | solution.py:718
